TPU v7x, 32 devices: a whole 2x2x4 slice. The times are simulated.
32 devices in a mesh: ctx: 8 (over y, x, core), head: 4 (over z).
Axes of the slice: x: 2, y: 2, z: 4, core: 2. Of those that a mesh axis runs over, the one named last changes fastest.
Arguments:
- queries: bfloat16 [2048, 2048], P('ctx', 'head'), may hold values from -120 to 120
- key_rows: bfloat16 [2048, 128], P('ctx'), may hold values from -4 to 4
- value_rows: bfloat16 [2048, 128], P('ctx'), may hold values from -6 to 6
- lengths: int32 [8], replicated, may hold values from 1 to 1024, 2048 in all
- out_weight: bfloat16 [2048, 8192], P('head'), may hold values from -0.125 to 0.125
Outputs:
- layer_out: bfloat16 [2048, 8192], P(('ctx', 'head'))
Inputs may be any that keep to these rules, and one draw needn't show every extreme that they name: The lengths of the 8 documents sum to 2048; the longest is exactly 1024.
All inputs are finite; a program needn't handle non-finite values.
Results may differ from a plain program's by a relative error of at most 0.023.
Values may be sent and summed in bfloat16 or wider, within the bound.
No kernel may reach another device: no remote copies, remote signals or barrier semaphores. Data moves between devices by JAX's collectives and lax.ppermute only.
A program may use at most 64 MiB of HBM per device.

v0:
```python
import math

import jax
import jax.numpy as jnp
from jax import lax
from jax.sharding import PartitionSpec as P

HD = 128
GROUP = 16
SPAN = 4


big_negative = -1e30


def shifted(shard, axis, by):
    length = lax.axis_size(axis)
    pairs = [(i, i + by) for i in range(length) if 0 <= i + by < length]
    return lax.ppermute(shard, axis, pairs)


def document_of(positions, doc_ends):
    return jnp.sum((positions[:, None] >= doc_ends[None, :]).astype(jnp.int32), axis=1)


def absorb_block(
    running, query_heads, key_piece, value_piece, offset, query_pos, query_docs, doc_ends
):
    row_count = key_piece.shape[0]
    key_pos = offset + jnp.arange(row_count, dtype=jnp.int32)
    same_doc = query_docs[:, None] == document_of(key_pos, doc_ends)[None, :]
    allowed = same_doc & (key_pos[None, :] <= query_pos[:, None]) & (key_pos[None, :] >= 0)
    scores = jnp.einsum(
        "qhd,kd->hqk", query_heads, key_piece, preferred_element_type=jnp.float32
    ) * (1.0 / math.sqrt(HD))
    top_old, total_old, summed_old = running
    top_new = jnp.maximum(top_old, jnp.max(jnp.where(allowed[None], scores, big_negative), axis=2))
    expo = jnp.where(allowed[None], jnp.exp(scores - top_new[:, :, None]), 0.0)
    factor = jnp.exp(top_old - top_new)
    total_new = total_old * factor + jnp.sum(expo, axis=2)
    added = jnp.einsum(
        "hqk,kd->qhd", expo.astype(jnp.bfloat16), value_piece, preferred_element_type=jnp.float32
    )
    summed_new = summed_old * factor.T[:, :, None] + added
    return (top_new, total_new, summed_new)


def absorb(running, query_heads, key_piece, value_piece, offset, query_pos, query_docs, doc_ends):
    return absorb_block(
        running, query_heads, key_piece, value_piece, offset, query_pos, query_docs, doc_ends
    )


def body(queries, key_rows, value_rows, lengths, out_weight):
    rows_here = queries.shape[0]
    heads_here = queries.shape[1] // HD
    ctx_index = lax.axis_index("ctx")
    head_index = lax.axis_index("head")
    kv_index = head_index * heads_here // GROUP
    own_keys = lax.dynamic_slice_in_dim(key_rows, kv_index * HD, HD, 1)
    own_values = lax.dynamic_slice_in_dim(value_rows, kv_index * HD, HD, 1)
    doc_ends = jnp.cumsum(lengths)
    first_row = ctx_index * rows_here
    query_pos = first_row + jnp.arange(rows_here, dtype=jnp.int32)
    query_docs = document_of(query_pos, doc_ends)
    query_heads = queries.reshape(rows_here, heads_here, HD)
    running = (
        jnp.full((heads_here, rows_here), big_negative, jnp.float32),
        jnp.zeros((heads_here, rows_here), jnp.float32),
        jnp.zeros((rows_here, heads_here, HD), jnp.float32),
    )

    def fold_piece(current, pieces, offset):
        return absorb(
            current, query_heads, pieces[0], pieces[1], offset, query_pos, query_docs, doc_ends
        )

    running = fold_piece(running, (own_keys, own_values), first_row)
    for distance in range(1, SPAN + 1):
        earlier = shifted((own_keys, own_values), "ctx", distance)
        running = fold_piece(running, earlier, first_row - distance * rows_here)
    attended = (
        (running[2] / running[1].T[:, :, None])
        .astype(jnp.bfloat16)
        .reshape(rows_here, heads_here * HD)
    )
    layer_out = lax.psum_scatter(
        jnp.dot(attended, out_weight, preferred_element_type=jnp.float32).astype(jnp.bfloat16),
        "head",
        scatter_dimension=0,
        tiled=True,
    )
    return layer_out


def solution(mesh):
    placed = (P("ctx", "head"), P("ctx", None), P("ctx", None), P(), P("head", None))
    return jax.shard_map(
        body, mesh=mesh, in_specs=placed, out_specs=P(("ctx", "head"), None), check_vma=False
    )
```

profile of v0, /device:TPU:0, one launch (start us, length us, event | category | flops | bytes accessed | tf_op | source)
XLA Modules:
  0.0 122.4 jit_solution(17725449513482729085)
XLA Ops:
  6.5 5.0 %collective-permute-start.6 = (bf16[256,128]{1,0:T(8,128)(2,1)}, bf16[256,128]{1,0:T(8,128)(2,1)S(1)}, u32[]{:S(2)}, u32[]{:S(2)}) collective-permute-start(bf16[256,128]{1,0:T(8,128)(2,1)} %param.6), channel_id=1, source_target_pairs={{0,16},{4,20},{8,24},{12,28},{1,17},{5,21},{9,25},{13,29},{2,18},{... | collective-permute-start | bytes 196616 | tf_op jit(solution)/shard_map/ppermute | solution.py:19
  11.5 2.6 %collective-permute-start.4 = (bf16[256,128]{1,0:T(8,128)(2,1)}, bf16[256,128]{1,0:T(8,128)(2,1)S(1)}, u32[]{:S(2)}, u32[]{:S(2)}) collective-permute-start(bf16[256,128]{1,0:T(8,128)(2,1)} %param.6), channel_id=1, source_target_pairs={{0,12},{4,16},{8,20},{12,24},{16,28},{1,13},{5,17},{9,21},{13,25},... | collective-permute-start | bytes 196616 | tf_op jit(solution)/shard_map/ppermute | solution.py:19
  14.1 2.1 %collective-permute-start.2 = (bf16[256,128]{1,0:T(8,128)(2,1)}, bf16[256,128]{1,0:T(8,128)(2,1)S(1)}, u32[]{:S(2)}, u32[]{:S(2)}) collective-permute-start(bf16[256,128]{1,0:T(8,128)(2,1)} %param.6), channel_id=1, source_target_pairs={{0,8},{4,12},{8,16},{12,20},{16,24},{20,28},{1,9},{5,13},{9,17},{1... | collective-permute-start | bytes 196616 | tf_op jit(solution)/shard_map/ppermute | solution.py:19
  16.3 1.8 %collective-permute-start = (bf16[256,128]{1,0:T(8,128)(2,1)}, bf16[256,128]{1,0:T(8,128)(2,1)S(1)}, u32[]{:S(2)}, u32[]{:S(2)}) collective-permute-start(bf16[256,128]{1,0:T(8,128)(2,1)} %param.6), channel_id=1, source_target_pairs={{0,4},{4,8},{8,12},{12,16},{16,20},{20,24},{24,28},{1,5},{5,9},{9,... | collective-permute-start | bytes 196616 | tf_op jit(solution)/shard_map/ppermute | solution.py:19
  18.1 0.9 copy.25
  19.0 2.9 %collective-permute-start.3 = (bf16[256,128]{0,1:T(8,128)(2,1)S(1)}, bf16[256,128]{0,1:T(8,128)(2,1)S(1)}, u32[]{:S(2)}, u32[]{:S(2)}) collective-permute-start(bf16[256,128]{0,1:T(8,128)(2,1)S(1)} %copy.25), channel_id=1, source_target_pairs={{0,8},{4,12},{8,16},{12,20},{16,24},{20,28},{1,9},{5,13},{9,17},{1... | collective-permute-start | bytes 196616 | tf_op jit(solution)/shard_map/ppermute | solution.py:19
  22.0 0.8 reduce-window.8
  22.9 0.1 convert_reduce_fusion
  23.0 0.7 and_and_fusion.4
  23.7 1.2 select_reduce_fusion.4
  24.9 1.6 %collective-permute-start.5 = (bf16[256,128]{0,1:T(8,128)(2,1)S(1)}, bf16[256,128]{0,1:T(8,128)(2,1)S(1)}, u32[]{:S(2)}, u32[]{:S(2)}) collective-permute-start(bf16[256,128]{0,1:T(8,128)(2,1)S(1)} %copy.25), channel_id=1, source_target_pairs={{0,12},{4,16},{8,20},{12,24},{16,28},{1,13},{5,17},{9,21},{13,25},... | collective-permute-start | bytes 196616 | tf_op jit(solution)/shard_map/ppermute | solution.py:19
  26.5 0.3 select_reduce_fusion
  26.9 1.3 %collective-permute-start.7 = (bf16[256,128]{0,1:T(8,128)(2,1)S(1)}, bf16[256,128]{0,1:T(8,128)(2,1)S(1)}, u32[]{:S(2)}, u32[]{:S(2)}) collective-permute-start(bf16[256,128]{0,1:T(8,128)(2,1)S(1)} %copy.25), channel_id=1, source_target_pairs={{0,16},{4,20},{8,24},{12,28},{1,17},{5,21},{9,25},{13,29},{2,18},{... | collective-permute-start | bytes 196616 | tf_op jit(solution)/shard_map/ppermute | solution.py:19
  28.2 0.3 select_reduce_fusion.1
  28.5 1.4 %collective-permute-start.1 = (bf16[256,128]{0,1:T(8,128)(2,1)S(1)}, bf16[256,128]{0,1:T(8,128)(2,1)S(1)}, u32[]{:S(2)}, u32[]{:S(2)}) collective-permute-start(bf16[256,128]{0,1:T(8,128)(2,1)S(1)} %copy.25), channel_id=1, source_target_pairs={{0,4},{4,8},{8,12},{12,16},{16,20},{20,24},{24,28},{1,5},{5,9},{9,... | collective-permute-start | bytes 196616 | tf_op jit(solution)/shard_map/ppermute | solution.py:19
  29.9 0.3 select_reduce_fusion.2
  30.3 0.3 select_reduce_fusion.3
  30.6 0.2 fusion.18
  30.9 0.2 fusion.20
  31.1 0.2 fusion.22
  31.3 0.2 fusion.24
  31.5 0.2 fusion.16
  31.7 0.3 fusion.6
  32.1 0.0 slice-start.1
  32.1 0.3 convolution_bitcast_fusion.2
  32.4 0.3 convolution_bitcast_fusion.1
  32.8 0.3 convolution_bitcast_fusion
  33.1 0.4 fusion.15
  33.6 0.9 slice-done.1
  34.4 4.4 %convolution_convert_fusion = bf16[256,8192]{1,0:T(8,128)(2,1)} fusion(bf16[256,512]{0,1:T(8,128)(2,1)S(1)} %bitcast.222, bf16[512,8192]{1,0:T(8,128)(2,1)S(1)} %bitcast.221), kind=kOutput, calls=%fused_computation | convolution fusion | flops 2149580800 | bytes 12845056 | tf_op jit(solution)/shard_map/dot_general | solution.py:88
  38.9 0.0 reduce-scatter.2.cloned.1.call-update
  38.9 76.6 %reduce-scatter.2.cloned.1.call-done = bf16[64,8192]{1,0:T(8,128)(2,1)} async-done(((bf16[256,8192]{1,0:T(8,128)(2,1)}), bf16[64,8192]{1,0:T(8,128)(2,1)}) %reduce-scatter.2.cloned.1.call-update) | async-done | bytes 1048592 | tf_op jit(solution)/shard_map/reduce_scatter | solution.py:87
  (24 shorter events, 0.1 us)
Async XLA Ops:
  6.5 17.2 %copy-start = (bf16[256,512]{1,0:T(8,128)(2,1)S(1)}, bf16[256,512]{1,0:T(8,128)(2,1)}, u32[]{:S(2)}) copy-start(bf16[256,512]{1,0:T(8,128)(2,1)} %param.5) | copy-start | bytes 786436
  6.5 25.2 %copy-start.1 = (bf16[256,128]{1,0:T(8,128)(2,1)S(1)}, bf16[256,128]{1,0:T(8,128)(2,1)}, u32[]{:S(2)}) copy-start(bf16[256,128]{1,0:T(8,128)(2,1)} %param.7) | copy-start | bytes 196612
  6.5 109.0 %reduce-scatter.2.cloned.1.call-start = ((), (), s32[]{:S(2)}) async-start(), calls=%async_computation.1 | async-start | bytes 5242880 | tf_op jit(solution)/shard_map/reduce_scatter | solution.py:87
  6.5 18.3 %collective-permute-start.6 = (bf16[256,128]{1,0:T(8,128)(2,1)}, bf16[256,128]{1,0:T(8,128)(2,1)S(1)}, u32[]{:S(2)}, u32[]{:S(2)}) collective-permute-start(bf16[256,128]{1,0:T(8,128)(2,1)} %param.6), channel_id=1, source_target_pairs={{0,16},{4,20},{8,24},{12,28},{1,17},{5,21},{9,25},{13,29},{2,18},{... | collective-permute-start | bytes 196616 | tf_op jit(solution)/shard_map/ppermute | solution.py:19
  11.5 15.3 %collective-permute-start.4 = (bf16[256,128]{1,0:T(8,128)(2,1)}, bf16[256,128]{1,0:T(8,128)(2,1)S(1)}, u32[]{:S(2)}, u32[]{:S(2)}) collective-permute-start(bf16[256,128]{1,0:T(8,128)(2,1)} %param.6), channel_id=1, source_target_pairs={{0,12},{4,16},{8,20},{12,24},{16,28},{1,13},{5,17},{9,21},{13,25},... | collective-permute-start | bytes 196616 | tf_op jit(solution)/shard_map/ppermute | solution.py:19
  14.1 14.4 %collective-permute-start.2 = (bf16[256,128]{1,0:T(8,128)(2,1)}, bf16[256,128]{1,0:T(8,128)(2,1)S(1)}, u32[]{:S(2)}, u32[]{:S(2)}) collective-permute-start(bf16[256,128]{1,0:T(8,128)(2,1)} %param.6), channel_id=1, source_target_pairs={{0,8},{4,12},{8,16},{12,20},{16,24},{20,28},{1,9},{5,13},{9,17},{1... | collective-permute-start | bytes 196616 | tf_op jit(solution)/shard_map/ppermute | solution.py:19
  16.3 14.0 %collective-permute-start = (bf16[256,128]{1,0:T(8,128)(2,1)}, bf16[256,128]{1,0:T(8,128)(2,1)S(1)}, u32[]{:S(2)}, u32[]{:S(2)}) collective-permute-start(bf16[256,128]{1,0:T(8,128)(2,1)} %param.6), channel_id=1, source_target_pairs={{0,4},{4,8},{8,12},{12,16},{16,20},{20,24},{24,28},{1,5},{5,9},{9,... | collective-permute-start | bytes 196616 | tf_op jit(solution)/shard_map/ppermute | solution.py:19
  19.0 13.1 %collective-permute-start.3 = (bf16[256,128]{0,1:T(8,128)(2,1)S(1)}, bf16[256,128]{0,1:T(8,128)(2,1)S(1)}, u32[]{:S(2)}, u32[]{:S(2)}) collective-permute-start(bf16[256,128]{0,1:T(8,128)(2,1)S(1)} %copy.25), channel_id=1, source_target_pairs={{0,8},{4,12},{8,16},{12,20},{16,24},{20,28},{1,9},{5,13},{9,17},{1... | collective-permute-start | bytes 196616 | tf_op jit(solution)/shard_map/ppermute | solution.py:19
  24.9 7.5 %collective-permute-start.5 = (bf16[256,128]{0,1:T(8,128)(2,1)S(1)}, bf16[256,128]{0,1:T(8,128)(2,1)S(1)}, u32[]{:S(2)}, u32[]{:S(2)}) collective-permute-start(bf16[256,128]{0,1:T(8,128)(2,1)S(1)} %copy.25), channel_id=1, source_target_pairs={{0,12},{4,16},{8,20},{12,24},{16,28},{1,13},{5,17},{9,21},{13,25},... | collective-permute-start | bytes 196616 | tf_op jit(solution)/shard_map/ppermute | solution.py:19
  26.9 5.9 %collective-permute-start.7 = (bf16[256,128]{0,1:T(8,128)(2,1)S(1)}, bf16[256,128]{0,1:T(8,128)(2,1)S(1)}, u32[]{:S(2)}, u32[]{:S(2)}) collective-permute-start(bf16[256,128]{0,1:T(8,128)(2,1)S(1)} %copy.25), channel_id=1, source_target_pairs={{0,16},{4,20},{8,24},{12,28},{1,17},{5,21},{9,25},{13,29},{2,18},{... | collective-permute-start | bytes 196616 | tf_op jit(solution)/shard_map/ppermute | solution.py:19
  28.5 4.6 %collective-permute-start.1 = (bf16[256,128]{0,1:T(8,128)(2,1)S(1)}, bf16[256,128]{0,1:T(8,128)(2,1)S(1)}, u32[]{:S(2)}, u32[]{:S(2)}) collective-permute-start(bf16[256,128]{0,1:T(8,128)(2,1)S(1)} %copy.25), channel_id=1, source_target_pairs={{0,4},{4,8},{8,12},{12,16},{16,20},{20,24},{24,28},{1,5},{5,9},{9,... | collective-permute-start | bytes 196616 | tf_op jit(solution)/shard_map/ppermute | solution.py:19
  30.6 2.9 %slice-start = ((s8[8388608]{0:T(1024)(128)(4,1)}), s8[4194304]{0:T(1024)(128)(4,1)S(1)}, s32[]{:S(2)}) async-start(s8[8388608]{0:T(1024)(128)(4,1)} %bitcast.220), calls=%async_computation.2 | async-start | bytes 8388608
  32.1 2.4 %slice-start.1 = ((s8[8388608]{0:T(1024)(128)(4,1)}), s8[4194304]{0:T(1024)(128)(4,1)S(1)}, s32[]{:S(2)}) async-start(s8[8388608]{0:T(1024)(128)(4,1)} %bitcast.220), calls=%async_computation.3 | async-start | bytes 8388608
Sparse Core Ops, SparseCore 0:
  39.0 76.4 reduce-scatter.1
where the time goes:
time: 123 us; the launch traced here: 122 us
  waiting for transfers between devices  76.7 us (62%)
  starting transfers between devices  18.8 us (15%)
  between operations  13.7 us (11%)
  matrix products  8.62 us (7%)
  other arithmetic  2.79 us (2%)
  local copies, waits for them, and re-layouts  1.86 us (2%)
    reduce_scatter x1, waiting for transfers between devices, body(): lax.psum_scatter(jnp.dot(attended, out_weight, preferred_element_type=jnp...  76.6 us
    ppermute x8, starting transfers between devices, shifted(): return lax.ppermute(shard, axis, pairs)  18.8 us
    dot_general x1, matrix products, body(): jnp.dot(attended, out_weight, preferred_element_type=jnp.float32)  4.44 us
    dot_general x5, matrix products, absorb_block(): jnp.einsum('qhd,kd->hqk', query_heads, key_piece, preferred_element_type=...  2.48 us
  transfers between devices with their start and end apart: 9, of which 1 were waited for; matrix products, arithmetic and copies ran while one was open for 6% of the time, Pallas kernels for 0%

commit v1 on v0

v1 whole, which is shorter than its diff:
```python
import functools
import math

import jax
import jax.numpy as jnp
from jax import lax
from jax.experimental import pallas as pl
from jax.experimental.pallas import tpu as pltpu
from jax.sharding import PartitionSpec as P

HD = 128
GROUP = 16
SPAN = 4
CORES = 2
MIB = 1024 * 1024

big_negative = -1e30
log2_scale = math.log2(math.e) / math.sqrt(HD)


def attention_kernel(place_ref, query_hbm, *refs):
    piece_refs, (out_ref, query_ref, sem) = refs[:-3], refs[-3:]
    query_copy = pltpu.make_async_copy(query_hbm, query_ref, sem)
    query_copy.start()
    rows = query_ref.shape[0]
    heads = query_ref.shape[1] // HD
    window = rows * len(piece_refs)
    first = place_ref[0]
    query_pos = first + lax.broadcasted_iota(jnp.int32, (rows, 1), 0)

    def step(d, carry):
        end, start = carry
        end = end + place_ref[1 + d]
        return end, jnp.where(query_pos >= end, end, start)

    _, doc_start = lax.fori_loop(
        0, place_ref.shape[0] - 1, step, (jnp.int32(0), jnp.zeros((rows, 1), jnp.int32))
    )
    key_pos = first - (window - rows) + lax.broadcasted_iota(jnp.int32, (rows, window), 1)
    allowed = (key_pos >= doc_start) & (key_pos <= query_pos)
    keys = jnp.concatenate([ref[:rows] for ref in piece_refs], axis=0)
    values = jnp.concatenate([ref[rows:] for ref in piece_refs], axis=0)
    query_copy.wait()
    for head in range(heads):
        query = query_ref[:, head * HD : (head + 1) * HD]
        scores = lax.dot_general(
            query, keys, (((1,), (1,)), ((), ())), preferred_element_type=jnp.float32
        )
        scores = jnp.where(allowed, scores * log2_scale, big_negative)
        top = jnp.max(scores, axis=1, keepdims=True)
        expo = jnp.where(allowed, jnp.exp2(scores - top), 0.0)
        total = jnp.sum(expo, axis=1, keepdims=True)
        summed = jnp.dot(expo.astype(jnp.bfloat16), values, preferred_element_type=jnp.float32)
        out_ref[:, head * HD : (head + 1) * HD] = (summed / total).astype(jnp.bfloat16)


def attention(queries, pieces, lengths, first_row):
    vmem = pl.BlockSpec(memory_space=pltpu.VMEM)
    return pl.pallas_call(
        attention_kernel,
        out_shape=jax.ShapeDtypeStruct(queries.shape, jnp.bfloat16),
        in_specs=[
            pl.BlockSpec(memory_space=pltpu.SMEM),
            pl.BlockSpec(memory_space=pltpu.HBM),
        ]
        + [vmem] * len(pieces),
        out_specs=vmem,
        scratch_shapes=[pltpu.VMEM(queries.shape, queries.dtype), pltpu.SemaphoreType.DMA],
        compiler_params=pltpu.CompilerParams(vmem_limit_bytes=24 * MIB),
        cost_estimate=pl.CostEstimate(flops=0, bytes_accessed=0, transcendentals=0),
        name="attention",
    )(jnp.concatenate([first_row[None], lengths]), queries, *pieces)


def tie(values, after):
    return lax.optimization_barrier((values, after))[0]


def chip_order(chips, core):
    bits = chips.bit_length() - 1
    return [
        sum(((k >> t) & 1) << (t if core == 0 else bits - 1 - t) for t in range(bits))
        for k in range(chips)
    ]


def plane_order(planes):
    order, mask = [0], planes - 1
    while mask:
        order += [x ^ mask for x in order]
        mask >>= 1
    return order


def project(attended, own_weight, weights, layout, half, place, chips):
    order = plane_order(sum(part.shape[0] for part in attended))
    planes = len(order)
    _, rows, depth = attended[0].shape
    cols = own_weight.shape[1] // CORES
    share = depth // chips
    rows_out = rows // planes
    block = min(cols, 256)
    size = (planes - 1) * depth
    aligned = share % HD == 0
    chip_orders = [chip_order(chips, core) for core in range(CORES)]
    operands = list(attended)
    if not aligned:
        others = jnp.concatenate(attended).reshape(planes, rows, chips, share)
        chip_index = place[1] ^ jnp.asarray(chip_orders)[(place[2] + half) % CORES]
        chip_index = chip_index[jnp.asarray([k for k, _ in layout])]
        plane_index = jnp.asarray([order.index(x) for _, x in layout])
        others = others.transpose(0, 2, 1, 3)[plane_index, chip_index]
        operands = [attended[0][0], others.transpose(1, 0, 2).reshape(rows, size)]

    def kernel(place_ref, *refs):
        attended_refs, refs = refs[: len(operands)], refs[len(operands) :]
        own_ref, refs = refs[0], refs[1:]
        weight_refs, refs = refs[: len(weights)], refs[len(weights) :]
        out_refs, (flat_ref, wide_ref) = refs[:planes], refs[planes:]
        head, chip = place_ref[0], place_ref[1]
        core = (place_ref[2] + half) % CORES

        blocks = [(ref, i) for ref in attended_refs for i in range(ref.shape[0])] * aligned
        for d, dest in enumerate(order):
            source = pl.ds(pl.multiple_of((head ^ dest) * rows_out, rows_out), rows_out)
            to = slice(d * rows_out, (d + 1) * rows_out)
            if not aligned:
                flat_ref[to, :] = attended_refs[0][source, :]
                wide_ref[to, :] = attended_refs[1][source, :]
                continue
            flat_ref[to, :] = attended_refs[0][0, source, :]
            for at, (k, x) in enumerate(layout):
                low, high = (chip_orders[c][k] for c in range(CORES))
                index = chip ^ (low + core * (high - low))
                column = pl.ds(pl.multiple_of(index * share, share), share)
                ref, i = blocks[order.index(x)]
                wide_ref[to, at * share : (at + 1) * share] = ref[i, source, column]

        for j in range(cols // block):
            columns = slice(j * block, (j + 1) * block)
            own = own_ref[:, pl.ds(pl.multiple_of(core * cols + j * block, HD), block)]
            acc = jnp.dot(flat_ref[...], own, preferred_element_type=jnp.float32)
            at = 0
            for ref in weight_refs:
                acc += jnp.dot(
                    wide_ref[:, at : at + ref.shape[0]],
                    ref[:, columns],
                    preferred_element_type=jnp.float32,
                )
                at += ref.shape[0]
            acc = acc.astype(jnp.bfloat16)
            for d, out_ref in enumerate(out_refs):
                out_ref[:, columns] = acc[d * rows_out : (d + 1) * rows_out]

    vmem = pl.BlockSpec(memory_space=pltpu.VMEM)
    return pl.pallas_call(
        kernel,
        out_shape=[jax.ShapeDtypeStruct((rows_out, cols), jnp.bfloat16)] * planes,
        in_specs=[pl.BlockSpec(memory_space=pltpu.SMEM)]
        + [vmem] * (len(operands) + 1 + len(weights)),
        out_specs=[vmem] * planes,
        scratch_shapes=[
            pltpu.VMEM((rows, depth), jnp.bfloat16),
            pltpu.VMEM((rows, size), jnp.bfloat16),
        ],
        compiler_params=pltpu.CompilerParams(vmem_limit_bytes=20 * MIB),
        cost_estimate=pl.CostEstimate(
            flops=2 * rows * planes * depth * cols,
            bytes_accessed=2 * (planes * depth * (rows + cols) + rows * cols),
            transcendentals=0,
        ),
        name="project",
    )(place, *operands, own_weight, *weights)


def assemble(pieces, half, width, place, out=None):
    order = plane_order(len(pieces))
    rows, cols = pieces[0].shape
    filled = [] if out is None else [out]

    def kernel(place_ref, *refs):
        out_ref, sem = refs[-2:]
        copies = []
        for k, x in enumerate(order):
            at = ((place_ref[0] ^ x) * CORES + (place_ref[2] + half) % CORES) * cols
            copies.append(
                pltpu.make_async_copy(
                    refs[k], out_ref.at[:, pl.ds(pl.multiple_of(at, HD), cols)], sem.at[k]
                )
            )
        for copy in copies:
            copy.start()
        for copy in copies:
            copy.wait()

    anywhere = pl.BlockSpec(memory_space=pl.ANY)
    return pl.pallas_call(
        kernel,
        out_shape=jax.ShapeDtypeStruct((rows, width), jnp.bfloat16),
        in_specs=[pl.BlockSpec(memory_space=pltpu.SMEM)]
        + [pl.BlockSpec(memory_space=pltpu.VMEM)] * len(pieces)
        + [anywhere] * len(filled),
        out_specs=anywhere,
        scratch_shapes=[pltpu.SemaphoreType.DMA((len(pieces),))],
        input_output_aliases={1 + len(pieces): 0} if filled else {},
        compiler_params=pltpu.CompilerParams(vmem_limit_bytes=4 * MIB),
        name="assemble",
    )(place, *pieces, *filled)


def paired(shard, x):
    length = lax.axis_size("head")
    return lax.ppermute(shard, "head", [(i, i ^ x) for i in range(length)])


def swapped(shard):
    length = lax.axis_size("ctx")
    return lax.ppermute(shard, "ctx", [(i, i ^ 1) for i in range(length)])


def crossed(shard, stage):
    length = lax.axis_size("ctx")
    bits = (length // CORES).bit_length() - 1
    bit = [stage, bits - 1 - stage]
    return lax.ppermute(
        shard, "ctx", [(i, i ^ (CORES << bit[i % CORES])) for i in range(length)]
    )


def later(shard, by):
    length = lax.axis_size("ctx")
    return lax.ppermute(shard, "ctx", [(i, i + by) for i in range(length - by)])


def body(queries, key_rows, value_rows, lengths, out_weight):
    rows = queries.shape[0]
    heads = queries.shape[1] // HD
    depth, width = out_weight.shape
    ctx, planes = lax.axis_size("ctx"), lax.axis_size("head")
    chips = ctx // CORES
    ctx_index, head_index = lax.axis_index("ctx"), lax.axis_index("head")
    chip, core = ctx_index // CORES, ctx_index % CORES
    share = depth // chips
    cols = width // (planes * CORES)
    place = jnp.stack([head_index, chip, core]).astype(jnp.int32)
    others = plane_order(planes)[1:]

    def share_of(x):
        column = ((head_index ^ x) * CORES + core) * cols
        return lax.dynamic_slice(out_weight, (chip * share, column), (share, cols))

    fetched = {x: paired(share_of(x), x) for x in others if x in (1, planes - 1)}
    for x in others:
        if x not in fetched:
            fetched[x] = paired(tie(share_of(x), fetched[planes - 1]), x)

    own = [key_rows, value_rows]
    if key_rows.shape[1] > HD:
        column = head_index * heads // GROUP * HD
        own = [lax.dynamic_slice_in_dim(part, column, HD, 1) for part in own]
    own = jnp.concatenate(own)
    late = tie(own, [fetched[1], fetched[planes - 1]])
    pieces = [later(own if d < 3 else late, d) for d in range(SPAN, 0, -1)] + [own]
    groups = [[1], [x for x in others if x > 1]]
    gathered = [fetched[1][None, None]]
    near = crossed(gathered[0], 0)
    attended = [attention(queries, pieces, lengths, ctx_index * rows)[None]]
    own_weight = lax.dynamic_slice_in_dim(
        tie(out_weight, attended), head_index * CORES * cols, CORES * cols, 1
    )

    shares, near, _ = lax.optimization_barrier(([fetched[x] for x in groups[1]], near, attended))
    gathered = [jnp.concatenate([gathered[0], near]), jnp.stack(shares)[None]]
    last = None
    plane_stages, chip_stages = planes.bit_length() - 1, chips.bit_length() - 1
    for stage in range(max(plane_stages, chip_stages)):
        new, near, far = [], [], []
        if stage < plane_stages:
            new = [paired(jnp.concatenate(attended), (planes - 1) >> stage)]
        if stage < chip_stages - 1:
            near = [crossed(gathered[0], stage + 1)]
        if stage < chip_stages:
            far = [crossed(gathered[1], stage)]
        new, near, far, own_weight = lax.optimization_barrier((new, near, far, own_weight))
        attended = attended + new
        gathered[0] = jnp.concatenate([gathered[0]] + near)
        if stage < chip_stages - 1:
            gathered[1] = jnp.concatenate([gathered[1]] + far)
        elif far:
            last = far[0]
    weights = [part.reshape(-1, cols) for part in gathered + [last]]
    layout = [(k, x) for k in range(chips) for x in groups[0]]
    layout += [(k, x) for k in range(chips) for x in groups[1]]

    result = project(attended, own_weight, weights, layout, 0, place, chips)
    moved = [result[0]] + [paired(part, x) for part, x in zip(result[1:], others)]
    weights = [swapped(part) for part in weights]
    out = assemble(moved, 0, width, place)
    result = project(attended, own_weight, weights, layout, 1, place, chips)
    moved = [result[0]] + [paired(part, x) for part, x in zip(result[1:], others)]
    return assemble(moved, 1, width, place, out)


def solution(mesh):
    placed = (P("ctx", "head"), P("ctx", None), P("ctx", None), P(), P("head", None))
    return jax.shard_map(
        body, mesh=mesh, in_specs=placed, out_specs=P(("ctx", "head"), None), check_vma=False
    )
```

time: 123 us -> 96.6 us (0.79)
  waiting for transfers between devices: 76.7 us -> 37.9 us
  starting transfers between devices: 18.8 us -> 41.2 us
  between operations: 13.7 us -> 0.16 us
  Pallas kernels: 0 us -> 10.3 us
  matrix products: 8.62 us -> 0 us
  local copies, waits for them, and re-layouts: 1.86 us -> 5.53 us
  other arithmetic: 2.79 us -> 1.16 us
    reduce_scatter x1 -> x0, waiting for transfers between devices: 76.6 us -> none  [body(): lax.psum_scatter(jnp.dot(attended, out_weight, preferred_element_type=jnp...]
    ppermute x8 -> x22, waiting for transfers between devices: 0.02 us -> 37.9 us  [the longest x11 32.2 us: paired(): return lax.ppermute(shard, 'head', [(i, i ^ x) for i in range(length)])]
    ppermute x8 -> x22, starting transfers between devices: 18.8 us -> 41.2 us  [the longest x11 21.8 us: paired(): return lax.ppermute(shard, 'head', [(i, i ^ x) for i in range(length)])]
    pallas_call x0 -> x5, Pallas kernels: none -> 10.3 us  [the longest x1 3.86 us: attention(): pl.pallas_call(attention_kernel, out_shape=jax.ShapeDtypeStruct(queries.s...]
    dot_general x11 -> x0, matrix products: 8.62 us -> none  [the longest x1 4.44 us: body(): jnp.dot(attended, out_weight, preferred_element_type=jnp.float32)]
    dynamic_slice x0 -> x2, local copies, waits for them, and re-layouts: none -> 2.89 us  [the longest x1 1.73 us: body(): lax.dynamic_slice_in_dim(tie(out_weight, attended), head_index * CORES *...]
  transfers between devices with their start and end apart: 9 -> 22, of which waited for: 1 -> 11; matrix products, arithmetic and copies ran while one was open for 6% -> 5% of each run, Pallas kernels for 0% -> 9%
where the time goes in v1:
time: 96.6 us; the launch traced here: 96.2 us
  starting transfers between devices  41.2 us (43%)
  waiting for transfers between devices  37.9 us (39%)
  Pallas kernels  10.3 us (11%)
  local copies, waits for them, and re-layouts  5.53 us (6%)
  other arithmetic  1.16 us (1%)
    ppermute x11, waiting for transfers between devices, paired(): return lax.ppermute(shard, 'head', [(i, i ^ x) for i in range(length)])  32.2 us
    ppermute x11, starting transfers between devices, paired(): return lax.ppermute(shard, 'head', [(i, i ^ x) for i in range(length)])  21.8 us
    ppermute x4, starting transfers between devices, later(): return lax.ppermute(shard, 'ctx', [(i, i + by) for i in range(length - by)])  11.2 us
    ppermute x4, starting transfers between devices, crossed(): lax.ppermute(shard, 'ctx', [(i, i ^ CORES << bit[i % CORES]) for i in ran...  7.55 us
    ppermute x4, waiting for transfers between devices, crossed(): lax.ppermute(shard, 'ctx', [(i, i ^ CORES << bit[i % CORES]) for i in ran...  3.92 us
    pallas_call x1, Pallas kernels, attention(): pl.pallas_call(attention_kernel, out_shape=jax.ShapeDtypeStruct(queries.s...  3.86 us
    pallas_call x2, Pallas kernels, project(): pl.pallas_call(kernel, out_shape=[jax.ShapeDtypeStruct((rows_out, cols),...  3.69 us
    pallas_call x2, Pallas kernels, assemble(): pl.pallas_call(kernel, out_shape=jax.ShapeDtypeStruct((rows, width), jnp....  2.73 us
  transfers between devices with their start and end apart: 22, of which 11 were waited for; matrix products, arithmetic and copies ran while one was open for 5% of the time, Pallas kernels for 9%

profile of v1, /device:TPU:0, one launch (start us, length us, event | category | flops | bytes accessed | tf_op | source)
XLA Modules:
  0.0 96.2 jit_solution(12242898303818640481)
XLA Ops:
  0.0 1.2 %fusion = (bf16[128,1024]{1,0:T(8,128)(2,1)S(1)}, bf16[128,1024]{1,0:T(8,128)(2,1)S(1)}, bf16[128,1024]{1,0:T(8,128)(2,1)S(1)}) fusion(bf16[512,8192]{1,0:T(8,128)(2,1)} %param.9, s32[]{:T(128)S(6)} %select_n.30, s32[]{:T(128)S(6)} %select_n.33, s32[]{:T(128)S(6)} %select_n.32, s32[]{:T(128)S(6)} %select_n.31), kind=kLoop, calls=%fused_computation.10 | loop fusion | bytes 1572880 | tf_op jit(solution)/shard_map/dynamic_slice | solution.py:250
  1.2 5.1 %collective-permute-start.1 = (bf16[128,1024]{1,0:T(8,128)(2,1)S(1)}, bf16[128,1024]{1,0:T(8,128)(2,1)S(1)}, u32[]{:S(2)}, u32[]{:S(2)}) collective-permute-start(bf16[128,1024]{1,0:T(8,128)(2,1)S(1)} %get-tuple-element.48), channel_id=1, source_target_pairs={{0,3},{1,2},{2,1},{3,0},{4,7},{5,6},{6,5},{7,4},{8,11},{9,10},{10,... | collective-permute-start | bytes 786440 | tf_op jit(solution)/shard_map/ppermute | solution.py:213
  8.0 3.4 %collective-permute-start.4 = (bf16[512,128]{1,0:T(8,128)(2,1)S(1)}, bf16[512,128]{1,0:T(8,128)(2,1)S(1)}, u32[]{:S(2)}, u32[]{:S(2)}) collective-permute-start(bf16[512,128]{1,0:T(8,128)(2,1)S(1)} %constant_dynamic-update-slice_fusion.refs_4_), channel_id=1, source_target_pairs={{0,8},{4,12},{8,16},{12,20},{16,24},{20,28},{1,9},{5,13},{9,17},{1... | collective-permute-start | bytes 393224 | tf_op jit(solution)/shard_map/ppermute | solution.py:232
  11.4 2.1 %collective-permute-done.1 = bf16[128,1024]{1,0:T(8,128)(2,1)S(1)} collective-permute-done((bf16[128,1024]{1,0:T(8,128)(2,1)S(1)}, bf16[128,1024]{1,0:T(8,128)(2,1)S(1)}, u32[]{:S(2)}, u32[]{:S(2)}) %collective-permute-start.1) | collective-permute-done | bytes 262176 | tf_op jit(solution)/shard_map/ppermute | solution.py:213
  13.5 5.4 %collective-permute-start.7 = (bf16[128,1024]{1,0:T(8,128)(2,1)S(1)}, bf16[128,1024]{1,0:T(8,128)(2,1)S(1)}, u32[]{:S(2)}, u32[]{:S(2)}) collective-permute-start(bf16[128,1024]{1,0:T(8,128)(2,1)S(1)} %get-tuple-element.27), channel_id=1, source_target_pairs={{0,2},{1,3},{2,0},{3,1},{4,6},{5,7},{6,4},{7,5},{8,10},{9,11},{10,... | collective-permute-start | bytes 786440 | tf_op jit(solution)/shard_map/ppermute | solution.py:213
  18.9 1.5 %collective-permute-start.8 = (bf16[1,1,128,1024]{3,2,1,0:T(8,128)(2,1)S(1)}, bf16[1,1,128,1024]{3,2,1,0:T(8,128)(2,1)S(1)}, u32[]{:S(2)}, u32[]{:S(2)}) collective-permute-start(bf16[1,1,128,1024]{3,2,1,0:T(8,128)(2,1)S(1)} %bitcast.23), channel_id=1, source_target_pairs={{0,8},{4,20},{8,0},{12,28},{16,24},{20,4},{24,16},{28,12},{1,9},{5... | collective-permute-start | bytes 786440 | tf_op jit(solution)/shard_map/ppermute | solution.py:225
  20.4 1.3 %collective-permute-start.5 = (bf16[512,128]{1,0:T(8,128)(2,1)S(1)}, bf16[512,128]{1,0:T(8,128)(2,1)S(1)}, u32[]{:S(2)}, u32[]{:S(2)}) collective-permute-start(bf16[512,128]{1,0:T(8,128)(2,1)S(1)} %constant_dynamic-update-slice_fusion.refs_4_), channel_id=1, source_target_pairs={{0,4},{4,8},{8,12},{12,16},{16,20},{20,24},{24,28},{1,5},{5,9},{9,... | collective-permute-start | bytes 393224 | tf_op jit(solution)/shard_map/ppermute | solution.py:232
  21.7 4.1 %collective-permute-start.2 = (bf16[512,128]{1,0:T(8,128)(2,1)S(1)}, bf16[512,128]{1,0:T(8,128)(2,1)S(1)}, u32[]{:S(2)}, u32[]{:S(2)}) collective-permute-start(bf16[512,128]{1,0:T(8,128)(2,1)S(1)} %constant_dynamic-update-slice_fusion.refs_4_), channel_id=1, source_target_pairs={{0,16},{4,20},{8,24},{12,28},{1,17},{5,21},{9,25},{13,29},{2,18},{... | collective-permute-start | bytes 393224 | tf_op jit(solution)/shard_map/ppermute | solution.py:232
  25.8 2.5 %collective-permute-start.3 = (bf16[512,128]{1,0:T(8,128)(2,1)S(1)}, bf16[512,128]{1,0:T(8,128)(2,1)S(1)}, u32[]{:S(2)}, u32[]{:S(2)}) collective-permute-start(bf16[512,128]{1,0:T(8,128)(2,1)S(1)} %constant_dynamic-update-slice_fusion.refs_4_), channel_id=1, source_target_pairs={{0,12},{4,16},{8,20},{12,24},{16,28},{1,13},{5,17},{9,21},{13,25},... | collective-permute-start | bytes 393224 | tf_op jit(solution)/shard_map/ppermute | solution.py:232
  29.5 1.3 %collective-permute-done.3.refs_1_ = bf16[512,128]{1,0:T(8,128)(2,1)S(1)} collective-permute-done((bf16[512,128]{1,0:T(8,128)(2,1)S(1)}, bf16[512,128]{1,0:T(8,128)(2,1)S(1)}, u32[]{:S(2)}, u32[]{:S(2)}) %collective-permute-start.3) | collective-permute-done | bytes 131104 | tf_op jit(solution)/shard_map/ppermute | solution.py:232
  30.8 0.9 copy-done
  31.7 3.9 %attention.1 = bf16[256,512]{1,0:T(8,128)(2,1)S(1)} custom-call(s32[9]{0:T(128)S(1)} %pad_add_fusion.1.place_ref, bf16[256,512]{1,0:T(8,128)(2,1)S(1)} %copy-done, bf16[512,128]{1,0:T(8,128)(2,1)S(1)} %collective-permute-done.2.refs_0_, bf16[512,128]{1,0:T(8,128)(2,1)S(1)} %collective-permute-done.3.refs_1_, ...), custom_call_target="tpu_custom_call" | custom-call | tf_op jit(solution)/shard_map/attention/pallas_call | solution.py:59
  36.3 3.5 %collective-permute-start.9 = (bf16[2,1,128,1024]{3,2,1,0:T(8,128)(2,1)S(1)}, bf16[2,1,128,1024]{3,2,1,0:T(8,128)(2,1)S(1)}, u32[]{:S(2)}, u32[]{:S(2)}) collective-permute-start(bf16[2,1,128,1024]{3,2,1,0:T(8,128)(2,1)S(1)} %pad_maximum_fusion.2), channel_id=1, source_target_pairs={{0,16},{4,12},{8,24},{12,4},{16,0},{20,28},{24,8},{28,20},{1,17},{... | collective-permute-start | bytes 1572872 | tf_op jit(solution)/shard_map/ppermute | solution.py:225
  39.8 1.3 %collective-permute-start.6 = (bf16[1,256,512]{2,1,0:T(8,128)(2,1)S(1)}, bf16[1,256,512]{2,1,0:T(8,128)(2,1)S(1)}, u32[]{:S(2)}, u32[]{:S(2)}) collective-permute-start(bf16[1,256,512]{2,1,0:T(8,128)(2,1)S(1)} %bitcast.17), channel_id=1, source_target_pairs={{0,3},{1,2},{2,1},{3,0},{4,7},{5,6},{6,5},{7,4},{8,11},{9,10},{10,... | collective-permute-start | bytes 786440 | tf_op jit(solution)/shard_map/ppermute | solution.py:213
  41.2 1.7 %constant_dynamic-slice_fusion.refs_3_ = bf16[512,2048]{1,0:T(8,128)(2,1)S(1)} fusion(bf16[512,8192]{1,0:T(8,128)(2,1)} %param.9, s32[]{:T(128)S(6)} %select_n.34), kind=kLoop, calls=%fused_computation.9 | loop fusion | bytes 4194308 | tf_op jit(solution)/shard_map/dynamic_slice | solution.py:268
  42.9 5.2 %collective-permute-done.6.refs_1_ = bf16[1,256,512]{2,1,0:T(8,128)(2,1)S(1)} collective-permute-done((bf16[1,256,512]{2,1,0:T(8,128)(2,1)S(1)}, bf16[1,256,512]{2,1,0:T(8,128)(2,1)S(1)}, u32[]{:S(2)}, u32[]{:S(2)}) %collective-permute-start.6) | collective-permute-done | bytes 262176 | tf_op jit(solution)/shard_map/ppermute | solution.py:213
  48.1 1.2 %collective-permute-done.10 = bf16[1,2,128,1024]{3,2,1,0:T(8,128)(2,1)S(1)} collective-permute-done((bf16[1,2,128,1024]{3,2,1,0:T(8,128)(2,1)S(1)}, bf16[1,2,128,1024]{3,2,1,0:T(8,128)(2,1)S(1)}, u32[]{:S(2)}, u32[]{:S(2)}) %collective-permute-start.10) | collective-permute-done | bytes 524320 | tf_op jit(solution)/shard_map/ppermute | solution.py:225
  49.3 1.9 %collective-permute-done.9 = bf16[2,1,128,1024]{3,2,1,0:T(8,128)(2,1)S(1)} collective-permute-done((bf16[2,1,128,1024]{3,2,1,0:T(8,128)(2,1)S(1)}, bf16[2,1,128,1024]{3,2,1,0:T(8,128)(2,1)S(1)}, u32[]{:S(2)}, u32[]{:S(2)}) %collective-permute-start.9) | collective-permute-done | bytes 524320 | tf_op jit(solution)/shard_map/ppermute | solution.py:225
  51.3 1.9 %collective-permute-start.12 = (bf16[2,2,128,1024]{3,2,1,0:T(8,128)(2,1)S(1)}, bf16[2,2,128,1024]{3,2,1,0:T(8,128)(2,1)S(1)}, u32[]{:S(2)}, u32[]{:S(2)}) collective-permute-start(bf16[2,2,128,1024]{3,2,1,0:T(8,128)(2,1)S(1)} %pad_maximum_fusion), channel_id=1, source_target_pairs={{0,16},{4,12},{8,24},{12,4},{16,0},{20,28},{24,8},{28,20},{1,17},{... | collective-permute-start | bytes 3145736 | tf_op jit(solution)/shard_map/ppermute | solution.py:225
  53.3 1.5 %collective-permute-start.11 = (bf16[2,256,512]{2,1,0:T(8,128)(2,1)S(1)}, bf16[2,256,512]{2,1,0:T(8,128)(2,1)S(1)}, u32[]{:S(2)}, u32[]{:S(2)}) collective-permute-start(bf16[2,256,512]{2,1,0:T(8,128)(2,1)S(1)} %pad_maximum_fusion.3), channel_id=1, source_target_pairs={{0,1},{1,0},{2,3},{3,2},{4,5},{5,4},{6,7},{7,6},{8,9},{9,8},{10,11... | collective-permute-start | bytes 1572872 | tf_op jit(solution)/shard_map/ppermute | solution.py:213
  55.4 9.8 %collective-permute-done.11.refs_2_ = bf16[2,256,512]{2,1,0:T(8,128)(2,1)S(1)} collective-permute-done((bf16[2,256,512]{2,1,0:T(8,128)(2,1)S(1)}, bf16[2,256,512]{2,1,0:T(8,128)(2,1)S(1)}, u32[]{:S(2)}, u32[]{:S(2)}) %collective-permute-start.11) | collective-permute-done | bytes 524320 | tf_op jit(solution)/shard_map/ppermute | solution.py:213
  65.3 0.9 collective-permute-done.12
  66.2 1.9 %project.3 = (bf16[64,1024]{1,0:T(8,128)(2,1)S(1)}, bf16[64,1024]{1,0:T(8,128)(2,1)S(1)}, bf16[64,1024]{1,0:T(8,128)(2,1)S(1)}, bf16[64,1024]{1,0:T(8,128)(2,1)S(1)}) custom-call(s32[3]{0:T(128)S(1)} %pad_add_fusion.place_ref, bf16[1,256,512]{2,1,0:T(8,128)(2,1)S(1)} %bitcast.19, bf16[1,256,512]{2,1,0:T(8,128)(2,1)S(1)} %collective-permute-done.6.refs_1_, ...), custom_call_target="tpu_custom_call" | custom-call | flops 1073741824 | bytes 5767168 | tf_op jit(solution)/shard_map/project/pallas_call | solution.py:156
  68.1 1.4 %collective-permute-start.19 = (bf16[64,1024]{1,0:T(8,128)(2,1)S(1)}, bf16[64,1024]{1,0:T(8,128)(2,1)S(1)}, u32[]{:S(2)}, u32[]{:S(2)}) collective-permute-start(bf16[64,1024]{1,0:T(8,128)(2,1)S(1)} %get-tuple-element.44), channel_id=1, source_target_pairs={{0,3},{1,2},{2,1},{3,0},{4,7},{5,6},{6,5},{7,4},{8,11},{9,10},{10,... | collective-permute-start | bytes 393224 | tf_op jit(solution)/shard_map/ppermute | solution.py:213
  70.1 2.4 %collective-permute-start.21 = (bf16[64,1024]{1,0:T(8,128)(2,1)S(1)}, bf16[64,1024]{1,0:T(8,128)(2,1)S(1)}, u32[]{:S(2)}, u32[]{:S(2)}) collective-permute-start(bf16[64,1024]{1,0:T(8,128)(2,1)S(1)} %get-tuple-element.46), channel_id=1, source_target_pairs={{0,2},{1,3},{2,0},{3,1},{4,6},{5,7},{6,4},{7,5},{8,10},{9,11},{10,... | collective-permute-start | bytes 393224 | tf_op jit(solution)/shard_map/ppermute | solution.py:213
  72.5 1.8 %project.2 = (bf16[64,1024]{1,0:T(8,128)(2,1)S(1)}, bf16[64,1024]{1,0:T(8,128)(2,1)S(1)}, bf16[64,1024]{1,0:T(8,128)(2,1)S(1)}, bf16[64,1024]{1,0:T(8,128)(2,1)S(1)}) custom-call(s32[3]{0:T(128)S(1)} %pad_add_fusion.place_ref, bf16[1,256,512]{2,1,0:T(8,128)(2,1)S(1)} %bitcast.20, bf16[1,256,512]{2,1,0:T(8,128)(2,1)S(1)} %collective-permute-done.6.refs_1_, ...), custom_call_target="tpu_custom_call" | custom-call | flops 1073741824 | bytes 5767168 | tf_op jit(solution)/shard_map/project/pallas_call | solution.py:156
  74.4 1.4 %collective-permute-start.16 = (bf16[64,1024]{1,0:T(8,128)(2,1)S(1)}, bf16[64,1024]{1,0:T(8,128)(2,1)S(1)}, u32[]{:S(2)}, u32[]{:S(2)}) collective-permute-start(bf16[64,1024]{1,0:T(8,128)(2,1)S(1)} %get-tuple-element.40), channel_id=1, source_target_pairs={{0,3},{1,2},{2,1},{3,0},{4,7},{5,6},{6,5},{7,4},{8,11},{9,10},{10,... | collective-permute-start | bytes 393224 | tf_op jit(solution)/shard_map/ppermute | solution.py:213
  76.3 2.6 %collective-permute-start.18 = (bf16[64,1024]{1,0:T(8,128)(2,1)S(1)}, bf16[64,1024]{1,0:T(8,128)(2,1)S(1)}, u32[]{:S(2)}, u32[]{:S(2)}) collective-permute-start(bf16[64,1024]{1,0:T(8,128)(2,1)S(1)} %get-tuple-element.42), channel_id=1, source_target_pairs={{0,2},{1,3},{2,0},{3,1},{4,6},{5,7},{6,4},{7,5},{8,10},{9,11},{10,... | collective-permute-start | bytes 393224 | tf_op jit(solution)/shard_map/ppermute | solution.py:213
  78.8 8.0 %collective-permute-done.21.refs_3_ = bf16[64,1024]{1,0:T(8,128)(2,1)S(1)} collective-permute-done((bf16[64,1024]{1,0:T(8,128)(2,1)S(1)}, bf16[64,1024]{1,0:T(8,128)(2,1)S(1)}, u32[]{:S(2)}, u32[]{:S(2)}) %collective-permute-start.21) | collective-permute-done | bytes 131104 | tf_op jit(solution)/shard_map/ppermute | solution.py:213
  86.8 1.4 %assemble.2.refs_4_ = bf16[64,8192]{1,0:T(8,128)(2,1)} custom-call(s32[3]{0:T(128)S(1)} %pad_add_fusion.place_ref, bf16[64,1024]{1,0:T(8,128)(2,1)S(1)} %get-tuple-element.43.refs_0_, bf16[64,1024]{1,0:T(8,128)(2,1)S(1)} %collective-permute-done.19.refs_1_, bf16[64,1024]{1,0:T(8,128)(2,1)S(1)} %collective-permute-done.20.refs_2_, ...), custom_call_target="tpu_custom_call" | custom-call | tf_op jit(solution)/shard_map/assemble/pallas_call | solution.py:197
  88.2 6.6 %collective-permute-done.18.refs_3_ = bf16[64,1024]{1,0:T(8,128)(2,1)S(1)} collective-permute-done((bf16[64,1024]{1,0:T(8,128)(2,1)S(1)}, bf16[64,1024]{1,0:T(8,128)(2,1)S(1)}, u32[]{:S(2)}, u32[]{:S(2)}) %collective-permute-start.18) | collective-permute-done | bytes 131104 | tf_op jit(solution)/shard_map/ppermute | solution.py:213
  94.9 1.4 %assemble.3 = bf16[64,8192]{1,0:T(8,128)(2,1)} custom-call(s32[3]{0:T(128)S(1)} %pad_add_fusion.place_ref, bf16[64,1024]{1,0:T(8,128)(2,1)S(1)} %get-tuple-element.39.refs_0_, bf16[64,1024]{1,0:T(8,128)(2,1)S(1)} %collective-permute-done.16.refs_1_, bf16[64,1024]{1,0:T(8,128)(2,1)S(1)} %collective-permute-done.17.refs_2_, ...), custom_call_target="tpu_custom_call", output_to_operand_aliasing={{}: (5, {})} | custom-call | tf_op jit(solution)/shard_map/assemble/pallas_call | solution.py:197
  (30 shorter events, 5.7 us)
Async XLA Ops:
  1.2 12.3 %collective-permute-start.1 = (bf16[128,1024]{1,0:T(8,128)(2,1)S(1)}, bf16[128,1024]{1,0:T(8,128)(2,1)S(1)}, u32[]{:S(2)}, u32[]{:S(2)}) collective-permute-start(bf16[128,1024]{1,0:T(8,128)(2,1)S(1)} %get-tuple-element.48), channel_id=1, source_target_pairs={{0,3},{1,2},{2,1},{3,0},{4,7},{5,6},{6,5},{7,4},{8,11},{9,10},{10,... | collective-permute-start | bytes 786440 | tf_op jit(solution)/shard_map/ppermute | solution.py:213
  6.3 12.7 %collective-permute-start = (bf16[128,1024]{1,0:T(8,128)(2,1)S(1)}, bf16[128,1024]{1,0:T(8,128)(2,1)S(1)}, u32[]{:S(2)}, u32[]{:S(2)}) collective-permute-start(bf16[128,1024]{1,0:T(8,128)(2,1)S(1)} %get-tuple-element.49), channel_id=1, source_target_pairs={{0,1},{1,0},{2,3},{3,2},{4,5},{5,4},{6,7},{7,6},{8,9},{9,8},{10,11... | collective-permute-start | bytes 786440 | tf_op jit(solution)/shard_map/ppermute | solution.py:213
  8.0 17.8 %collective-permute-start.4 = (bf16[512,128]{1,0:T(8,128)(2,1)S(1)}, bf16[512,128]{1,0:T(8,128)(2,1)S(1)}, u32[]{:S(2)}, u32[]{:S(2)}) collective-permute-start(bf16[512,128]{1,0:T(8,128)(2,1)S(1)} %constant_dynamic-update-slice_fusion.refs_4_), channel_id=1, source_target_pairs={{0,8},{4,12},{8,16},{12,20},{16,24},{20,28},{1,9},{5,13},{9,17},{1... | collective-permute-start | bytes 393224 | tf_op jit(solution)/shard_map/ppermute | solution.py:232
  13.5 22.1 %collective-permute-start.7 = (bf16[128,1024]{1,0:T(8,128)(2,1)S(1)}, bf16[128,1024]{1,0:T(8,128)(2,1)S(1)}, u32[]{:S(2)}, u32[]{:S(2)}) collective-permute-start(bf16[128,1024]{1,0:T(8,128)(2,1)S(1)} %get-tuple-element.27), channel_id=1, source_target_pairs={{0,2},{1,3},{2,0},{3,1},{4,6},{5,7},{6,4},{7,5},{8,10},{9,11},{10,... | collective-permute-start | bytes 786440 | tf_op jit(solution)/shard_map/ppermute | solution.py:213
  18.9 16.7 %collective-permute-start.8 = (bf16[1,1,128,1024]{3,2,1,0:T(8,128)(2,1)S(1)}, bf16[1,1,128,1024]{3,2,1,0:T(8,128)(2,1)S(1)}, u32[]{:S(2)}, u32[]{:S(2)}) collective-permute-start(bf16[1,1,128,1024]{3,2,1,0:T(8,128)(2,1)S(1)} %bitcast.23), channel_id=1, source_target_pairs={{0,8},{4,20},{8,0},{12,28},{16,24},{20,4},{24,16},{28,12},{1,9},{5... | collective-permute-start | bytes 786440 | tf_op jit(solution)/shard_map/ppermute | solution.py:225
  20.4 8.6 %collective-permute-start.5 = (bf16[512,128]{1,0:T(8,128)(2,1)S(1)}, bf16[512,128]{1,0:T(8,128)(2,1)S(1)}, u32[]{:S(2)}, u32[]{:S(2)}) collective-permute-start(bf16[512,128]{1,0:T(8,128)(2,1)S(1)} %constant_dynamic-update-slice_fusion.refs_4_), channel_id=1, source_target_pairs={{0,4},{4,8},{8,12},{12,16},{16,20},{20,24},{24,28},{1,5},{5,9},{9,... | collective-permute-start | bytes 393224 | tf_op jit(solution)/shard_map/ppermute | solution.py:232
  21.7 7.8 %collective-permute-start.2 = (bf16[512,128]{1,0:T(8,128)(2,1)S(1)}, bf16[512,128]{1,0:T(8,128)(2,1)S(1)}, u32[]{:S(2)}, u32[]{:S(2)}) collective-permute-start(bf16[512,128]{1,0:T(8,128)(2,1)S(1)} %constant_dynamic-update-slice_fusion.refs_4_), channel_id=1, source_target_pairs={{0,16},{4,20},{8,24},{12,28},{1,17},{5,21},{9,25},{13,29},{2,18},{... | collective-permute-start | bytes 393224 | tf_op jit(solution)/shard_map/ppermute | solution.py:232
  25.8 5.0 %collective-permute-start.3 = (bf16[512,128]{1,0:T(8,128)(2,1)S(1)}, bf16[512,128]{1,0:T(8,128)(2,1)S(1)}, u32[]{:S(2)}, u32[]{:S(2)}) collective-permute-start(bf16[512,128]{1,0:T(8,128)(2,1)S(1)} %constant_dynamic-update-slice_fusion.refs_4_), channel_id=1, source_target_pairs={{0,12},{4,16},{8,20},{12,24},{16,28},{1,13},{5,17},{9,21},{13,25},... | collective-permute-start | bytes 393224 | tf_op jit(solution)/shard_map/ppermute | solution.py:232
  30.8 0.9 copy-start
  35.7 13.6 %collective-permute-start.10 = (bf16[1,2,128,1024]{3,2,1,0:T(8,128)(2,1)S(1)}, bf16[1,2,128,1024]{3,2,1,0:T(8,128)(2,1)S(1)}, u32[]{:S(2)}, u32[]{:S(2)}) collective-permute-start(bf16[1,2,128,1024]{3,2,1,0:T(8,128)(2,1)S(1)} %maximum_bitcast_fusion), channel_id=1, source_target_pairs={{0,8},{4,20},{8,0},{12,28},{16,24},{20,4},{24,16},{28,12},{1,9},{5... | collective-permute-start | bytes 1572872 | tf_op jit(solution)/shard_map/ppermute | solution.py:225
  36.3 14.8 %collective-permute-start.9 = (bf16[2,1,128,1024]{3,2,1,0:T(8,128)(2,1)S(1)}, bf16[2,1,128,1024]{3,2,1,0:T(8,128)(2,1)S(1)}, u32[]{:S(2)}, u32[]{:S(2)}) collective-permute-start(bf16[2,1,128,1024]{3,2,1,0:T(8,128)(2,1)S(1)} %pad_maximum_fusion.2), channel_id=1, source_target_pairs={{0,16},{4,12},{8,24},{12,4},{16,0},{20,28},{24,8},{28,20},{1,17},{... | collective-permute-start | bytes 1572872 | tf_op jit(solution)/shard_map/ppermute | solution.py:225
  39.8 8.3 %collective-permute-start.6 = (bf16[1,256,512]{2,1,0:T(8,128)(2,1)S(1)}, bf16[1,256,512]{2,1,0:T(8,128)(2,1)S(1)}, u32[]{:S(2)}, u32[]{:S(2)}) collective-permute-start(bf16[1,256,512]{2,1,0:T(8,128)(2,1)S(1)} %bitcast.17), channel_id=1, source_target_pairs={{0,3},{1,2},{2,1},{3,0},{4,7},{5,6},{6,5},{7,4},{8,11},{9,10},{10,... | collective-permute-start | bytes 786440 | tf_op jit(solution)/shard_map/ppermute | solution.py:213
  51.3 14.9 %collective-permute-start.12 = (bf16[2,2,128,1024]{3,2,1,0:T(8,128)(2,1)S(1)}, bf16[2,2,128,1024]{3,2,1,0:T(8,128)(2,1)S(1)}, u32[]{:S(2)}, u32[]{:S(2)}) collective-permute-start(bf16[2,2,128,1024]{3,2,1,0:T(8,128)(2,1)S(1)} %pad_maximum_fusion), channel_id=1, source_target_pairs={{0,16},{4,12},{8,24},{12,4},{16,0},{20,28},{24,8},{28,20},{1,17},{... | collective-permute-start | bytes 3145736 | tf_op jit(solution)/shard_map/ppermute | solution.py:225
  53.3 12.0 %collective-permute-start.11 = (bf16[2,256,512]{2,1,0:T(8,128)(2,1)S(1)}, bf16[2,256,512]{2,1,0:T(8,128)(2,1)S(1)}, u32[]{:S(2)}, u32[]{:S(2)}) collective-permute-start(bf16[2,256,512]{2,1,0:T(8,128)(2,1)S(1)} %pad_maximum_fusion.3), channel_id=1, source_target_pairs={{0,1},{1,0},{2,3},{3,2},{4,5},{5,4},{6,7},{7,6},{8,9},{9,8},{10,11... | collective-permute-start | bytes 1572872 | tf_op jit(solution)/shard_map/ppermute | solution.py:213
  54.9 15.3 %collective-permute-start.13 = (bf16[512,1024]{1,0:T(8,128)(2,1)S(1)}, bf16[512,1024]{1,0:T(8,128)(2,1)S(1)}, u32[]{:S(2)}, u32[]{:S(2)}) collective-permute-start(bf16[512,1024]{1,0:T(8,128)(2,1)S(1)} %bitcast.15), channel_id=1, source_target_pairs={{0,4},{4,0},{8,12},{12,8},{16,20},{20,16},{24,28},{28,24},{1,5},{5... | collective-permute-start | bytes 3145736 | tf_op jit(solution)/shard_map/ppermute | solution.py:218
  54.9 17.6 %collective-permute-start.14 = (bf16[512,1024]{1,0:T(8,128)(2,1)S(1)}, bf16[512,1024]{1,0:T(8,128)(2,1)S(1)}, u32[]{:S(2)}, u32[]{:S(2)}) collective-permute-start(bf16[512,1024]{1,0:T(8,128)(2,1)S(1)} %bitcast.13), channel_id=1, source_target_pairs={{0,4},{4,0},{8,12},{12,8},{16,20},{20,16},{24,28},{28,24},{1,5},{5... | collective-permute-start | bytes 3145736 | tf_op jit(solution)/shard_map/ppermute | solution.py:218
  66.1 6.4 %collective-permute-start.15 = (bf16[512,1024]{1,0:T(8,128)(2,1)S(1)}, bf16[512,1024]{1,0:T(8,128)(2,1)S(1)}, u32[]{:S(2)}, u32[]{:S(2)}) collective-permute-start(bf16[512,1024]{1,0:T(8,128)(2,1)S(1)} %bitcast.21), channel_id=1, source_target_pairs={{0,4},{4,0},{8,12},{12,8},{16,20},{20,16},{24,28},{28,24},{1,5},{5... | collective-permute-start | bytes 3145736 | tf_op jit(solution)/shard_map/ppermute | solution.py:218
  68.1 8.2 %collective-permute-start.19 = (bf16[64,1024]{1,0:T(8,128)(2,1)S(1)}, bf16[64,1024]{1,0:T(8,128)(2,1)S(1)}, u32[]{:S(2)}, u32[]{:S(2)}) collective-permute-start(bf16[64,1024]{1,0:T(8,128)(2,1)S(1)} %get-tuple-element.44), channel_id=1, source_target_pairs={{0,3},{1,2},{2,1},{3,0},{4,7},{5,6},{6,5},{7,4},{8,11},{9,10},{10,... | collective-permute-start | bytes 393224 | tf_op jit(solution)/shard_map/ppermute | solution.py:213
  69.5 9.4 %collective-permute-start.20 = (bf16[64,1024]{1,0:T(8,128)(2,1)S(1)}, bf16[64,1024]{1,0:T(8,128)(2,1)S(1)}, u32[]{:S(2)}, u32[]{:S(2)}) collective-permute-start(bf16[64,1024]{1,0:T(8,128)(2,1)S(1)} %get-tuple-element.45), channel_id=1, source_target_pairs={{0,1},{1,0},{2,3},{3,2},{4,5},{5,4},{6,7},{7,6},{8,9},{9,8},{10,11... | collective-permute-start | bytes 393224 | tf_op jit(solution)/shard_map/ppermute | solution.py:213
  70.1 16.7 %collective-permute-start.21 = (bf16[64,1024]{1,0:T(8,128)(2,1)S(1)}, bf16[64,1024]{1,0:T(8,128)(2,1)S(1)}, u32[]{:S(2)}, u32[]{:S(2)}) collective-permute-start(bf16[64,1024]{1,0:T(8,128)(2,1)S(1)} %get-tuple-element.46), channel_id=1, source_target_pairs={{0,2},{1,3},{2,0},{3,1},{4,6},{5,7},{6,4},{7,5},{8,10},{9,11},{10,... | collective-permute-start | bytes 393224 | tf_op jit(solution)/shard_map/ppermute | solution.py:213
  74.4 13.8 %collective-permute-start.16 = (bf16[64,1024]{1,0:T(8,128)(2,1)S(1)}, bf16[64,1024]{1,0:T(8,128)(2,1)S(1)}, u32[]{:S(2)}, u32[]{:S(2)}) collective-permute-start(bf16[64,1024]{1,0:T(8,128)(2,1)S(1)} %get-tuple-element.40), channel_id=1, source_target_pairs={{0,3},{1,2},{2,1},{3,0},{4,7},{5,6},{6,5},{7,4},{8,11},{9,10},{10,... | collective-permute-start | bytes 393224 | tf_op jit(solution)/shard_map/ppermute | solution.py:213
  75.8 12.4 %collective-permute-start.17 = (bf16[64,1024]{1,0:T(8,128)(2,1)S(1)}, bf16[64,1024]{1,0:T(8,128)(2,1)S(1)}, u32[]{:S(2)}, u32[]{:S(2)}) collective-permute-start(bf16[64,1024]{1,0:T(8,128)(2,1)S(1)} %get-tuple-element.41), channel_id=1, source_target_pairs={{0,1},{1,0},{2,3},{3,2},{4,5},{5,4},{6,7},{7,6},{8,9},{9,8},{10,11... | collective-permute-start | bytes 393224 | tf_op jit(solution)/shard_map/ppermute | solution.py:213
  76.3 18.6 %collective-permute-start.18 = (bf16[64,1024]{1,0:T(8,128)(2,1)S(1)}, bf16[64,1024]{1,0:T(8,128)(2,1)S(1)}, u32[]{:S(2)}, u32[]{:S(2)}) collective-permute-start(bf16[64,1024]{1,0:T(8,128)(2,1)S(1)} %get-tuple-element.42), channel_id=1, source_target_pairs={{0,2},{1,3},{2,0},{3,1},{4,6},{5,7},{6,4},{7,5},{8,10},{9,11},{10,... | collective-permute-start | bytes 393224 | tf_op jit(solution)/shard_map/ppermute | solution.py:213

commit v2 on v1

--- a/solution.py
+++ b/solution.py
@@ -250,45 +250,45 @@
         return lax.dynamic_slice(out_weight, (chip * share, column), (share, cols))
 
     fetched = {x: paired(share_of(x), x) for x in others if x in (1, planes - 1)}
-    for x in others:
-        if x not in fetched:
-            fetched[x] = paired(tie(share_of(x), fetched[planes - 1]), x)
-
     own = [key_rows, value_rows]
     if key_rows.shape[1] > HD:
         column = head_index * heads // GROUP * HD
         own = [lax.dynamic_slice_in_dim(part, column, HD, 1) for part in own]
     own = jnp.concatenate(own)
-    late = tie(own, [fetched[1], fetched[planes - 1]])
-    pieces = [later(own if d < 3 else late, d) for d in range(SPAN, 0, -1)] + [own]
-    groups = [[1], [x for x in others if x > 1]]
-    gathered = [fetched[1][None, None]]
-    near = crossed(gathered[0], 0)
+    pieces = [later(own, d) for d in range(SPAN, 0, -1)] + [own]
+    for x in others:
+        if x not in fetched:
+            fetched[x] = paired(tie(share_of(x), (fetched[planes - 1], pieces[1:-1])), x)
+    groups = [[x for x in others if x in (1, planes - 1)]]
+    groups.append([x for x in others if x not in groups[0]])
+    plane_stages, chip_stages = planes.bit_length() - 1, chips.bit_length() - 1
+    first = jnp.stack(tie([fetched[x] for x in groups[0]], pieces[1:-1]))[None]
+    first = jnp.concatenate([first, crossed(first, 0)])
+    pieces, first = lax.optimization_barrier((pieces, first))
+    rest = crossed(first, 1)
     attended = [attention(queries, pieces, lengths, ctx_index * rows)[None]]
     own_weight = lax.dynamic_slice_in_dim(
         tie(out_weight, attended), head_index * CORES * cols, CORES * cols, 1
     )
 
-    shares, near, _ = lax.optimization_barrier(([fetched[x] for x in groups[1]], near, attended))
-    gathered = [jnp.concatenate([gathered[0], near]), jnp.stack(shares)[None]]
-    last = None
-    plane_stages, chip_stages = planes.bit_length() - 1, chips.bit_length() - 1
+    second = jnp.stack(tie([fetched[x] for x in groups[1]], (attended, first)))[None]
+    early, latest = [], attended
     for stage in range(max(plane_stages, chip_stages)):
-        new, near, far = [], [], []
+        ahead, new, more = [], [], []
         if stage < plane_stages:
-            new = [paired(jnp.concatenate(attended), (planes - 1) >> stage)]
-        if stage < chip_stages - 1:
-            near = [crossed(gathered[0], stage + 1)]
+            new = [paired(jnp.concatenate(latest), (planes - 1) >> stage)]
+        if stage + 1 < plane_stages:
+            ahead = [paired(jnp.concatenate(attended), (planes - 1) >> (stage + 1))]
         if stage < chip_stages:
-            far = [crossed(gathered[1], stage)]
-        new, near, far, own_weight = lax.optimization_barrier((new, near, far, own_weight))
-        attended = attended + new
-        gathered[0] = jnp.concatenate([gathered[0]] + near)
-        if stage < chip_stages - 1:
-            gathered[1] = jnp.concatenate([gathered[1]] + far)
-        elif far:
-            last = far[0]
-    weights = [part.reshape(-1, cols) for part in gathered + [last]]
+            more = [crossed(second, stage)]
+        ahead, new, more, own_weight = lax.optimization_barrier((ahead, new, more, own_weight))
+        latest = early + new
+        attended, early = attended + latest, ahead
+        second = jnp.concatenate([second] + more)
+        if stage > 0 and stage + 1 < chip_stages:
+            first, rest = jnp.concatenate([first, rest]), None
+            rest = crossed(first, stage + 1)
+    weights = [part.reshape(-1, cols) for part in (first, rest, second)]
     layout = [(k, x) for k in range(chips) for x in groups[0]]
     layout += [(k, x) for k in range(chips) for x in groups[1]]
 

time: 96.6 us -> 88.3 us (0.914)
  waiting for transfers between devices: 37.9 us -> 30.6 us
  starting transfers between devices: 41.2 us -> 40.1 us
    ppermute x11 -> x12, waiting for transfers between devices: 32.2 us -> 18.1 us  [paired(): return lax.ppermute(shard, 'head', [(i, i ^ x) for i in range(length)])]
    ppermute x4, waiting for transfers between devices: 3.92 us -> 11.3 us  [crossed(): lax.ppermute(shard, 'ctx', [(i, i ^ CORES << bit[i % CORES]) for i in ran...]
    ppermute x11 -> x12, starting transfers between devices: 21.8 us -> 19.5 us  [paired(): return lax.ppermute(shard, 'head', [(i, i ^ x) for i in range(length)])]
    ppermute x4, starting transfers between devices: 7.55 us -> 9.59 us  [crossed(): lax.ppermute(shard, 'ctx', [(i, i ^ CORES << bit[i % CORES]) for i in ran...]
  transfers between devices with their start and end apart: 22 -> 23, of which waited for: 11 -> 9; matrix products, arithmetic and copies ran while one was open for 5% -> 5% of each run, Pallas kernels for 9% -> 10%
where the time goes in v2:
time: 88.3 us; the launch traced here: 87.9 us
  starting transfers between devices  40.1 us (45%)
  waiting for transfers between devices  30.6 us (35%)
  Pallas kernels  10.3 us (12%)
  local copies, waits for them, and re-layouts  5.63 us (6%)
  other arithmetic  1.11 us (1%)
    ppermute x12, starting transfers between devices, paired(): return lax.ppermute(shard, 'head', [(i, i ^ x) for i in range(length)])  19.5 us
    ppermute x12, waiting for transfers between devices, paired(): return lax.ppermute(shard, 'head', [(i, i ^ x) for i in range(length)])  18.1 us
    ppermute x4, waiting for transfers between devices, crossed(): lax.ppermute(shard, 'ctx', [(i, i ^ CORES << bit[i % CORES]) for i in ran...  11.3 us
    ppermute x4, starting transfers between devices, later(): return lax.ppermute(shard, 'ctx', [(i, i + by) for i in range(length - by)])  10.4 us
    ppermute x4, starting transfers between devices, crossed(): lax.ppermute(shard, 'ctx', [(i, i ^ CORES << bit[i % CORES]) for i in ran...  9.59 us
    pallas_call x1, Pallas kernels, attention(): pl.pallas_call(attention_kernel, out_shape=jax.ShapeDtypeStruct(queries.s...  3.85 us
    pallas_call x2, Pallas kernels, project(): pl.pallas_call(kernel, out_shape=[jax.ShapeDtypeStruct((rows_out, cols),...  3.71 us
    pallas_call x2, Pallas kernels, assemble(): pl.pallas_call(kernel, out_shape=jax.ShapeDtypeStruct((rows, width), jnp....  2.73 us
  transfers between devices with their start and end apart: 23, of which 9 were waited for; matrix products, arithmetic and copies ran while one was open for 5% of the time, Pallas kernels for 10%

profile of v2, /device:TPU:0, one launch (start us, length us, event | category | flops | bytes accessed | tf_op | source)
XLA Modules:
  0.0 87.9 jit_solution(4287481025246281144)
XLA Ops:
  0.0 1.2 %fusion = (bf16[128,1024]{1,0:T(8,128)(2,1)S(1)}, bf16[128,1024]{1,0:T(8,128)(2,1)S(1)}, bf16[128,1024]{1,0:T(8,128)(2,1)S(1)}) fusion(bf16[512,8192]{1,0:T(8,128)(2,1)} %param.9, s32[]{:T(128)S(6)} %select_n.30, s32[]{:T(128)S(6)} %select_n.33, s32[]{:T(128)S(6)} %select_n.32, s32[]{:T(128)S(6)} %select_n.31), kind=kLoop, calls=%fused_computation.9 | loop fusion | bytes 1572880 | tf_op jit(solution)/shard_map/dynamic_slice | solution.py:250
  1.2 5.1 %collective-permute-start.4 = (bf16[128,1024]{1,0:T(8,128)(2,1)S(1)}, bf16[128,1024]{1,0:T(8,128)(2,1)S(1)}, u32[]{:S(2)}, u32[]{:S(2)}) collective-permute-start(bf16[128,1024]{1,0:T(8,128)(2,1)S(1)} %get-tuple-element.59), channel_id=1, source_target_pairs={{0,3},{1,2},{2,1},{3,0},{4,7},{5,6},{6,5},{7,4},{8,11},{9,10},{10,... | collective-permute-start | bytes 786440 | tf_op jit(solution)/shard_map/ppermute | solution.py:213
  6.3 0.8 constant_dynamic-update-slice_fusion.1
  7.1 0.9 constant_dynamic-update-slice_fusion.refs_4_
  8.0 2.6 %collective-permute-start.1 = (bf16[512,128]{1,0:T(8,128)(2,1)S(1)}, bf16[512,128]{1,0:T(8,128)(2,1)S(1)}, u32[]{:S(2)}, u32[]{:S(2)}) collective-permute-start(bf16[512,128]{1,0:T(8,128)(2,1)S(1)} %constant_dynamic-update-slice_fusion.refs_4_), channel_id=1, source_target_pairs={{0,12},{4,16},{8,20},{12,24},{16,28},{1,13},{5,17},{9,21},{13,25},... | collective-permute-start | bytes 393224 | tf_op jit(solution)/shard_map/ppermute | solution.py:232
  10.5 3.4 %collective-permute-start.2 = (bf16[512,128]{1,0:T(8,128)(2,1)S(1)}, bf16[512,128]{1,0:T(8,128)(2,1)S(1)}, u32[]{:S(2)}, u32[]{:S(2)}) collective-permute-start(bf16[512,128]{1,0:T(8,128)(2,1)S(1)} %constant_dynamic-update-slice_fusion.refs_4_), channel_id=1, source_target_pairs={{0,8},{4,12},{8,16},{12,20},{16,24},{20,28},{1,9},{5,13},{9,17},{1... | collective-permute-start | bytes 393224 | tf_op jit(solution)/shard_map/ppermute | solution.py:232
  14.0 2.6 %collective-permute-start.3 = (bf16[512,128]{1,0:T(8,128)(2,1)S(1)}, bf16[512,128]{1,0:T(8,128)(2,1)S(1)}, u32[]{:S(2)}, u32[]{:S(2)}) collective-permute-start(bf16[512,128]{1,0:T(8,128)(2,1)S(1)} %constant_dynamic-update-slice_fusion.refs_4_), channel_id=1, source_target_pairs={{0,4},{4,8},{8,12},{12,16},{16,20},{20,24},{24,28},{1,5},{5,9},{9,... | collective-permute-start | bytes 393224 | tf_op jit(solution)/shard_map/ppermute | solution.py:232
  16.6 1.2 %collective-permute-done.2.refs_2_ = bf16[512,128]{1,0:T(8,128)(2,1)S(1)} collective-permute-done((bf16[512,128]{1,0:T(8,128)(2,1)S(1)}, bf16[512,128]{1,0:T(8,128)(2,1)S(1)}, u32[]{:S(2)}, u32[]{:S(2)}) %collective-permute-start.2) | collective-permute-done | bytes 131104 | tf_op jit(solution)/shard_map/ppermute | solution.py:232
  18.4 3.5 %collective-permute-start.6 = (bf16[1,2,128,1024]{3,2,1,0:T(8,128)(2,1)S(1)}, bf16[1,2,128,1024]{3,2,1,0:T(8,128)(2,1)S(1)}, u32[]{:S(2)}, u32[]{:S(2)}) collective-permute-start(bf16[1,2,128,1024]{3,2,1,0:T(8,128)(2,1)S(1)} %maximum_bitcast_fusion), channel_id=1, source_target_pairs={{0,8},{4,20},{8,0},{12,28},{16,24},{20,4},{24,16},{28,12},{1,9},{5... | collective-permute-start | bytes 1572872 | tf_op jit(solution)/shard_map/ppermute | solution.py:225
  22.5 1.8 %collective-permute-start = (bf16[512,128]{1,0:T(8,128)(2,1)S(1)}, bf16[512,128]{1,0:T(8,128)(2,1)S(1)}, u32[]{:S(2)}, u32[]{:S(2)}) collective-permute-start(bf16[512,128]{1,0:T(8,128)(2,1)S(1)} %constant_dynamic-update-slice_fusion.refs_4_), channel_id=1, source_target_pairs={{0,16},{4,20},{8,24},{12,28},{1,17},{5,21},{9,25},{13,29},{2,18},{... | collective-permute-start | bytes 393224 | tf_op jit(solution)/shard_map/ppermute | solution.py:232
  25.1 3.9 %collective-permute-done.6 = bf16[1,2,128,1024]{3,2,1,0:T(8,128)(2,1)S(1)} collective-permute-done((bf16[1,2,128,1024]{3,2,1,0:T(8,128)(2,1)S(1)}, bf16[1,2,128,1024]{3,2,1,0:T(8,128)(2,1)S(1)}, u32[]{:S(2)}, u32[]{:S(2)}) %collective-permute-start.6) | collective-permute-done | bytes 524320 | tf_op jit(solution)/shard_map/ppermute | solution.py:225
  29.1 0.9 %copy-done = bf16[256,512]{1,0:T(8,128)(2,1)S(1)} copy-done((bf16[256,512]{1,0:T(8,128)(2,1)S(1)}, bf16[256,512]{1,0:T(8,128)(2,1)}, u32[]{:S(2)}) %copy-start) | copy-done | bytes 262168
  30.1 3.9 %attention.1 = bf16[256,512]{1,0:T(8,128)(2,1)S(1)} custom-call(s32[9]{0:T(128)S(1)} %pad_add_fusion.1.place_ref, bf16[256,512]{1,0:T(8,128)(2,1)S(1)} %copy-done, bf16[512,128]{1,0:T(8,128)(2,1)S(1)} %collective-permute-done.refs_0_, bf16[512,128]{1,0:T(8,128)(2,1)S(1)} %collective-permute-done.1.refs_1_, ...), custom_call_target="tpu_custom_call" | custom-call | tf_op jit(solution)/shard_map/attention/pallas_call | solution.py:59
  33.9 1.8 %collective-permute-start.7 = (bf16[1,256,512]{2,1,0:T(8,128)(2,1)S(1)}, bf16[1,256,512]{2,1,0:T(8,128)(2,1)S(1)}, u32[]{:S(2)}, u32[]{:S(2)}) collective-permute-start(bf16[1,256,512]{2,1,0:T(8,128)(2,1)S(1)} %bitcast.17), channel_id=1, source_target_pairs={{0,1},{1,0},{2,3},{3,2},{4,5},{5,4},{6,7},{7,6},{8,9},{9,8},{10,11... | collective-permute-start | bytes 786440 | tf_op jit(solution)/shard_map/ppermute | solution.py:213
  36.1 1.9 %collective-permute-start.14 = (bf16[2,2,128,1024]{3,2,1,0:T(8,128)(2,1)S(1)}, bf16[2,2,128,1024]{3,2,1,0:T(8,128)(2,1)S(1)}, u32[]{:S(2)}, u32[]{:S(2)}) collective-permute-start(bf16[2,2,128,1024]{3,2,1,0:T(8,128)(2,1)S(1)} %pad_maximum_fusion), channel_id=1, source_target_pairs={{0,16},{4,12},{8,24},{12,4},{16,0},{20,28},{24,8},{28,20},{1,17},{... | collective-permute-start | bytes 3145736 | tf_op jit(solution)/shard_map/ppermute | solution.py:225
  38.0 1.8 %collective-permute-start.10 = (bf16[1,1,128,1024]{3,2,1,0:T(8,128)(2,1)S(1)}, bf16[1,1,128,1024]{3,2,1,0:T(8,128)(2,1)S(1)}, u32[]{:S(2)}, u32[]{:S(2)}) collective-permute-start(bf16[1,1,128,1024]{3,2,1,0:T(8,128)(2,1)S(1)} %bitcast.23), channel_id=1, source_target_pairs={{0,8},{4,20},{8,0},{12,28},{16,24},{20,4},{24,16},{28,12},{1,9},{5... | collective-permute-start | bytes 786440 | tf_op jit(solution)/shard_map/ppermute | solution.py:225
  39.8 1.8 %constant_dynamic-slice_fusion.refs_4_ = bf16[512,2048]{1,0:T(8,128)(2,1)S(1)} fusion(bf16[512,8192]{1,0:T(8,128)(2,1)} %param.9, s32[]{:T(128)S(6)} %select_n.34), kind=kLoop, calls=%fused_computation.8 | loop fusion | bytes 4194308 | tf_op jit(solution)/shard_map/dynamic_slice | solution.py:270
  41.6 5.6 %collective-permute-done.10 = bf16[1,1,128,1024]{3,2,1,0:T(8,128)(2,1)S(1)} collective-permute-done((bf16[1,1,128,1024]{3,2,1,0:T(8,128)(2,1)S(1)}, bf16[1,1,128,1024]{3,2,1,0:T(8,128)(2,1)S(1)}, u32[]{:S(2)}, u32[]{:S(2)}) %collective-permute-start.10) | collective-permute-done | bytes 262176 | tf_op jit(solution)/shard_map/ppermute | solution.py:225
  47.4 2.4 %collective-permute-start.12 = (bf16[2,1,128,1024]{3,2,1,0:T(8,128)(2,1)S(1)}, bf16[2,1,128,1024]{3,2,1,0:T(8,128)(2,1)S(1)}, u32[]{:S(2)}, u32[]{:S(2)}) collective-permute-start(bf16[2,1,128,1024]{3,2,1,0:T(8,128)(2,1)S(1)} %pad_maximum_fusion.2), channel_id=1, source_target_pairs={{0,16},{4,12},{8,24},{12,4},{16,0},{20,28},{24,8},{28,20},{1,17},{... | collective-permute-start | bytes 1572872 | tf_op jit(solution)/shard_map/ppermute | solution.py:225
  49.8 1.8 %collective-permute-start.11 = (bf16[1,256,512]{2,1,0:T(8,128)(2,1)S(1)}, bf16[1,256,512]{2,1,0:T(8,128)(2,1)S(1)}, u32[]{:S(2)}, u32[]{:S(2)}) collective-permute-start(bf16[1,256,512]{2,1,0:T(8,128)(2,1)S(1)} %collective-permute-done.8.refs_1_), channel_id=1, source_target_pairs={{0,1},{1,0},{2,3},{3,2},{4,5},{5,4},{6,7},{7,6},{8,9},{9,8},{10,11... | collective-permute-start | bytes 786440 | tf_op jit(solution)/shard_map/ppermute | solution.py:213
  51.6 4.6 %collective-permute-done.11.refs_3_ = bf16[1,256,512]{2,1,0:T(8,128)(2,1)S(1)} collective-permute-done((bf16[1,256,512]{2,1,0:T(8,128)(2,1)S(1)}, bf16[1,256,512]{2,1,0:T(8,128)(2,1)S(1)}, u32[]{:S(2)}, u32[]{:S(2)}) %collective-permute-start.11) | collective-permute-done | bytes 262176 | tf_op jit(solution)/shard_map/ppermute | solution.py:213
  56.2 1.7 %collective-permute-done.12 = bf16[2,1,128,1024]{3,2,1,0:T(8,128)(2,1)S(1)} collective-permute-done((bf16[2,1,128,1024]{3,2,1,0:T(8,128)(2,1)S(1)}, bf16[2,1,128,1024]{3,2,1,0:T(8,128)(2,1)S(1)}, u32[]{:S(2)}, u32[]{:S(2)}) %collective-permute-start.12) | collective-permute-done | bytes 524320 | tf_op jit(solution)/shard_map/ppermute | solution.py:225
  58.6 1.9 %project.3 = (bf16[64,1024]{1,0:T(8,128)(2,1)S(1)}, bf16[64,1024]{1,0:T(8,128)(2,1)S(1)}, bf16[64,1024]{1,0:T(8,128)(2,1)S(1)}, bf16[64,1024]{1,0:T(8,128)(2,1)S(1)}) custom-call(s32[3]{0:T(128)S(1)} %pad_add_fusion.place_ref, bf16[1,256,512]{2,1,0:T(8,128)(2,1)S(1)} %bitcast.19, bf16[1,256,512]{2,1,0:T(8,128)(2,1)S(1)} %collective-permute-done.8.refs_1_, ...), custom_call_target="tpu_custom_call" | custom-call | flops 1073741824 | bytes 5767168 | tf_op jit(solution)/shard_map/project/pallas_call | solution.py:156
  60.5 3.5 %collective-permute-start.20 = (bf16[64,1024]{1,0:T(8,128)(2,1)S(1)}, bf16[64,1024]{1,0:T(8,128)(2,1)S(1)}, u32[]{:S(2)}, u32[]{:S(2)}) collective-permute-start(bf16[64,1024]{1,0:T(8,128)(2,1)S(1)} %get-tuple-element.54), channel_id=1, source_target_pairs={{0,3},{1,2},{2,1},{3,0},{4,7},{5,6},{6,5},{7,4},{8,11},{9,10},{10,... | collective-permute-start | bytes 393224 | tf_op jit(solution)/shard_map/ppermute | solution.py:213
  64.1 0.9 %collective-permute-start.22 = (bf16[64,1024]{1,0:T(8,128)(2,1)S(1)}, bf16[64,1024]{1,0:T(8,128)(2,1)S(1)}, u32[]{:S(2)}, u32[]{:S(2)}) collective-permute-start(bf16[64,1024]{1,0:T(8,128)(2,1)S(1)} %get-tuple-element.56), channel_id=1, source_target_pairs={{0,2},{1,3},{2,0},{3,1},{4,6},{5,7},{6,4},{7,5},{8,10},{9,11},{10,... | collective-permute-start | bytes 393224 | tf_op jit(solution)/shard_map/ppermute | solution.py:213
  65.0 1.8 %project.2 = (bf16[64,1024]{1,0:T(8,128)(2,1)S(1)}, bf16[64,1024]{1,0:T(8,128)(2,1)S(1)}, bf16[64,1024]{1,0:T(8,128)(2,1)S(1)}, bf16[64,1024]{1,0:T(8,128)(2,1)S(1)}) custom-call(s32[3]{0:T(128)S(1)} %pad_add_fusion.place_ref, bf16[1,256,512]{2,1,0:T(8,128)(2,1)S(1)} %bitcast.20, bf16[1,256,512]{2,1,0:T(8,128)(2,1)S(1)} %collective-permute-done.8.refs_1_, ...), custom_call_target="tpu_custom_call" | custom-call | flops 1073741824 | bytes 5767168 | tf_op jit(solution)/shard_map/project/pallas_call | solution.py:156
  66.8 3.5 %collective-permute-start.17 = (bf16[64,1024]{1,0:T(8,128)(2,1)S(1)}, bf16[64,1024]{1,0:T(8,128)(2,1)S(1)}, u32[]{:S(2)}, u32[]{:S(2)}) collective-permute-start(bf16[64,1024]{1,0:T(8,128)(2,1)S(1)} %get-tuple-element.50), channel_id=1, source_target_pairs={{0,3},{1,2},{2,1},{3,0},{4,7},{5,6},{6,5},{7,4},{8,11},{9,10},{10,... | collective-permute-start | bytes 393224 | tf_op jit(solution)/shard_map/ppermute | solution.py:213
  70.4 1.8 %collective-permute-start.19 = (bf16[64,1024]{1,0:T(8,128)(2,1)S(1)}, bf16[64,1024]{1,0:T(8,128)(2,1)S(1)}, u32[]{:S(2)}, u32[]{:S(2)}) collective-permute-start(bf16[64,1024]{1,0:T(8,128)(2,1)S(1)} %get-tuple-element.52), channel_id=1, source_target_pairs={{0,2},{1,3},{2,0},{3,1},{4,6},{5,7},{6,4},{7,5},{8,10},{9,11},{10,... | collective-permute-start | bytes 393224 | tf_op jit(solution)/shard_map/ppermute | solution.py:213
  72.2 7.5 %collective-permute-done.22.refs_3_ = bf16[64,1024]{1,0:T(8,128)(2,1)S(1)} collective-permute-done((bf16[64,1024]{1,0:T(8,128)(2,1)S(1)}, bf16[64,1024]{1,0:T(8,128)(2,1)S(1)}, u32[]{:S(2)}, u32[]{:S(2)}) %collective-permute-start.22) | collective-permute-done | bytes 131104 | tf_op jit(solution)/shard_map/ppermute | solution.py:213
  79.6 1.4 %assemble.2.refs_4_ = bf16[64,8192]{1,0:T(8,128)(2,1)} custom-call(s32[3]{0:T(128)S(1)} %pad_add_fusion.place_ref, bf16[64,1024]{1,0:T(8,128)(2,1)S(1)} %get-tuple-element.53.refs_0_, bf16[64,1024]{1,0:T(8,128)(2,1)S(1)} %collective-permute-done.20.refs_1_, bf16[64,1024]{1,0:T(8,128)(2,1)S(1)} %collective-permute-done.21.refs_2_, ...), custom_call_target="tpu_custom_call" | custom-call | tf_op jit(solution)/shard_map/assemble/pallas_call | solution.py:197
  81.0 5.5 %collective-permute-done.19.refs_3_ = bf16[64,1024]{1,0:T(8,128)(2,1)S(1)} collective-permute-done((bf16[64,1024]{1,0:T(8,128)(2,1)S(1)}, bf16[64,1024]{1,0:T(8,128)(2,1)S(1)}, u32[]{:S(2)}, u32[]{:S(2)}) %collective-permute-start.19) | collective-permute-done | bytes 131104 | tf_op jit(solution)/shard_map/ppermute | solution.py:213
  86.5 1.4 %assemble.3 = bf16[64,8192]{1,0:T(8,128)(2,1)} custom-call(s32[3]{0:T(128)S(1)} %pad_add_fusion.place_ref, bf16[64,1024]{1,0:T(8,128)(2,1)S(1)} %get-tuple-element.49.refs_0_, bf16[64,1024]{1,0:T(8,128)(2,1)S(1)} %collective-permute-done.17.refs_1_, bf16[64,1024]{1,0:T(8,128)(2,1)S(1)} %collective-permute-done.18.refs_2_, ...), custom_call_target="tpu_custom_call", output_to_operand_aliasing={{}: (5, {})} | custom-call | tf_op jit(solution)/shard_map/assemble/pallas_call | solution.py:197
  (31 shorter events, 3.3 us)
Async XLA Ops:
  1.2 16.6 %collective-permute-start.4 = (bf16[128,1024]{1,0:T(8,128)(2,1)S(1)}, bf16[128,1024]{1,0:T(8,128)(2,1)S(1)}, u32[]{:S(2)}, u32[]{:S(2)}) collective-permute-start(bf16[128,1024]{1,0:T(8,128)(2,1)S(1)} %get-tuple-element.59), channel_id=1, source_target_pairs={{0,3},{1,2},{2,1},{3,0},{4,7},{5,6},{6,5},{7,4},{8,11},{9,10},{10,... | collective-permute-start | bytes 786440 | tf_op jit(solution)/shard_map/ppermute | solution.py:213
  6.3 12.0 %collective-permute-start.5 = (bf16[128,1024]{1,0:T(8,128)(2,1)S(1)}, bf16[128,1024]{1,0:T(8,128)(2,1)S(1)}, u32[]{:S(2)}, u32[]{:S(2)}) collective-permute-start(bf16[128,1024]{1,0:T(8,128)(2,1)S(1)} %get-tuple-element.58), channel_id=1, source_target_pairs={{0,1},{1,0},{2,3},{3,2},{4,5},{5,4},{6,7},{7,6},{8,9},{9,8},{10,11... | collective-permute-start | bytes 786440 | tf_op jit(solution)/shard_map/ppermute | solution.py:213
  8.0 8.6 %collective-permute-start.1 = (bf16[512,128]{1,0:T(8,128)(2,1)S(1)}, bf16[512,128]{1,0:T(8,128)(2,1)S(1)}, u32[]{:S(2)}, u32[]{:S(2)}) collective-permute-start(bf16[512,128]{1,0:T(8,128)(2,1)S(1)} %constant_dynamic-update-slice_fusion.refs_4_), channel_id=1, source_target_pairs={{0,12},{4,16},{8,20},{12,24},{16,28},{1,13},{5,17},{9,21},{13,25},... | collective-permute-start | bytes 393224 | tf_op jit(solution)/shard_map/ppermute | solution.py:232
  10.5 7.3 %collective-permute-start.2 = (bf16[512,128]{1,0:T(8,128)(2,1)S(1)}, bf16[512,128]{1,0:T(8,128)(2,1)S(1)}, u32[]{:S(2)}, u32[]{:S(2)}) collective-permute-start(bf16[512,128]{1,0:T(8,128)(2,1)S(1)} %constant_dynamic-update-slice_fusion.refs_4_), channel_id=1, source_target_pairs={{0,8},{4,12},{8,16},{12,20},{16,24},{20,28},{1,9},{5,13},{9,17},{1... | collective-permute-start | bytes 393224 | tf_op jit(solution)/shard_map/ppermute | solution.py:232
  14.0 3.9 %collective-permute-start.3 = (bf16[512,128]{1,0:T(8,128)(2,1)S(1)}, bf16[512,128]{1,0:T(8,128)(2,1)S(1)}, u32[]{:S(2)}, u32[]{:S(2)}) collective-permute-start(bf16[512,128]{1,0:T(8,128)(2,1)S(1)} %constant_dynamic-update-slice_fusion.refs_4_), channel_id=1, source_target_pairs={{0,4},{4,8},{8,12},{12,16},{16,20},{20,24},{24,28},{1,5},{5,9},{9,... | collective-permute-start | bytes 393224 | tf_op jit(solution)/shard_map/ppermute | solution.py:232
  18.4 10.7 %collective-permute-start.6 = (bf16[1,2,128,1024]{3,2,1,0:T(8,128)(2,1)S(1)}, bf16[1,2,128,1024]{3,2,1,0:T(8,128)(2,1)S(1)}, u32[]{:S(2)}, u32[]{:S(2)}) collective-permute-start(bf16[1,2,128,1024]{3,2,1,0:T(8,128)(2,1)S(1)} %maximum_bitcast_fusion), channel_id=1, source_target_pairs={{0,8},{4,20},{8,0},{12,28},{16,24},{20,4},{24,16},{28,12},{1,9},{5... | collective-permute-start | bytes 1572872 | tf_op jit(solution)/shard_map/ppermute | solution.py:225
  21.9 16.1 %collective-permute-start.9 = (bf16[128,1024]{1,0:T(8,128)(2,1)S(1)}, bf16[128,1024]{1,0:T(8,128)(2,1)S(1)}, u32[]{:S(2)}, u32[]{:S(2)}) collective-permute-start(bf16[128,1024]{1,0:T(8,128)(2,1)S(1)} %get-tuple-element.38), channel_id=1, source_target_pairs={{0,2},{1,3},{2,0},{3,1},{4,6},{5,7},{6,4},{7,5},{8,10},{9,11},{10,... | collective-permute-start | bytes 786440 | tf_op jit(solution)/shard_map/ppermute | solution.py:213
  22.5 6.6 %collective-permute-start = (bf16[512,128]{1,0:T(8,128)(2,1)S(1)}, bf16[512,128]{1,0:T(8,128)(2,1)S(1)}, u32[]{:S(2)}, u32[]{:S(2)}) collective-permute-start(bf16[512,128]{1,0:T(8,128)(2,1)S(1)} %constant_dynamic-update-slice_fusion.refs_4_), channel_id=1, source_target_pairs={{0,16},{4,20},{8,24},{12,28},{1,17},{5,21},{9,25},{13,29},{2,18},{... | collective-permute-start | bytes 393224 | tf_op jit(solution)/shard_map/ppermute | solution.py:232
  29.1 1.0 %copy-start = (bf16[256,512]{1,0:T(8,128)(2,1)S(1)}, bf16[256,512]{1,0:T(8,128)(2,1)}, u32[]{:S(2)}) copy-start(bf16[256,512]{1,0:T(8,128)(2,1)} %query_hbm.1) | copy-start | bytes 786436
  33.9 13.4 %collective-permute-start.7 = (bf16[1,256,512]{2,1,0:T(8,128)(2,1)S(1)}, bf16[1,256,512]{2,1,0:T(8,128)(2,1)S(1)}, u32[]{:S(2)}, u32[]{:S(2)}) collective-permute-start(bf16[1,256,512]{2,1,0:T(8,128)(2,1)S(1)} %bitcast.17), channel_id=1, source_target_pairs={{0,1},{1,0},{2,3},{3,2},{4,5},{5,4},{6,7},{7,6},{8,9},{9,8},{10,11... | collective-permute-start | bytes 786440 | tf_op jit(solution)/shard_map/ppermute | solution.py:213
  35.8 11.6 %collective-permute-start.8 = (bf16[1,256,512]{2,1,0:T(8,128)(2,1)S(1)}, bf16[1,256,512]{2,1,0:T(8,128)(2,1)S(1)}, u32[]{:S(2)}, u32[]{:S(2)}) collective-permute-start(bf16[1,256,512]{2,1,0:T(8,128)(2,1)S(1)} %bitcast.18), channel_id=1, source_target_pairs={{0,3},{1,2},{2,1},{3,0},{4,7},{5,6},{6,5},{7,4},{8,11},{9,10},{10,... | collective-permute-start | bytes 786440 | tf_op jit(solution)/shard_map/ppermute | solution.py:213
  36.1 22.0 %collective-permute-start.14 = (bf16[2,2,128,1024]{3,2,1,0:T(8,128)(2,1)S(1)}, bf16[2,2,128,1024]{3,2,1,0:T(8,128)(2,1)S(1)}, u32[]{:S(2)}, u32[]{:S(2)}) collective-permute-start(bf16[2,2,128,1024]{3,2,1,0:T(8,128)(2,1)S(1)} %pad_maximum_fusion), channel_id=1, source_target_pairs={{0,16},{4,12},{8,24},{12,4},{16,0},{20,28},{24,8},{28,20},{1,17},{... | collective-permute-start | bytes 3145736 | tf_op jit(solution)/shard_map/ppermute | solution.py:225
  38.0 9.2 %collective-permute-start.10 = (bf16[1,1,128,1024]{3,2,1,0:T(8,128)(2,1)S(1)}, bf16[1,1,128,1024]{3,2,1,0:T(8,128)(2,1)S(1)}, u32[]{:S(2)}, u32[]{:S(2)}) collective-permute-start(bf16[1,1,128,1024]{3,2,1,0:T(8,128)(2,1)S(1)} %bitcast.23), channel_id=1, source_target_pairs={{0,8},{4,20},{8,0},{12,28},{16,24},{20,4},{24,16},{28,12},{1,9},{5... | collective-permute-start | bytes 786440 | tf_op jit(solution)/shard_map/ppermute | solution.py:225
  47.4 10.5 %collective-permute-start.12 = (bf16[2,1,128,1024]{3,2,1,0:T(8,128)(2,1)S(1)}, bf16[2,1,128,1024]{3,2,1,0:T(8,128)(2,1)S(1)}, u32[]{:S(2)}, u32[]{:S(2)}) collective-permute-start(bf16[2,1,128,1024]{3,2,1,0:T(8,128)(2,1)S(1)} %pad_maximum_fusion.2), channel_id=1, source_target_pairs={{0,16},{4,12},{8,24},{12,4},{16,0},{20,28},{24,8},{28,20},{1,17},{... | collective-permute-start | bytes 1572872 | tf_op jit(solution)/shard_map/ppermute | solution.py:225
  49.8 6.4 %collective-permute-start.11 = (bf16[1,256,512]{2,1,0:T(8,128)(2,1)S(1)}, bf16[1,256,512]{2,1,0:T(8,128)(2,1)S(1)}, u32[]{:S(2)}, u32[]{:S(2)}) collective-permute-start(bf16[1,256,512]{2,1,0:T(8,128)(2,1)S(1)} %collective-permute-done.8.refs_1_), channel_id=1, source_target_pairs={{0,1},{1,0},{2,3},{3,2},{4,5},{5,4},{6,7},{7,6},{8,9},{9,8},{10,11... | collective-permute-start | bytes 786440 | tf_op jit(solution)/shard_map/ppermute | solution.py:213
  51.6 12.5 %collective-permute-start.13 = (bf16[512,1024]{1,0:T(8,128)(2,1)S(1)}, bf16[512,1024]{1,0:T(8,128)(2,1)S(1)}, u32[]{:S(2)}, u32[]{:S(2)}) collective-permute-start(bf16[512,1024]{1,0:T(8,128)(2,1)S(1)} %bitcast.13), channel_id=1, source_target_pairs={{0,4},{4,0},{8,12},{12,8},{16,20},{20,16},{24,28},{28,24},{1,5},{5... | collective-permute-start | bytes 3145736 | tf_op jit(solution)/shard_map/ppermute | solution.py:218
  58.0 7.0 %collective-permute-start.16 = (bf16[512,1024]{1,0:T(8,128)(2,1)S(1)}, bf16[512,1024]{1,0:T(8,128)(2,1)S(1)}, u32[]{:S(2)}, u32[]{:S(2)}) collective-permute-start(bf16[512,1024]{1,0:T(8,128)(2,1)S(1)} %bitcast.15), channel_id=1, source_target_pairs={{0,4},{4,0},{8,12},{12,8},{16,20},{20,16},{24,28},{28,24},{1,5},{5... | collective-permute-start | bytes 3145736 | tf_op jit(solution)/shard_map/ppermute | solution.py:218
  58.1 6.9 %collective-permute-start.15 = (bf16[512,1024]{1,0:T(8,128)(2,1)S(1)}, bf16[512,1024]{1,0:T(8,128)(2,1)S(1)}, u32[]{:S(2)}, u32[]{:S(2)}) collective-permute-start(bf16[512,1024]{1,0:T(8,128)(2,1)S(1)} %bitcast.21), channel_id=1, source_target_pairs={{0,4},{4,0},{8,12},{12,8},{16,20},{20,16},{24,28},{28,24},{1,5},{5... | collective-permute-start | bytes 3145736 | tf_op jit(solution)/shard_map/ppermute | solution.py:218
  60.5 9.9 %collective-permute-start.20 = (bf16[64,1024]{1,0:T(8,128)(2,1)S(1)}, bf16[64,1024]{1,0:T(8,128)(2,1)S(1)}, u32[]{:S(2)}, u32[]{:S(2)}) collective-permute-start(bf16[64,1024]{1,0:T(8,128)(2,1)S(1)} %get-tuple-element.54), channel_id=1, source_target_pairs={{0,3},{1,2},{2,1},{3,0},{4,7},{5,6},{6,5},{7,4},{8,11},{9,10},{10,... | collective-permute-start | bytes 393224 | tf_op jit(solution)/shard_map/ppermute | solution.py:213
  64.0 8.1 %collective-permute-start.21 = (bf16[64,1024]{1,0:T(8,128)(2,1)S(1)}, bf16[64,1024]{1,0:T(8,128)(2,1)S(1)}, u32[]{:S(2)}, u32[]{:S(2)}) collective-permute-start(bf16[64,1024]{1,0:T(8,128)(2,1)S(1)} %get-tuple-element.55), channel_id=1, source_target_pairs={{0,1},{1,0},{2,3},{3,2},{4,5},{5,4},{6,7},{7,6},{8,9},{9,8},{10,11... | collective-permute-start | bytes 393224 | tf_op jit(solution)/shard_map/ppermute | solution.py:213
  64.1 15.6 %collective-permute-start.22 = (bf16[64,1024]{1,0:T(8,128)(2,1)S(1)}, bf16[64,1024]{1,0:T(8,128)(2,1)S(1)}, u32[]{:S(2)}, u32[]{:S(2)}) collective-permute-start(bf16[64,1024]{1,0:T(8,128)(2,1)S(1)} %get-tuple-element.56), channel_id=1, source_target_pairs={{0,2},{1,3},{2,0},{3,1},{4,6},{5,7},{6,4},{7,5},{8,10},{9,11},{10,... | collective-permute-start | bytes 393224 | tf_op jit(solution)/shard_map/ppermute | solution.py:213
  66.8 14.2 %collective-permute-start.17 = (bf16[64,1024]{1,0:T(8,128)(2,1)S(1)}, bf16[64,1024]{1,0:T(8,128)(2,1)S(1)}, u32[]{:S(2)}, u32[]{:S(2)}) collective-permute-start(bf16[64,1024]{1,0:T(8,128)(2,1)S(1)} %get-tuple-element.50), channel_id=1, source_target_pairs={{0,3},{1,2},{2,1},{3,0},{4,7},{5,6},{6,5},{7,4},{8,11},{9,10},{10,... | collective-permute-start | bytes 393224 | tf_op jit(solution)/shard_map/ppermute | solution.py:213
  70.4 10.7 %collective-permute-start.18 = (bf16[64,1024]{1,0:T(8,128)(2,1)S(1)}, bf16[64,1024]{1,0:T(8,128)(2,1)S(1)}, u32[]{:S(2)}, u32[]{:S(2)}) collective-permute-start(bf16[64,1024]{1,0:T(8,128)(2,1)S(1)} %get-tuple-element.51), channel_id=1, source_target_pairs={{0,1},{1,0},{2,3},{3,2},{4,5},{5,4},{6,7},{7,6},{8,9},{9,8},{10,11... | collective-permute-start | bytes 393224 | tf_op jit(solution)/shard_map/ppermute | solution.py:213
  70.4 16.1 %collective-permute-start.19 = (bf16[64,1024]{1,0:T(8,128)(2,1)S(1)}, bf16[64,1024]{1,0:T(8,128)(2,1)S(1)}, u32[]{:S(2)}, u32[]{:S(2)}) collective-permute-start(bf16[64,1024]{1,0:T(8,128)(2,1)S(1)} %get-tuple-element.52), channel_id=1, source_target_pairs={{0,2},{1,3},{2,0},{3,1},{4,6},{5,7},{6,4},{7,5},{8,10},{9,11},{10,... | collective-permute-start | bytes 393224 | tf_op jit(solution)/shard_map/ppermute | solution.py:213

commit v3 on v2

--- a/solution.py
+++ b/solution.py
@@ -255,23 +255,25 @@
         column = head_index * heads // GROUP * HD
         own = [lax.dynamic_slice_in_dim(part, column, HD, 1) for part in own]
     own = jnp.concatenate(own)
-    pieces = [later(own, d) for d in range(SPAN, 0, -1)] + [own]
+    late = tie(own, fetched[1])
+    pieces = [later(own if d < SPAN else late, d) for d in range(SPAN, 0, -1)] + [own]
     for x in others:
         if x not in fetched:
-            fetched[x] = paired(tie(share_of(x), (fetched[planes - 1], pieces[1:-1])), x)
+            fetched[x] = paired(tie(share_of(x), (fetched[planes - 1], pieces[2:-1])), x)
     groups = [[x for x in others if x in (1, planes - 1)]]
     groups.append([x for x in others if x not in groups[0]])
     plane_stages, chip_stages = planes.bit_length() - 1, chips.bit_length() - 1
-    first = jnp.stack(tie([fetched[x] for x in groups[0]], pieces[1:-1]))[None]
+    first = jnp.stack(tie([fetched[x] for x in groups[0]], pieces[2:-1]))[None]
     first = jnp.concatenate([first, crossed(first, 0)])
-    pieces, first = lax.optimization_barrier((pieces, first))
     rest = crossed(first, 1)
     attended = [attention(queries, pieces, lengths, ctx_index * rows)[None]]
+    middle = [fetched[x] for x in groups[1]]
+    attended, middle = lax.optimization_barrier((attended, middle))
     own_weight = lax.dynamic_slice_in_dim(
         tie(out_weight, attended), head_index * CORES * cols, CORES * cols, 1
     )
 
-    second = jnp.stack(tie([fetched[x] for x in groups[1]], (attended, first)))[None]
+    second = jnp.stack(tie(middle, first))[None]
     early, latest = [], attended
     for stage in range(max(plane_stages, chip_stages)):
         ahead, new, more = [], [], []

time: 88.3 us -> 90.7 us (1.027)
  waiting for transfers between devices: 30.6 us -> 35.7 us
  starting transfers between devices: 40.1 us -> 37.6 us
    ppermute x12, waiting for transfers between devices: 18.1 us -> 29.3 us  [paired(): return lax.ppermute(shard, 'head', [(i, i ^ x) for i in range(length)])]
    ppermute x4, waiting for transfers between devices: 11.3 us -> 1.99 us  [crossed(): lax.ppermute(shard, 'ctx', [(i, i ^ CORES << bit[i % CORES]) for i in ran...]
    ppermute x4, waiting for transfers between devices: 1.23 us -> 4.39 us  [later(): return lax.ppermute(shard, 'ctx', [(i, i + by) for i in range(length - by)])]
    ppermute x4, starting transfers between devices: 9.59 us -> 6.46 us  [crossed(): lax.ppermute(shard, 'ctx', [(i, i ^ CORES << bit[i % CORES]) for i in ran...]
    ppermute x12, starting transfers between devices: 19.5 us -> 20.5 us  [paired(): return lax.ppermute(shard, 'head', [(i, i ^ x) for i in range(length)])]
  transfers between devices with their start and end apart: 23 -> 23, of which waited for: 9 -> 12; matrix products, arithmetic and copies ran while one was open for 5% -> 5% of each run, Pallas kernels for 10% -> 10%
where the time goes in v3:
time: 90.7 us; the launch traced here: 90.4 us
  starting transfers between devices  37.6 us (41%)
  waiting for transfers between devices  35.7 us (39%)
  Pallas kernels  10.3 us (11%)
  local copies, waits for them, and re-layouts  5.63 us (6%)
  other arithmetic  1.11 us (1%)
    ppermute x12, waiting for transfers between devices, paired(): return lax.ppermute(shard, 'head', [(i, i ^ x) for i in range(length)])  29.3 us
    ppermute x12, starting transfers between devices, paired(): return lax.ppermute(shard, 'head', [(i, i ^ x) for i in range(length)])  20.5 us
    ppermute x4, starting transfers between devices, later(): return lax.ppermute(shard, 'ctx', [(i, i + by) for i in range(length - by)])  10 us
    ppermute x4, starting transfers between devices, crossed(): lax.ppermute(shard, 'ctx', [(i, i ^ CORES << bit[i % CORES]) for i in ran...  6.46 us
    ppermute x4, waiting for transfers between devices, later(): return lax.ppermute(shard, 'ctx', [(i, i + by) for i in range(length - by)])  4.39 us
    pallas_call x1, Pallas kernels, attention(): pl.pallas_call(attention_kernel, out_shape=jax.ShapeDtypeStruct(queries.s...  3.85 us
    pallas_call x2, Pallas kernels, project(): pl.pallas_call(kernel, out_shape=[jax.ShapeDtypeStruct((rows_out, cols),...  3.69 us
    pallas_call x2, Pallas kernels, assemble(): pl.pallas_call(kernel, out_shape=jax.ShapeDtypeStruct((rows, width), jnp....  2.73 us
  transfers between devices with their start and end apart: 23, of which 12 were waited for; matrix products, arithmetic and copies ran while one was open for 5% of the time, Pallas kernels for 10%

profile of v3, /device:TPU:0, one launch (start us, length us, event | category | flops | bytes accessed | tf_op | source)
XLA Modules:
  0.0 90.4 jit_solution(14045015151751118082)
XLA Ops:
  1.2 3.1 %collective-permute-start = (bf16[128,1024]{1,0:T(8,128)(2,1)S(1)}, bf16[128,1024]{1,0:T(8,128)(2,1)S(1)}, u32[]{:S(2)}, u32[]{:S(2)}) collective-permute-start(bf16[128,1024]{1,0:T(8,128)(2,1)S(1)} %get-tuple-element.53), channel_id=1, source_target_pairs={{0,1},{1,0},{2,3},{3,2},{4,5},{5,4},{6,7},{7,6},{8,9},{9,8},{10,11... | collective-permute-start | bytes 786440 | tf_op jit(solution)/shard_map/ppermute | solution.py:213
  4.3 2.5 %collective-permute-start.5 = (bf16[128,1024]{1,0:T(8,128)(2,1)S(1)}, bf16[128,1024]{1,0:T(8,128)(2,1)S(1)}, u32[]{:S(2)}, u32[]{:S(2)}) collective-permute-start(bf16[128,1024]{1,0:T(8,128)(2,1)S(1)} %get-tuple-element.51), channel_id=1, source_target_pairs={{0,3},{1,2},{2,1},{3,0},{4,7},{5,6},{6,5},{7,4},{8,11},{9,10},{10,... | collective-permute-start | bytes 786440 | tf_op jit(solution)/shard_map/ppermute | solution.py:213
  8.4 3.4 %collective-permute-start.3 = (bf16[512,128]{1,0:T(8,128)(2,1)S(1)}, bf16[512,128]{1,0:T(8,128)(2,1)S(1)}, u32[]{:S(2)}, u32[]{:S(2)}) collective-permute-start(bf16[512,128]{1,0:T(8,128)(2,1)S(1)} %constant_dynamic-update-slice_fusion.refs_4_), channel_id=1, source_target_pairs={{0,8},{4,12},{8,16},{12,20},{16,24},{20,28},{1,9},{5,13},{9,17},{1... | collective-permute-start | bytes 393224 | tf_op jit(solution)/shard_map/ppermute | solution.py:232
  11.8 1.3 %collective-permute-start.4 = (bf16[512,128]{1,0:T(8,128)(2,1)S(1)}, bf16[512,128]{1,0:T(8,128)(2,1)S(1)}, u32[]{:S(2)}, u32[]{:S(2)}) collective-permute-start(bf16[512,128]{1,0:T(8,128)(2,1)S(1)} %constant_dynamic-update-slice_fusion.refs_4_), channel_id=1, source_target_pairs={{0,4},{4,8},{8,12},{12,16},{16,20},{20,24},{24,28},{1,5},{5,9},{9,... | collective-permute-start | bytes 393224 | tf_op jit(solution)/shard_map/ppermute | solution.py:232
  13.1 1.2 %collective-permute-done.3.refs_2_ = bf16[512,128]{1,0:T(8,128)(2,1)S(1)} collective-permute-done((bf16[512,128]{1,0:T(8,128)(2,1)S(1)}, bf16[512,128]{1,0:T(8,128)(2,1)S(1)}, u32[]{:S(2)}, u32[]{:S(2)}) %collective-permute-start.3) | collective-permute-done | bytes 131104 | tf_op jit(solution)/shard_map/ppermute | solution.py:232
  14.3 4.1 %collective-permute-done.5 = bf16[128,1024]{1,0:T(8,128)(2,1)S(1)} collective-permute-done((bf16[128,1024]{1,0:T(8,128)(2,1)S(1)}, bf16[128,1024]{1,0:T(8,128)(2,1)S(1)}, u32[]{:S(2)}, u32[]{:S(2)}) %collective-permute-start.5) | collective-permute-done | bytes 262176 | tf_op jit(solution)/shard_map/ppermute | solution.py:213
  18.5 1.6 %collective-permute-start.9 = (bf16[1,2,128,1024]{3,2,1,0:T(8,128)(2,1)S(1)}, bf16[1,2,128,1024]{3,2,1,0:T(8,128)(2,1)S(1)}, u32[]{:S(2)}, u32[]{:S(2)}) collective-permute-start(bf16[1,2,128,1024]{3,2,1,0:T(8,128)(2,1)S(1)} %maximum_bitcast_fusion), channel_id=1, source_target_pairs={{0,8},{4,20},{8,0},{12,28},{16,24},{20,4},{24,16},{28,12},{1,9},{5... | collective-permute-start | bytes 1572872 | tf_op jit(solution)/shard_map/ppermute | solution.py:225
  20.1 1.8 %collective-permute-start.6 = (bf16[128,1024]{1,0:T(8,128)(2,1)S(1)}, bf16[128,1024]{1,0:T(8,128)(2,1)S(1)}, u32[]{:S(2)}, u32[]{:S(2)}) collective-permute-start(bf16[128,1024]{1,0:T(8,128)(2,1)S(1)} %get-tuple-element.29), channel_id=1, source_target_pairs={{0,2},{1,3},{2,0},{3,1},{4,6},{5,7},{6,4},{7,5},{8,10},{9,11},{10,... | collective-permute-start | bytes 786440 | tf_op jit(solution)/shard_map/ppermute | solution.py:213
  21.8 1.3 %collective-permute-start.2 = (bf16[512,128]{1,0:T(8,128)(2,1)S(1)}, bf16[512,128]{1,0:T(8,128)(2,1)S(1)}, u32[]{:S(2)}, u32[]{:S(2)}) collective-permute-start(bf16[512,128]{1,0:T(8,128)(2,1)S(1)} %constant_dynamic-update-slice_fusion.refs_4_), channel_id=1, source_target_pairs={{0,12},{4,16},{8,20},{12,24},{16,28},{1,13},{5,17},{9,21},{13,25},... | collective-permute-start | bytes 393224 | tf_op jit(solution)/shard_map/ppermute | solution.py:232
  23.1 4.1 %collective-permute-start.1 = (bf16[512,128]{1,0:T(8,128)(2,1)S(1)}, bf16[512,128]{1,0:T(8,128)(2,1)S(1)}, u32[]{:S(2)}, u32[]{:S(2)}) collective-permute-start(bf16[512,128]{1,0:T(8,128)(2,1)S(1)} %constant_dynamic-update-slice_fusion.refs_4_), channel_id=1, source_target_pairs={{0,16},{4,20},{8,24},{12,28},{1,17},{5,21},{9,25},{13,29},{2,18},{... | collective-permute-start | bytes 393224 | tf_op jit(solution)/shard_map/ppermute | solution.py:232
  28.2 2.9 %collective-permute-done.1.refs_0_ = bf16[512,128]{1,0:T(8,128)(2,1)S(1)} collective-permute-done((bf16[512,128]{1,0:T(8,128)(2,1)S(1)}, bf16[512,128]{1,0:T(8,128)(2,1)S(1)}, u32[]{:S(2)}, u32[]{:S(2)}) %collective-permute-start.1) | collective-permute-done | bytes 131104 | tf_op jit(solution)/shard_map/ppermute | solution.py:232
  32.1 3.9 %attention.1 = bf16[256,512]{1,0:T(8,128)(2,1)S(1)} custom-call(s32[9]{0:T(128)S(1)} %pad_add_fusion.1.place_ref, bf16[256,512]{1,0:T(8,128)(2,1)S(1)} %copy-done, bf16[512,128]{1,0:T(8,128)(2,1)S(1)} %collective-permute-done.1.refs_0_, bf16[512,128]{1,0:T(8,128)(2,1)S(1)} %collective-permute-done.2.refs_1_, ...), custom_call_target="tpu_custom_call" | custom-call | tf_op jit(solution)/shard_map/attention/pallas_call | solution.py:59
  36.6 2.4 %collective-permute-start.8 = (bf16[1,256,512]{2,1,0:T(8,128)(2,1)S(1)}, bf16[1,256,512]{2,1,0:T(8,128)(2,1)S(1)}, u32[]{:S(2)}, u32[]{:S(2)}) collective-permute-start(bf16[1,256,512]{2,1,0:T(8,128)(2,1)S(1)} %bitcast.18), channel_id=1, source_target_pairs={{0,3},{1,2},{2,1},{3,0},{4,7},{5,6},{6,5},{7,4},{8,11},{9,10},{10,... | collective-permute-start | bytes 786440 | tf_op jit(solution)/shard_map/ppermute | solution.py:213
  39.0 2.5 %collective-permute-start.14 = (bf16[2,2,128,1024]{3,2,1,0:T(8,128)(2,1)S(1)}, bf16[2,2,128,1024]{3,2,1,0:T(8,128)(2,1)S(1)}, u32[]{:S(2)}, u32[]{:S(2)}) collective-permute-start(bf16[2,2,128,1024]{3,2,1,0:T(8,128)(2,1)S(1)} %pad_maximum_fusion), channel_id=1, source_target_pairs={{0,16},{4,12},{8,24},{12,4},{16,0},{20,28},{24,8},{28,20},{1,17},{... | collective-permute-start | bytes 3145736 | tf_op jit(solution)/shard_map/ppermute | solution.py:225
  41.6 1.8 %constant_dynamic-slice_fusion.refs_4_ = bf16[512,2048]{1,0:T(8,128)(2,1)S(1)} fusion(bf16[512,8192]{1,0:T(8,128)(2,1)} %param.9, s32[]{:T(128)S(6)} %select_n.34), kind=kLoop, calls=%fused_computation.8 | loop fusion | bytes 4194308 | tf_op jit(solution)/shard_map/dynamic_slice | solution.py:272
  43.4 2.1 %collective-permute-done.7.refs_2_ = bf16[1,256,512]{2,1,0:T(8,128)(2,1)S(1)} collective-permute-done((bf16[1,256,512]{2,1,0:T(8,128)(2,1)S(1)}, bf16[1,256,512]{2,1,0:T(8,128)(2,1)S(1)}, u32[]{:S(2)}, u32[]{:S(2)}) %collective-permute-start.7) | collective-permute-done | bytes 262176 | tf_op jit(solution)/shard_map/ppermute | solution.py:213
  45.5 5.1 %collective-permute-done.8.refs_1_ = bf16[1,256,512]{2,1,0:T(8,128)(2,1)S(1)} collective-permute-done((bf16[1,256,512]{2,1,0:T(8,128)(2,1)S(1)}, bf16[1,256,512]{2,1,0:T(8,128)(2,1)S(1)}, u32[]{:S(2)}, u32[]{:S(2)}) %collective-permute-start.8) | collective-permute-done | bytes 262176 | tf_op jit(solution)/shard_map/ppermute | solution.py:213
  50.9 2.4 %collective-permute-start.12 = (bf16[2,1,128,1024]{3,2,1,0:T(8,128)(2,1)S(1)}, bf16[2,1,128,1024]{3,2,1,0:T(8,128)(2,1)S(1)}, u32[]{:S(2)}, u32[]{:S(2)}) collective-permute-start(bf16[2,1,128,1024]{3,2,1,0:T(8,128)(2,1)S(1)} %pad_maximum_fusion.2), channel_id=1, source_target_pairs={{0,16},{4,12},{8,24},{12,4},{16,0},{20,28},{24,8},{28,20},{1,17},{... | collective-permute-start | bytes 1572872 | tf_op jit(solution)/shard_map/ppermute | solution.py:225
  53.2 1.3 %collective-permute-start.11 = (bf16[1,256,512]{2,1,0:T(8,128)(2,1)S(1)}, bf16[1,256,512]{2,1,0:T(8,128)(2,1)S(1)}, u32[]{:S(2)}, u32[]{:S(2)}) collective-permute-start(bf16[1,256,512]{2,1,0:T(8,128)(2,1)S(1)} %collective-permute-done.8.refs_1_), channel_id=1, source_target_pairs={{0,1},{1,0},{2,3},{3,2},{4,5},{5,4},{6,7},{7,6},{8,9},{9,8},{10,11... | collective-permute-start | bytes 786440 | tf_op jit(solution)/shard_map/ppermute | solution.py:213
  54.6 5.0 %collective-permute-done.11.refs_3_ = bf16[1,256,512]{2,1,0:T(8,128)(2,1)S(1)} collective-permute-done((bf16[1,256,512]{2,1,0:T(8,128)(2,1)S(1)}, bf16[1,256,512]{2,1,0:T(8,128)(2,1)S(1)}, u32[]{:S(2)}, u32[]{:S(2)}) %collective-permute-start.11) | collective-permute-done | bytes 262176 | tf_op jit(solution)/shard_map/ppermute | solution.py:213
  59.6 1.8 %collective-permute-done.12 = bf16[2,1,128,1024]{3,2,1,0:T(8,128)(2,1)S(1)} collective-permute-done((bf16[2,1,128,1024]{3,2,1,0:T(8,128)(2,1)S(1)}, bf16[2,1,128,1024]{3,2,1,0:T(8,128)(2,1)S(1)}, u32[]{:S(2)}, u32[]{:S(2)}) %collective-permute-start.12) | collective-permute-done | bytes 524320 | tf_op jit(solution)/shard_map/ppermute | solution.py:225
  62.2 1.8 %project.3 = (bf16[64,1024]{1,0:T(8,128)(2,1)S(1)}, bf16[64,1024]{1,0:T(8,128)(2,1)S(1)}, bf16[64,1024]{1,0:T(8,128)(2,1)S(1)}, bf16[64,1024]{1,0:T(8,128)(2,1)S(1)}) custom-call(s32[3]{0:T(128)S(1)} %pad_add_fusion.place_ref, bf16[1,256,512]{2,1,0:T(8,128)(2,1)S(1)} %bitcast.19, bf16[1,256,512]{2,1,0:T(8,128)(2,1)S(1)} %collective-permute-done.8.refs_1_, ...), custom_call_target="tpu_custom_call" | custom-call | flops 1073741824 | bytes 5767168 | tf_op jit(solution)/shard_map/project/pallas_call | solution.py:156
  64.0 1.9 %collective-permute-start.20 = (bf16[64,1024]{1,0:T(8,128)(2,1)S(1)}, bf16[64,1024]{1,0:T(8,128)(2,1)S(1)}, u32[]{:S(2)}, u32[]{:S(2)}) collective-permute-start(bf16[64,1024]{1,0:T(8,128)(2,1)S(1)} %get-tuple-element.48), channel_id=1, source_target_pairs={{0,3},{1,2},{2,1},{3,0},{4,7},{5,6},{6,5},{7,4},{8,11},{9,10},{10,... | collective-permute-start | bytes 393224 | tf_op jit(solution)/shard_map/ppermute | solution.py:213
  65.9 2.5 %collective-permute-start.22 = (bf16[64,1024]{1,0:T(8,128)(2,1)S(1)}, bf16[64,1024]{1,0:T(8,128)(2,1)S(1)}, u32[]{:S(2)}, u32[]{:S(2)}) collective-permute-start(bf16[64,1024]{1,0:T(8,128)(2,1)S(1)} %get-tuple-element.50), channel_id=1, source_target_pairs={{0,2},{1,3},{2,0},{3,1},{4,6},{5,7},{6,4},{7,5},{8,10},{9,11},{10,... | collective-permute-start | bytes 393224 | tf_op jit(solution)/shard_map/ppermute | solution.py:213
  68.5 1.8 %project.2 = (bf16[64,1024]{1,0:T(8,128)(2,1)S(1)}, bf16[64,1024]{1,0:T(8,128)(2,1)S(1)}, bf16[64,1024]{1,0:T(8,128)(2,1)S(1)}, bf16[64,1024]{1,0:T(8,128)(2,1)S(1)}) custom-call(s32[3]{0:T(128)S(1)} %pad_add_fusion.place_ref, bf16[1,256,512]{2,1,0:T(8,128)(2,1)S(1)} %bitcast.20, bf16[1,256,512]{2,1,0:T(8,128)(2,1)S(1)} %collective-permute-done.8.refs_1_, ...), custom_call_target="tpu_custom_call" | custom-call | flops 1073741824 | bytes 5767168 | tf_op jit(solution)/shard_map/project/pallas_call | solution.py:156
  70.3 1.9 %collective-permute-start.17 = (bf16[64,1024]{1,0:T(8,128)(2,1)S(1)}, bf16[64,1024]{1,0:T(8,128)(2,1)S(1)}, u32[]{:S(2)}, u32[]{:S(2)}) collective-permute-start(bf16[64,1024]{1,0:T(8,128)(2,1)S(1)} %get-tuple-element.44), channel_id=1, source_target_pairs={{0,3},{1,2},{2,1},{3,0},{4,7},{5,6},{6,5},{7,4},{8,11},{9,10},{10,... | collective-permute-start | bytes 393224 | tf_op jit(solution)/shard_map/ppermute | solution.py:213
  72.3 2.5 %collective-permute-start.19 = (bf16[64,1024]{1,0:T(8,128)(2,1)S(1)}, bf16[64,1024]{1,0:T(8,128)(2,1)S(1)}, u32[]{:S(2)}, u32[]{:S(2)}) collective-permute-start(bf16[64,1024]{1,0:T(8,128)(2,1)S(1)} %get-tuple-element.46), channel_id=1, source_target_pairs={{0,2},{1,3},{2,0},{3,1},{4,6},{5,7},{6,4},{7,5},{8,10},{9,11},{10,... | collective-permute-start | bytes 393224 | tf_op jit(solution)/shard_map/ppermute | solution.py:213
  74.8 2.0 %collective-permute-done.21.refs_2_ = bf16[64,1024]{1,0:T(8,128)(2,1)S(1)} collective-permute-done((bf16[64,1024]{1,0:T(8,128)(2,1)S(1)}, bf16[64,1024]{1,0:T(8,128)(2,1)S(1)}, u32[]{:S(2)}, u32[]{:S(2)}) %collective-permute-start.21) | collective-permute-done | bytes 131104 | tf_op jit(solution)/shard_map/ppermute | solution.py:213
  76.8 4.4 %collective-permute-done.22.refs_3_ = bf16[64,1024]{1,0:T(8,128)(2,1)S(1)} collective-permute-done((bf16[64,1024]{1,0:T(8,128)(2,1)S(1)}, bf16[64,1024]{1,0:T(8,128)(2,1)S(1)}, u32[]{:S(2)}, u32[]{:S(2)}) %collective-permute-start.22) | collective-permute-done | bytes 131104 | tf_op jit(solution)/shard_map/ppermute | solution.py:213
  81.2 1.4 %assemble.2.refs_4_ = bf16[64,8192]{1,0:T(8,128)(2,1)} custom-call(s32[3]{0:T(128)S(1)} %pad_add_fusion.place_ref, bf16[64,1024]{1,0:T(8,128)(2,1)S(1)} %get-tuple-element.47.refs_0_, bf16[64,1024]{1,0:T(8,128)(2,1)S(1)} %collective-permute-done.20.refs_1_, bf16[64,1024]{1,0:T(8,128)(2,1)S(1)} %collective-permute-done.21.refs_2_, ...), custom_call_target="tpu_custom_call" | custom-call | tf_op jit(solution)/shard_map/assemble/pallas_call | solution.py:197
  82.6 6.4 %collective-permute-done.19.refs_3_ = bf16[64,1024]{1,0:T(8,128)(2,1)S(1)} collective-permute-done((bf16[64,1024]{1,0:T(8,128)(2,1)S(1)}, bf16[64,1024]{1,0:T(8,128)(2,1)S(1)}, u32[]{:S(2)}, u32[]{:S(2)}) %collective-permute-start.19) | collective-permute-done | bytes 131104 | tf_op jit(solution)/shard_map/ppermute | solution.py:213
  89.0 1.4 %assemble.3 = bf16[64,8192]{1,0:T(8,128)(2,1)} custom-call(s32[3]{0:T(128)S(1)} %pad_add_fusion.place_ref, bf16[64,1024]{1,0:T(8,128)(2,1)S(1)} %get-tuple-element.43.refs_0_, bf16[64,1024]{1,0:T(8,128)(2,1)S(1)} %collective-permute-done.17.refs_1_, bf16[64,1024]{1,0:T(8,128)(2,1)S(1)} %collective-permute-done.18.refs_2_, ...), custom_call_target="tpu_custom_call", output_to_operand_aliasing={{}: (5, {})} | custom-call | tf_op jit(solution)/shard_map/assemble/pallas_call | solution.py:197
  (31 shorter events, 6.6 us)
Async XLA Ops:
  1.2 13.2 %collective-permute-start = (bf16[128,1024]{1,0:T(8,128)(2,1)S(1)}, bf16[128,1024]{1,0:T(8,128)(2,1)S(1)}, u32[]{:S(2)}, u32[]{:S(2)}) collective-permute-start(bf16[128,1024]{1,0:T(8,128)(2,1)S(1)} %get-tuple-element.53), channel_id=1, source_target_pairs={{0,1},{1,0},{2,3},{3,2},{4,5},{5,4},{6,7},{7,6},{8,9},{9,8},{10,11... | collective-permute-start | bytes 786440 | tf_op jit(solution)/shard_map/ppermute | solution.py:213
  4.3 14.2 %collective-permute-start.5 = (bf16[128,1024]{1,0:T(8,128)(2,1)S(1)}, bf16[128,1024]{1,0:T(8,128)(2,1)S(1)}, u32[]{:S(2)}, u32[]{:S(2)}) collective-permute-start(bf16[128,1024]{1,0:T(8,128)(2,1)S(1)} %get-tuple-element.51), channel_id=1, source_target_pairs={{0,3},{1,2},{2,1},{3,0},{4,7},{5,6},{6,5},{7,4},{8,11},{9,10},{10,... | collective-permute-start | bytes 786440 | tf_op jit(solution)/shard_map/ppermute | solution.py:213
  8.4 5.9 %collective-permute-start.3 = (bf16[512,128]{1,0:T(8,128)(2,1)S(1)}, bf16[512,128]{1,0:T(8,128)(2,1)S(1)}, u32[]{:S(2)}, u32[]{:S(2)}) collective-permute-start(bf16[512,128]{1,0:T(8,128)(2,1)S(1)} %constant_dynamic-update-slice_fusion.refs_4_), channel_id=1, source_target_pairs={{0,8},{4,12},{8,16},{12,20},{16,24},{20,28},{1,9},{5,13},{9,17},{1... | collective-permute-start | bytes 393224 | tf_op jit(solution)/shard_map/ppermute | solution.py:232
  11.8 2.5 %collective-permute-start.4 = (bf16[512,128]{1,0:T(8,128)(2,1)S(1)}, bf16[512,128]{1,0:T(8,128)(2,1)S(1)}, u32[]{:S(2)}, u32[]{:S(2)}) collective-permute-start(bf16[512,128]{1,0:T(8,128)(2,1)S(1)} %constant_dynamic-update-slice_fusion.refs_4_), channel_id=1, source_target_pairs={{0,4},{4,8},{8,12},{12,16},{16,20},{20,24},{24,28},{1,5},{5,9},{9,... | collective-permute-start | bytes 393224 | tf_op jit(solution)/shard_map/ppermute | solution.py:232
  18.5 20.4 %collective-permute-start.9 = (bf16[1,2,128,1024]{3,2,1,0:T(8,128)(2,1)S(1)}, bf16[1,2,128,1024]{3,2,1,0:T(8,128)(2,1)S(1)}, u32[]{:S(2)}, u32[]{:S(2)}) collective-permute-start(bf16[1,2,128,1024]{3,2,1,0:T(8,128)(2,1)S(1)} %maximum_bitcast_fusion), channel_id=1, source_target_pairs={{0,8},{4,20},{8,0},{12,28},{16,24},{20,4},{24,16},{28,12},{1,9},{5... | collective-permute-start | bytes 1572872 | tf_op jit(solution)/shard_map/ppermute | solution.py:225
  20.1 15.9 %collective-permute-start.6 = (bf16[128,1024]{1,0:T(8,128)(2,1)S(1)}, bf16[128,1024]{1,0:T(8,128)(2,1)S(1)}, u32[]{:S(2)}, u32[]{:S(2)}) collective-permute-start(bf16[128,1024]{1,0:T(8,128)(2,1)S(1)} %get-tuple-element.29), channel_id=1, source_target_pairs={{0,2},{1,3},{2,0},{3,1},{4,6},{5,7},{6,4},{7,5},{8,10},{9,11},{10,... | collective-permute-start | bytes 786440 | tf_op jit(solution)/shard_map/ppermute | solution.py:213
  21.8 6.3 %collective-permute-start.2 = (bf16[512,128]{1,0:T(8,128)(2,1)S(1)}, bf16[512,128]{1,0:T(8,128)(2,1)S(1)}, u32[]{:S(2)}, u32[]{:S(2)}) collective-permute-start(bf16[512,128]{1,0:T(8,128)(2,1)S(1)} %constant_dynamic-update-slice_fusion.refs_4_), channel_id=1, source_target_pairs={{0,12},{4,16},{8,20},{12,24},{16,28},{1,13},{5,17},{9,21},{13,25},... | collective-permute-start | bytes 393224 | tf_op jit(solution)/shard_map/ppermute | solution.py:232
  23.1 8.0 %collective-permute-start.1 = (bf16[512,128]{1,0:T(8,128)(2,1)S(1)}, bf16[512,128]{1,0:T(8,128)(2,1)S(1)}, u32[]{:S(2)}, u32[]{:S(2)}) collective-permute-start(bf16[512,128]{1,0:T(8,128)(2,1)S(1)} %constant_dynamic-update-slice_fusion.refs_4_), channel_id=1, source_target_pairs={{0,16},{4,20},{8,24},{12,28},{1,17},{5,21},{9,25},{13,29},{2,18},{... | collective-permute-start | bytes 393224 | tf_op jit(solution)/shard_map/ppermute | solution.py:232
  31.1 0.9 %copy-start = (bf16[256,512]{1,0:T(8,128)(2,1)S(1)}, bf16[256,512]{1,0:T(8,128)(2,1)}, u32[]{:S(2)}) copy-start(bf16[256,512]{1,0:T(8,128)(2,1)} %query_hbm.1) | copy-start | bytes 786436
  35.9 9.5 %collective-permute-start.7 = (bf16[1,256,512]{2,1,0:T(8,128)(2,1)S(1)}, bf16[1,256,512]{2,1,0:T(8,128)(2,1)S(1)}, u32[]{:S(2)}, u32[]{:S(2)}) collective-permute-start(bf16[1,256,512]{2,1,0:T(8,128)(2,1)S(1)} %bitcast.17), channel_id=1, source_target_pairs={{0,1},{1,0},{2,3},{3,2},{4,5},{5,4},{6,7},{7,6},{8,9},{9,8},{10,11... | collective-permute-start | bytes 786440 | tf_op jit(solution)/shard_map/ppermute | solution.py:213
  36.6 14.1 %collective-permute-start.8 = (bf16[1,256,512]{2,1,0:T(8,128)(2,1)S(1)}, bf16[1,256,512]{2,1,0:T(8,128)(2,1)S(1)}, u32[]{:S(2)}, u32[]{:S(2)}) collective-permute-start(bf16[1,256,512]{2,1,0:T(8,128)(2,1)S(1)} %bitcast.18), channel_id=1, source_target_pairs={{0,3},{1,2},{2,1},{3,0},{4,7},{5,6},{6,5},{7,4},{8,11},{9,10},{10,... | collective-permute-start | bytes 786440 | tf_op jit(solution)/shard_map/ppermute | solution.py:213
  39.0 22.6 %collective-permute-start.14 = (bf16[2,2,128,1024]{3,2,1,0:T(8,128)(2,1)S(1)}, bf16[2,2,128,1024]{3,2,1,0:T(8,128)(2,1)S(1)}, u32[]{:S(2)}, u32[]{:S(2)}) collective-permute-start(bf16[2,2,128,1024]{3,2,1,0:T(8,128)(2,1)S(1)} %pad_maximum_fusion), channel_id=1, source_target_pairs={{0,16},{4,12},{8,24},{12,4},{16,0},{20,28},{24,8},{28,20},{1,17},{... | collective-permute-start | bytes 3145736 | tf_op jit(solution)/shard_map/ppermute | solution.py:225
  41.6 9.2 %collective-permute-start.10 = (bf16[1,1,128,1024]{3,2,1,0:T(8,128)(2,1)S(1)}, bf16[1,1,128,1024]{3,2,1,0:T(8,128)(2,1)S(1)}, u32[]{:S(2)}, u32[]{:S(2)}) collective-permute-start(bf16[1,1,128,1024]{3,2,1,0:T(8,128)(2,1)S(1)} %bitcast.23), channel_id=1, source_target_pairs={{0,8},{4,20},{8,0},{12,28},{16,24},{20,4},{24,16},{28,12},{1,9},{5... | collective-permute-start | bytes 786440 | tf_op jit(solution)/shard_map/ppermute | solution.py:225
  50.9 10.5 %collective-permute-start.12 = (bf16[2,1,128,1024]{3,2,1,0:T(8,128)(2,1)S(1)}, bf16[2,1,128,1024]{3,2,1,0:T(8,128)(2,1)S(1)}, u32[]{:S(2)}, u32[]{:S(2)}) collective-permute-start(bf16[2,1,128,1024]{3,2,1,0:T(8,128)(2,1)S(1)} %pad_maximum_fusion.2), channel_id=1, source_target_pairs={{0,16},{4,12},{8,24},{12,4},{16,0},{20,28},{24,8},{28,20},{1,17},{... | collective-permute-start | bytes 1572872 | tf_op jit(solution)/shard_map/ppermute | solution.py:225
  53.2 6.4 %collective-permute-start.11 = (bf16[1,256,512]{2,1,0:T(8,128)(2,1)S(1)}, bf16[1,256,512]{2,1,0:T(8,128)(2,1)S(1)}, u32[]{:S(2)}, u32[]{:S(2)}) collective-permute-start(bf16[1,256,512]{2,1,0:T(8,128)(2,1)S(1)} %collective-permute-done.8.refs_1_), channel_id=1, source_target_pairs={{0,1},{1,0},{2,3},{3,2},{4,5},{5,4},{6,7},{7,6},{8,9},{9,8},{10,11... | collective-permute-start | bytes 786440 | tf_op jit(solution)/shard_map/ppermute | solution.py:213
  54.5 11.4 %collective-permute-start.13 = (bf16[512,1024]{1,0:T(8,128)(2,1)S(1)}, bf16[512,1024]{1,0:T(8,128)(2,1)S(1)}, u32[]{:S(2)}, u32[]{:S(2)}) collective-permute-start(bf16[512,1024]{1,0:T(8,128)(2,1)S(1)} %bitcast.13), channel_id=1, source_target_pairs={{0,4},{4,0},{8,12},{12,8},{16,20},{20,16},{24,28},{28,24},{1,5},{5... | collective-permute-start | bytes 3145736 | tf_op jit(solution)/shard_map/ppermute | solution.py:218
  61.5 7.0 %collective-permute-start.16 = (bf16[512,1024]{1,0:T(8,128)(2,1)S(1)}, bf16[512,1024]{1,0:T(8,128)(2,1)S(1)}, u32[]{:S(2)}, u32[]{:S(2)}) collective-permute-start(bf16[512,1024]{1,0:T(8,128)(2,1)S(1)} %bitcast.15), channel_id=1, source_target_pairs={{0,4},{4,0},{8,12},{12,8},{16,20},{20,16},{24,28},{28,24},{1,5},{5... | collective-permute-start | bytes 3145736 | tf_op jit(solution)/shard_map/ppermute | solution.py:218
  61.6 6.9 %collective-permute-start.15 = (bf16[512,1024]{1,0:T(8,128)(2,1)S(1)}, bf16[512,1024]{1,0:T(8,128)(2,1)S(1)}, u32[]{:S(2)}, u32[]{:S(2)}) collective-permute-start(bf16[512,1024]{1,0:T(8,128)(2,1)S(1)} %bitcast.21), channel_id=1, source_target_pairs={{0,4},{4,0},{8,12},{12,8},{16,20},{20,16},{24,28},{28,24},{1,5},{5... | collective-permute-start | bytes 3145736 | tf_op jit(solution)/shard_map/ppermute | solution.py:218
  64.0 8.3 %collective-permute-start.20 = (bf16[64,1024]{1,0:T(8,128)(2,1)S(1)}, bf16[64,1024]{1,0:T(8,128)(2,1)S(1)}, u32[]{:S(2)}, u32[]{:S(2)}) collective-permute-start(bf16[64,1024]{1,0:T(8,128)(2,1)S(1)} %get-tuple-element.48), channel_id=1, source_target_pairs={{0,3},{1,2},{2,1},{3,0},{4,7},{5,6},{6,5},{7,4},{8,11},{9,10},{10,... | collective-permute-start | bytes 393224 | tf_op jit(solution)/shard_map/ppermute | solution.py:213
  65.9 10.9 %collective-permute-start.21 = (bf16[64,1024]{1,0:T(8,128)(2,1)S(1)}, bf16[64,1024]{1,0:T(8,128)(2,1)S(1)}, u32[]{:S(2)}, u32[]{:S(2)}) collective-permute-start(bf16[64,1024]{1,0:T(8,128)(2,1)S(1)} %get-tuple-element.49), channel_id=1, source_target_pairs={{0,1},{1,0},{2,3},{3,2},{4,5},{5,4},{6,7},{7,6},{8,9},{9,8},{10,11... | collective-permute-start | bytes 393224 | tf_op jit(solution)/shard_map/ppermute | solution.py:213
  65.9 15.3 %collective-permute-start.22 = (bf16[64,1024]{1,0:T(8,128)(2,1)S(1)}, bf16[64,1024]{1,0:T(8,128)(2,1)S(1)}, u32[]{:S(2)}, u32[]{:S(2)}) collective-permute-start(bf16[64,1024]{1,0:T(8,128)(2,1)S(1)} %get-tuple-element.50), channel_id=1, source_target_pairs={{0,2},{1,3},{2,0},{3,1},{4,6},{5,7},{6,4},{7,5},{8,10},{9,11},{10,... | collective-permute-start | bytes 393224 | tf_op jit(solution)/shard_map/ppermute | solution.py:213
  70.3 12.2 %collective-permute-start.17 = (bf16[64,1024]{1,0:T(8,128)(2,1)S(1)}, bf16[64,1024]{1,0:T(8,128)(2,1)S(1)}, u32[]{:S(2)}, u32[]{:S(2)}) collective-permute-start(bf16[64,1024]{1,0:T(8,128)(2,1)S(1)} %get-tuple-element.44), channel_id=1, source_target_pairs={{0,3},{1,2},{2,1},{3,0},{4,7},{5,6},{6,5},{7,4},{8,11},{9,10},{10,... | collective-permute-start | bytes 393224 | tf_op jit(solution)/shard_map/ppermute | solution.py:213
  72.2 10.3 %collective-permute-start.18 = (bf16[64,1024]{1,0:T(8,128)(2,1)S(1)}, bf16[64,1024]{1,0:T(8,128)(2,1)S(1)}, u32[]{:S(2)}, u32[]{:S(2)}) collective-permute-start(bf16[64,1024]{1,0:T(8,128)(2,1)S(1)} %get-tuple-element.45), channel_id=1, source_target_pairs={{0,1},{1,0},{2,3},{3,2},{4,5},{5,4},{6,7},{7,6},{8,9},{9,8},{10,11... | collective-permute-start | bytes 393224 | tf_op jit(solution)/shard_map/ppermute | solution.py:213
  72.3 16.7 %collective-permute-start.19 = (bf16[64,1024]{1,0:T(8,128)(2,1)S(1)}, bf16[64,1024]{1,0:T(8,128)(2,1)S(1)}, u32[]{:S(2)}, u32[]{:S(2)}) collective-permute-start(bf16[64,1024]{1,0:T(8,128)(2,1)S(1)} %get-tuple-element.46), channel_id=1, source_target_pairs={{0,2},{1,3},{2,0},{3,1},{4,6},{5,7},{6,4},{7,5},{8,10},{9,11},{10,... | collective-permute-start | bytes 393224 | tf_op jit(solution)/shard_map/ppermute | solution.py:213

commit v4 on v2

--- a/solution.py
+++ b/solution.py
@@ -48,7 +48,7 @@
         )
         scores = jnp.where(allowed, scores * log2_scale, big_negative)
         top = jnp.max(scores, axis=1, keepdims=True)
-        expo = jnp.where(allowed, jnp.exp2(scores - top), 0.0)
+        expo = jnp.exp2(scores - top)
         total = jnp.sum(expo, axis=1, keepdims=True)
         summed = jnp.dot(expo.astype(jnp.bfloat16), values, preferred_element_type=jnp.float32)
         out_ref[:, head * HD : (head + 1) * HD] = (summed / total).astype(jnp.bfloat16)
@@ -99,7 +99,7 @@
     cols = own_weight.shape[1] // CORES
     share = depth // chips
     rows_out = rows // planes
-    block = min(cols, 256)
+    block = min(cols, 512)
     size = (planes - 1) * depth
     aligned = share % HD == 0
     chip_orders = [chip_order(chips, core) for core in range(CORES)]
@@ -264,7 +264,6 @@
     plane_stages, chip_stages = planes.bit_length() - 1, chips.bit_length() - 1
     first = jnp.stack(tie([fetched[x] for x in groups[0]], pieces[1:-1]))[None]
     first = jnp.concatenate([first, crossed(first, 0)])
-    pieces, first = lax.optimization_barrier((pieces, first))
     rest = crossed(first, 1)
     attended = [attention(queries, pieces, lengths, ctx_index * rows)[None]]
     own_weight = lax.dynamic_slice_in_dim(

time: 88.3 us -> 87.8 us (level)
  starting transfers between devices: 40.1 us -> 36.9 us
  waiting for transfers between devices: 30.6 us -> 33.6 us
    ppermute x12, waiting for transfers between devices: 18.1 us -> 29.9 us  [paired(): return lax.ppermute(shard, 'head', [(i, i ^ x) for i in range(length)])]
    ppermute x4, waiting for transfers between devices: 11.3 us -> 0.14 us  [crossed(): lax.ppermute(shard, 'ctx', [(i, i ^ CORES << bit[i % CORES]) for i in ran...]
    ppermute x4, waiting for transfers between devices: 1.23 us -> 3.57 us  [later(): return lax.ppermute(shard, 'ctx', [(i, i + by) for i in range(length - by)])]
    ppermute x4, starting transfers between devices: 9.59 us -> 7.3 us  [crossed(): lax.ppermute(shard, 'ctx', [(i, i ^ CORES << bit[i % CORES]) for i in ran...]
  transfers between devices with their start and end apart: 23 -> 23, of which waited for: 9 -> 10; matrix products, arithmetic and copies ran while one was open for 5% -> 5% of each run, Pallas kernels for 10% -> 10%
where the time goes in v4:
time: 87.8 us; the launch traced here: 87.4 us
  starting transfers between devices  36.9 us (42%)
  waiting for transfers between devices  33.6 us (38%)
  Pallas kernels  9.98 us (11%)
  local copies, waits for them, and re-layouts  5.63 us (6%)
  other arithmetic  1.11 us (1%)
    ppermute x12, waiting for transfers between devices, paired(): return lax.ppermute(shard, 'head', [(i, i ^ x) for i in range(length)])  29.9 us
    ppermute x12, starting transfers between devices, paired(): return lax.ppermute(shard, 'head', [(i, i ^ x) for i in range(length)])  18.8 us
    ppermute x4, starting transfers between devices, later(): return lax.ppermute(shard, 'ctx', [(i, i + by) for i in range(length - by)])  10.2 us
    ppermute x4, starting transfers between devices, crossed(): lax.ppermute(shard, 'ctx', [(i, i ^ CORES << bit[i % CORES]) for i in ran...  7.3 us
    pallas_call x2, Pallas kernels, project(): pl.pallas_call(kernel, out_shape=[jax.ShapeDtypeStruct((rows_out, cols),...  3.64 us
    pallas_call x1, Pallas kernels, attention(): pl.pallas_call(attention_kernel, out_shape=jax.ShapeDtypeStruct(queries.s...  3.6 us
    ppermute x4, waiting for transfers between devices, later(): return lax.ppermute(shard, 'ctx', [(i, i + by) for i in range(length - by)])  3.57 us
    pallas_call x2, Pallas kernels, assemble(): pl.pallas_call(kernel, out_shape=jax.ShapeDtypeStruct((rows, width), jnp....  2.73 us
  transfers between devices with their start and end apart: 23, of which 10 were waited for; matrix products, arithmetic and copies ran while one was open for 5% of the time, Pallas kernels for 10%

profile of v4, /device:TPU:0, one launch (start us, length us, event | category | flops | bytes accessed | tf_op | source)
XLA Modules:
  0.0 87.4 jit_solution(15436139780769148077)
XLA Ops:
  0.0 1.2 %fusion = (bf16[128,1024]{1,0:T(8,128)(2,1)S(1)}, bf16[128,1024]{1,0:T(8,128)(2,1)S(1)}, bf16[128,1024]{1,0:T(8,128)(2,1)S(1)}) fusion(bf16[512,8192]{1,0:T(8,128)(2,1)} %param.9, s32[]{:T(128)S(6)} %select_n.30, s32[]{:T(128)S(6)} %select_n.33, s32[]{:T(128)S(6)} %select_n.32, s32[]{:T(128)S(6)} %select_n.31), kind=kLoop, calls=%fused_computation.9 | loop fusion | bytes 1572880 | tf_op jit(solution)/shard_map/dynamic_slice | solution.py:250
  1.2 5.1 %collective-permute-start.6 = (bf16[128,1024]{1,0:T(8,128)(2,1)S(1)}, bf16[128,1024]{1,0:T(8,128)(2,1)S(1)}, u32[]{:S(2)}, u32[]{:S(2)}) collective-permute-start(bf16[128,1024]{1,0:T(8,128)(2,1)S(1)} %get-tuple-element.46), channel_id=1, source_target_pairs={{0,3},{1,2},{2,1},{3,0},{4,7},{5,6},{6,5},{7,4},{8,11},{9,10},{10,... | collective-permute-start | bytes 786440 | tf_op jit(solution)/shard_map/ppermute | solution.py:213
  6.3 0.8 constant_dynamic-update-slice_fusion.1
  7.1 0.9 constant_dynamic-update-slice_fusion.refs_4_
  8.0 2.6 %collective-permute-start.1 = (bf16[512,128]{1,0:T(8,128)(2,1)S(1)}, bf16[512,128]{1,0:T(8,128)(2,1)S(1)}, u32[]{:S(2)}, u32[]{:S(2)}) collective-permute-start(bf16[512,128]{1,0:T(8,128)(2,1)S(1)} %constant_dynamic-update-slice_fusion.refs_4_), channel_id=1, source_target_pairs={{0,12},{4,16},{8,20},{12,24},{16,28},{1,13},{5,17},{9,21},{13,25},... | collective-permute-start | bytes 393224 | tf_op jit(solution)/shard_map/ppermute | solution.py:232
  10.5 3.4 %collective-permute-start.2 = (bf16[512,128]{1,0:T(8,128)(2,1)S(1)}, bf16[512,128]{1,0:T(8,128)(2,1)S(1)}, u32[]{:S(2)}, u32[]{:S(2)}) collective-permute-start(bf16[512,128]{1,0:T(8,128)(2,1)S(1)} %constant_dynamic-update-slice_fusion.refs_4_), channel_id=1, source_target_pairs={{0,8},{4,12},{8,16},{12,20},{16,24},{20,28},{1,9},{5,13},{9,17},{1... | collective-permute-start | bytes 393224 | tf_op jit(solution)/shard_map/ppermute | solution.py:232
  14.0 2.6 %collective-permute-start.3 = (bf16[512,128]{1,0:T(8,128)(2,1)S(1)}, bf16[512,128]{1,0:T(8,128)(2,1)S(1)}, u32[]{:S(2)}, u32[]{:S(2)}) collective-permute-start(bf16[512,128]{1,0:T(8,128)(2,1)S(1)} %constant_dynamic-update-slice_fusion.refs_4_), channel_id=1, source_target_pairs={{0,4},{4,8},{8,12},{12,16},{16,20},{20,24},{24,28},{1,5},{5,9},{9,... | collective-permute-start | bytes 393224 | tf_op jit(solution)/shard_map/ppermute | solution.py:232
  16.6 1.2 %collective-permute-done.2.refs_2_ = bf16[512,128]{1,0:T(8,128)(2,1)S(1)} collective-permute-done((bf16[512,128]{1,0:T(8,128)(2,1)S(1)}, bf16[512,128]{1,0:T(8,128)(2,1)S(1)}, u32[]{:S(2)}, u32[]{:S(2)}) %collective-permute-start.2) | collective-permute-done | bytes 131104 | tf_op jit(solution)/shard_map/ppermute | solution.py:232
  18.4 3.5 %collective-permute-start.9 = (bf16[1,2,128,1024]{3,2,1,0:T(8,128)(2,1)S(1)}, bf16[1,2,128,1024]{3,2,1,0:T(8,128)(2,1)S(1)}, u32[]{:S(2)}, u32[]{:S(2)}) collective-permute-start(bf16[1,2,128,1024]{3,2,1,0:T(8,128)(2,1)S(1)} %maximum_bitcast_fusion), channel_id=1, source_target_pairs={{0,8},{4,20},{8,0},{12,28},{16,24},{20,4},{24,16},{28,12},{1,9},{5... | collective-permute-start | bytes 1572872 | tf_op jit(solution)/shard_map/ppermute | solution.py:225
  21.9 1.6 %collective-permute-start = (bf16[512,128]{1,0:T(8,128)(2,1)S(1)}, bf16[512,128]{1,0:T(8,128)(2,1)S(1)}, u32[]{:S(2)}, u32[]{:S(2)}) collective-permute-start(bf16[512,128]{1,0:T(8,128)(2,1)S(1)} %constant_dynamic-update-slice_fusion.refs_4_), channel_id=1, source_target_pairs={{0,16},{4,20},{8,24},{12,28},{1,17},{5,21},{9,25},{13,29},{2,18},{... | collective-permute-start | bytes 393224 | tf_op jit(solution)/shard_map/ppermute | solution.py:232
  23.5 0.8 collective-permute-start.7
  25.1 2.3 %collective-permute-done.refs_0_ = bf16[512,128]{1,0:T(8,128)(2,1)S(1)} collective-permute-done((bf16[512,128]{1,0:T(8,128)(2,1)S(1)}, bf16[512,128]{1,0:T(8,128)(2,1)S(1)}, u32[]{:S(2)}, u32[]{:S(2)}) %collective-permute-start) | collective-permute-done | bytes 131104 | tf_op jit(solution)/shard_map/ppermute | solution.py:232
  27.4 0.9 %copy-done = bf16[256,512]{1,0:T(8,128)(2,1)S(1)} copy-done((bf16[256,512]{1,0:T(8,128)(2,1)S(1)}, bf16[256,512]{1,0:T(8,128)(2,1)}, u32[]{:S(2)}) %copy-start) | copy-done | bytes 262168
  28.4 3.6 %attention.1 = bf16[256,512]{1,0:T(8,128)(2,1)S(1)} custom-call(s32[9]{0:T(128)S(1)} %pad_add_fusion.1.place_ref, bf16[256,512]{1,0:T(8,128)(2,1)S(1)} %copy-done, bf16[512,128]{1,0:T(8,128)(2,1)S(1)} %collective-permute-done.refs_0_, bf16[512,128]{1,0:T(8,128)(2,1)S(1)} %collective-permute-done.1.refs_1_, ...), custom_call_target="tpu_custom_call" | custom-call | tf_op jit(solution)/shard_map/attention/pallas_call | solution.py:59
  32.0 2.1 %collective-permute-start.4 = (bf16[1,256,512]{2,1,0:T(8,128)(2,1)S(1)}, bf16[1,256,512]{2,1,0:T(8,128)(2,1)S(1)}, u32[]{:S(2)}, u32[]{:S(2)}) collective-permute-start(bf16[1,256,512]{2,1,0:T(8,128)(2,1)S(1)} %bitcast.17), channel_id=1, source_target_pairs={{0,1},{1,0},{2,3},{3,2},{4,5},{5,4},{6,7},{7,6},{8,9},{9,8},{10,11... | collective-permute-start | bytes 786440 | tf_op jit(solution)/shard_map/ppermute | solution.py:213
  34.4 2.5 %collective-permute-start.14 = (bf16[2,2,128,1024]{3,2,1,0:T(8,128)(2,1)S(1)}, bf16[2,2,128,1024]{3,2,1,0:T(8,128)(2,1)S(1)}, u32[]{:S(2)}, u32[]{:S(2)}) collective-permute-start(bf16[2,2,128,1024]{3,2,1,0:T(8,128)(2,1)S(1)} %pad_maximum_fusion), channel_id=1, source_target_pairs={{0,16},{4,12},{8,24},{12,4},{16,0},{20,28},{24,8},{28,20},{1,17},{... | collective-permute-start | bytes 3145736 | tf_op jit(solution)/shard_map/ppermute | solution.py:225
  37.0 1.3 %collective-permute-done.7 = bf16[128,1024]{1,0:T(8,128)(2,1)S(1)} collective-permute-done((bf16[128,1024]{1,0:T(8,128)(2,1)S(1)}, bf16[128,1024]{1,0:T(8,128)(2,1)S(1)}, u32[]{:S(2)}, u32[]{:S(2)}) %collective-permute-start.7) | collective-permute-done | bytes 262176 | tf_op jit(solution)/shard_map/ppermute | solution.py:213
  38.8 1.8 %constant_dynamic-slice_fusion.refs_4_ = bf16[512,2048]{1,0:T(8,128)(2,1)S(1)} fusion(bf16[512,8192]{1,0:T(8,128)(2,1)} %param.9, s32[]{:T(128)S(6)} %select_n.34), kind=kLoop, calls=%fused_computation.8 | loop fusion | bytes 4194308 | tf_op jit(solution)/shard_map/dynamic_slice | solution.py:269
  40.7 8.2 %collective-permute-done.4.refs_2_ = bf16[1,256,512]{2,1,0:T(8,128)(2,1)S(1)} collective-permute-done((bf16[1,256,512]{2,1,0:T(8,128)(2,1)S(1)}, bf16[1,256,512]{2,1,0:T(8,128)(2,1)S(1)}, u32[]{:S(2)}, u32[]{:S(2)}) %collective-permute-start.4) | collective-permute-done | bytes 262176 | tf_op jit(solution)/shard_map/ppermute | solution.py:213
  49.7 1.6 %collective-permute-start.11 = (bf16[1,256,512]{2,1,0:T(8,128)(2,1)S(1)}, bf16[1,256,512]{2,1,0:T(8,128)(2,1)S(1)}, u32[]{:S(2)}, u32[]{:S(2)}) collective-permute-start(bf16[1,256,512]{2,1,0:T(8,128)(2,1)S(1)} %collective-permute-done.5.refs_1_), channel_id=1, source_target_pairs={{0,1},{1,0},{2,3},{3,2},{4,5},{5,4},{6,7},{7,6},{8,9},{9,8},{10,11... | collective-permute-start | bytes 786440 | tf_op jit(solution)/shard_map/ppermute | solution.py:213
  51.4 6.7 %collective-permute-done.11.refs_3_ = bf16[1,256,512]{2,1,0:T(8,128)(2,1)S(1)} collective-permute-done((bf16[1,256,512]{2,1,0:T(8,128)(2,1)S(1)}, bf16[1,256,512]{2,1,0:T(8,128)(2,1)S(1)}, u32[]{:S(2)}, u32[]{:S(2)}) %collective-permute-start.11) | collective-permute-done | bytes 262176 | tf_op jit(solution)/shard_map/ppermute | solution.py:213
  59.0 1.8 %project.3 = (bf16[64,1024]{1,0:T(8,128)(2,1)S(1)}, bf16[64,1024]{1,0:T(8,128)(2,1)S(1)}, bf16[64,1024]{1,0:T(8,128)(2,1)S(1)}, bf16[64,1024]{1,0:T(8,128)(2,1)S(1)}) custom-call(s32[3]{0:T(128)S(1)} %pad_add_fusion.place_ref, bf16[1,256,512]{2,1,0:T(8,128)(2,1)S(1)} %bitcast.19, bf16[1,256,512]{2,1,0:T(8,128)(2,1)S(1)} %collective-permute-done.5.refs_1_, ...), custom_call_target="tpu_custom_call" | custom-call | flops 1073741824 | bytes 5767168 | tf_op jit(solution)/shard_map/project/pallas_call | solution.py:156
  60.8 3.2 %collective-permute-start.20 = (bf16[64,1024]{1,0:T(8,128)(2,1)S(1)}, bf16[64,1024]{1,0:T(8,128)(2,1)S(1)}, u32[]{:S(2)}, u32[]{:S(2)}) collective-permute-start(bf16[64,1024]{1,0:T(8,128)(2,1)S(1)} %get-tuple-element.42), channel_id=1, source_target_pairs={{0,3},{1,2},{2,1},{3,0},{4,7},{5,6},{6,5},{7,4},{8,11},{9,10},{10,... | collective-permute-start | bytes 393224 | tf_op jit(solution)/shard_map/ppermute | solution.py:213
  64.1 1.2 %collective-permute-start.22 = (bf16[64,1024]{1,0:T(8,128)(2,1)S(1)}, bf16[64,1024]{1,0:T(8,128)(2,1)S(1)}, u32[]{:S(2)}, u32[]{:S(2)}) collective-permute-start(bf16[64,1024]{1,0:T(8,128)(2,1)S(1)} %get-tuple-element.44), channel_id=1, source_target_pairs={{0,2},{1,3},{2,0},{3,1},{4,6},{5,7},{6,4},{7,5},{8,10},{9,11},{10,... | collective-permute-start | bytes 393224 | tf_op jit(solution)/shard_map/ppermute | solution.py:213
  65.3 1.8 %project.2 = (bf16[64,1024]{1,0:T(8,128)(2,1)S(1)}, bf16[64,1024]{1,0:T(8,128)(2,1)S(1)}, bf16[64,1024]{1,0:T(8,128)(2,1)S(1)}, bf16[64,1024]{1,0:T(8,128)(2,1)S(1)}) custom-call(s32[3]{0:T(128)S(1)} %pad_add_fusion.place_ref, bf16[1,256,512]{2,1,0:T(8,128)(2,1)S(1)} %bitcast.20, bf16[1,256,512]{2,1,0:T(8,128)(2,1)S(1)} %collective-permute-done.5.refs_1_, ...), custom_call_target="tpu_custom_call" | custom-call | flops 1073741824 | bytes 5767168 | tf_op jit(solution)/shard_map/project/pallas_call | solution.py:156
  67.1 3.2 %collective-permute-start.17 = (bf16[64,1024]{1,0:T(8,128)(2,1)S(1)}, bf16[64,1024]{1,0:T(8,128)(2,1)S(1)}, u32[]{:S(2)}, u32[]{:S(2)}) collective-permute-start(bf16[64,1024]{1,0:T(8,128)(2,1)S(1)} %get-tuple-element.38), channel_id=1, source_target_pairs={{0,3},{1,2},{2,1},{3,0},{4,7},{5,6},{6,5},{7,4},{8,11},{9,10},{10,... | collective-permute-start | bytes 393224 | tf_op jit(solution)/shard_map/ppermute | solution.py:213
  70.4 1.2 %collective-permute-start.19 = (bf16[64,1024]{1,0:T(8,128)(2,1)S(1)}, bf16[64,1024]{1,0:T(8,128)(2,1)S(1)}, u32[]{:S(2)}, u32[]{:S(2)}) collective-permute-start(bf16[64,1024]{1,0:T(8,128)(2,1)S(1)} %get-tuple-element.40), channel_id=1, source_target_pairs={{0,2},{1,3},{2,0},{3,1},{4,6},{5,7},{6,4},{7,5},{8,10},{9,11},{10,... | collective-permute-start | bytes 393224 | tf_op jit(solution)/shard_map/ppermute | solution.py:213
  71.6 1.6 %collective-permute-done.21.refs_2_ = bf16[64,1024]{1,0:T(8,128)(2,1)S(1)} collective-permute-done((bf16[64,1024]{1,0:T(8,128)(2,1)S(1)}, bf16[64,1024]{1,0:T(8,128)(2,1)S(1)}, u32[]{:S(2)}, u32[]{:S(2)}) %collective-permute-start.21) | collective-permute-done | bytes 131104 | tf_op jit(solution)/shard_map/ppermute | solution.py:213
  73.1 5.4 %collective-permute-done.22.refs_3_ = bf16[64,1024]{1,0:T(8,128)(2,1)S(1)} collective-permute-done((bf16[64,1024]{1,0:T(8,128)(2,1)S(1)}, bf16[64,1024]{1,0:T(8,128)(2,1)S(1)}, u32[]{:S(2)}, u32[]{:S(2)}) %collective-permute-start.22) | collective-permute-done | bytes 131104 | tf_op jit(solution)/shard_map/ppermute | solution.py:213
  78.5 1.4 %assemble.2.refs_4_ = bf16[64,8192]{1,0:T(8,128)(2,1)} custom-call(s32[3]{0:T(128)S(1)} %pad_add_fusion.place_ref, bf16[64,1024]{1,0:T(8,128)(2,1)S(1)} %get-tuple-element.41.refs_0_, bf16[64,1024]{1,0:T(8,128)(2,1)S(1)} %collective-permute-done.20.refs_1_, bf16[64,1024]{1,0:T(8,128)(2,1)S(1)} %collective-permute-done.21.refs_2_, ...), custom_call_target="tpu_custom_call" | custom-call | tf_op jit(solution)/shard_map/assemble/pallas_call | solution.py:197
  79.9 6.1 %collective-permute-done.19.refs_3_ = bf16[64,1024]{1,0:T(8,128)(2,1)S(1)} collective-permute-done((bf16[64,1024]{1,0:T(8,128)(2,1)S(1)}, bf16[64,1024]{1,0:T(8,128)(2,1)S(1)}, u32[]{:S(2)}, u32[]{:S(2)}) %collective-permute-start.19) | collective-permute-done | bytes 131104 | tf_op jit(solution)/shard_map/ppermute | solution.py:213
  86.1 1.4 %assemble.3 = bf16[64,8192]{1,0:T(8,128)(2,1)} custom-call(s32[3]{0:T(128)S(1)} %pad_add_fusion.place_ref, bf16[64,1024]{1,0:T(8,128)(2,1)S(1)} %get-tuple-element.37.refs_0_, bf16[64,1024]{1,0:T(8,128)(2,1)S(1)} %collective-permute-done.17.refs_1_, bf16[64,1024]{1,0:T(8,128)(2,1)S(1)} %collective-permute-done.18.refs_2_, ...), custom_call_target="tpu_custom_call", output_to_operand_aliasing={{}: (5, {})} | custom-call | tf_op jit(solution)/shard_map/assemble/pallas_call | solution.py:197
  (31 shorter events, 3.8 us)
Async XLA Ops:
  1.2 16.6 %collective-permute-start.6 = (bf16[128,1024]{1,0:T(8,128)(2,1)S(1)}, bf16[128,1024]{1,0:T(8,128)(2,1)S(1)}, u32[]{:S(2)}, u32[]{:S(2)}) collective-permute-start(bf16[128,1024]{1,0:T(8,128)(2,1)S(1)} %get-tuple-element.46), channel_id=1, source_target_pairs={{0,3},{1,2},{2,1},{3,0},{4,7},{5,6},{6,5},{7,4},{8,11},{9,10},{10,... | collective-permute-start | bytes 786440 | tf_op jit(solution)/shard_map/ppermute | solution.py:213
  6.3 12.0 %collective-permute-start.8 = (bf16[128,1024]{1,0:T(8,128)(2,1)S(1)}, bf16[128,1024]{1,0:T(8,128)(2,1)S(1)}, u32[]{:S(2)}, u32[]{:S(2)}) collective-permute-start(bf16[128,1024]{1,0:T(8,128)(2,1)S(1)} %get-tuple-element.45), channel_id=1, source_target_pairs={{0,1},{1,0},{2,3},{3,2},{4,5},{5,4},{6,7},{7,6},{8,9},{9,8},{10,11... | collective-permute-start | bytes 786440 | tf_op jit(solution)/shard_map/ppermute | solution.py:213
  8.0 8.6 %collective-permute-start.1 = (bf16[512,128]{1,0:T(8,128)(2,1)S(1)}, bf16[512,128]{1,0:T(8,128)(2,1)S(1)}, u32[]{:S(2)}, u32[]{:S(2)}) collective-permute-start(bf16[512,128]{1,0:T(8,128)(2,1)S(1)} %constant_dynamic-update-slice_fusion.refs_4_), channel_id=1, source_target_pairs={{0,12},{4,16},{8,20},{12,24},{16,28},{1,13},{5,17},{9,21},{13,25},... | collective-permute-start | bytes 393224 | tf_op jit(solution)/shard_map/ppermute | solution.py:232
  10.5 7.3 %collective-permute-start.2 = (bf16[512,128]{1,0:T(8,128)(2,1)S(1)}, bf16[512,128]{1,0:T(8,128)(2,1)S(1)}, u32[]{:S(2)}, u32[]{:S(2)}) collective-permute-start(bf16[512,128]{1,0:T(8,128)(2,1)S(1)} %constant_dynamic-update-slice_fusion.refs_4_), channel_id=1, source_target_pairs={{0,8},{4,12},{8,16},{12,20},{16,24},{20,28},{1,9},{5,13},{9,17},{1... | collective-permute-start | bytes 393224 | tf_op jit(solution)/shard_map/ppermute | solution.py:232
  14.0 3.9 %collective-permute-start.3 = (bf16[512,128]{1,0:T(8,128)(2,1)S(1)}, bf16[512,128]{1,0:T(8,128)(2,1)S(1)}, u32[]{:S(2)}, u32[]{:S(2)}) collective-permute-start(bf16[512,128]{1,0:T(8,128)(2,1)S(1)} %constant_dynamic-update-slice_fusion.refs_4_), channel_id=1, source_target_pairs={{0,4},{4,8},{8,12},{12,16},{16,20},{20,24},{24,28},{1,5},{5,9},{9,... | collective-permute-start | bytes 393224 | tf_op jit(solution)/shard_map/ppermute | solution.py:232
  18.4 16.0 %collective-permute-start.9 = (bf16[1,2,128,1024]{3,2,1,0:T(8,128)(2,1)S(1)}, bf16[1,2,128,1024]{3,2,1,0:T(8,128)(2,1)S(1)}, u32[]{:S(2)}, u32[]{:S(2)}) collective-permute-start(bf16[1,2,128,1024]{3,2,1,0:T(8,128)(2,1)S(1)} %maximum_bitcast_fusion), channel_id=1, source_target_pairs={{0,8},{4,20},{8,0},{12,28},{16,24},{20,4},{24,16},{28,12},{1,9},{5... | collective-permute-start | bytes 1572872 | tf_op jit(solution)/shard_map/ppermute | solution.py:225
  21.9 5.6 %collective-permute-start = (bf16[512,128]{1,0:T(8,128)(2,1)S(1)}, bf16[512,128]{1,0:T(8,128)(2,1)S(1)}, u32[]{:S(2)}, u32[]{:S(2)}) collective-permute-start(bf16[512,128]{1,0:T(8,128)(2,1)S(1)} %constant_dynamic-update-slice_fusion.refs_4_), channel_id=1, source_target_pairs={{0,16},{4,20},{8,24},{12,28},{1,17},{5,21},{9,25},{13,29},{2,18},{... | collective-permute-start | bytes 393224 | tf_op jit(solution)/shard_map/ppermute | solution.py:232
  23.5 14.8 %collective-permute-start.7 = (bf16[128,1024]{1,0:T(8,128)(2,1)S(1)}, bf16[128,1024]{1,0:T(8,128)(2,1)S(1)}, u32[]{:S(2)}, u32[]{:S(2)}) collective-permute-start(bf16[128,1024]{1,0:T(8,128)(2,1)S(1)} %get-tuple-element.25), channel_id=1, source_target_pairs={{0,2},{1,3},{2,0},{3,1},{4,6},{5,7},{6,4},{7,5},{8,10},{9,11},{10,... | collective-permute-start | bytes 786440 | tf_op jit(solution)/shard_map/ppermute | solution.py:213
  27.4 0.9 %copy-start = (bf16[256,512]{1,0:T(8,128)(2,1)S(1)}, bf16[256,512]{1,0:T(8,128)(2,1)}, u32[]{:S(2)}) copy-start(bf16[256,512]{1,0:T(8,128)(2,1)} %query_hbm.1) | copy-start | bytes 786436
  32.0 16.9 %collective-permute-start.4 = (bf16[1,256,512]{2,1,0:T(8,128)(2,1)S(1)}, bf16[1,256,512]{2,1,0:T(8,128)(2,1)S(1)}, u32[]{:S(2)}, u32[]{:S(2)}) collective-permute-start(bf16[1,256,512]{2,1,0:T(8,128)(2,1)S(1)} %bitcast.17), channel_id=1, source_target_pairs={{0,1},{1,0},{2,3},{3,2},{4,5},{5,4},{6,7},{7,6},{8,9},{9,8},{10,11... | collective-permute-start | bytes 786440 | tf_op jit(solution)/shard_map/ppermute | solution.py:213
  34.1 14.8 %collective-permute-start.5 = (bf16[1,256,512]{2,1,0:T(8,128)(2,1)S(1)}, bf16[1,256,512]{2,1,0:T(8,128)(2,1)S(1)}, u32[]{:S(2)}, u32[]{:S(2)}) collective-permute-start(bf16[1,256,512]{2,1,0:T(8,128)(2,1)S(1)} %bitcast.18), channel_id=1, source_target_pairs={{0,3},{1,2},{2,1},{3,0},{4,7},{5,6},{6,5},{7,4},{8,11},{9,10},{10,... | collective-permute-start | bytes 786440 | tf_op jit(solution)/shard_map/ppermute | solution.py:213
  34.4 24.0 %collective-permute-start.14 = (bf16[2,2,128,1024]{3,2,1,0:T(8,128)(2,1)S(1)}, bf16[2,2,128,1024]{3,2,1,0:T(8,128)(2,1)S(1)}, u32[]{:S(2)}, u32[]{:S(2)}) collective-permute-start(bf16[2,2,128,1024]{3,2,1,0:T(8,128)(2,1)S(1)} %pad_maximum_fusion), channel_id=1, source_target_pairs={{0,16},{4,12},{8,24},{12,4},{16,0},{20,28},{24,8},{28,20},{1,17},{... | collective-permute-start | bytes 3145736 | tf_op jit(solution)/shard_map/ppermute | solution.py:225
  38.3 10.6 %collective-permute-start.10 = (bf16[1,1,128,1024]{3,2,1,0:T(8,128)(2,1)S(1)}, bf16[1,1,128,1024]{3,2,1,0:T(8,128)(2,1)S(1)}, u32[]{:S(2)}, u32[]{:S(2)}) collective-permute-start(bf16[1,1,128,1024]{3,2,1,0:T(8,128)(2,1)S(1)} %bitcast.23), channel_id=1, source_target_pairs={{0,8},{4,20},{8,0},{12,28},{16,24},{20,4},{24,16},{28,12},{1,9},{5... | collective-permute-start | bytes 786440 | tf_op jit(solution)/shard_map/ppermute | solution.py:225
  49.0 9.2 %collective-permute-start.12 = (bf16[2,1,128,1024]{3,2,1,0:T(8,128)(2,1)S(1)}, bf16[2,1,128,1024]{3,2,1,0:T(8,128)(2,1)S(1)}, u32[]{:S(2)}, u32[]{:S(2)}) collective-permute-start(bf16[2,1,128,1024]{3,2,1,0:T(8,128)(2,1)S(1)} %pad_maximum_fusion.2), channel_id=1, source_target_pairs={{0,16},{4,12},{8,24},{12,4},{16,0},{20,28},{24,8},{28,20},{1,17},{... | collective-permute-start | bytes 1572872 | tf_op jit(solution)/shard_map/ppermute | solution.py:225
  49.7 8.4 %collective-permute-start.11 = (bf16[1,256,512]{2,1,0:T(8,128)(2,1)S(1)}, bf16[1,256,512]{2,1,0:T(8,128)(2,1)S(1)}, u32[]{:S(2)}, u32[]{:S(2)}) collective-permute-start(bf16[1,256,512]{2,1,0:T(8,128)(2,1)S(1)} %collective-permute-done.5.refs_1_), channel_id=1, source_target_pairs={{0,1},{1,0},{2,3},{3,2},{4,5},{5,4},{6,7},{7,6},{8,9},{9,8},{10,11... | collective-permute-start | bytes 786440 | tf_op jit(solution)/shard_map/ppermute | solution.py:213
  51.4 12.7 %collective-permute-start.13 = (bf16[512,1024]{1,0:T(8,128)(2,1)S(1)}, bf16[512,1024]{1,0:T(8,128)(2,1)S(1)}, u32[]{:S(2)}, u32[]{:S(2)}) collective-permute-start(bf16[512,1024]{1,0:T(8,128)(2,1)S(1)} %bitcast.13), channel_id=1, source_target_pairs={{0,4},{4,0},{8,12},{12,8},{16,20},{20,16},{24,28},{28,24},{1,5},{5... | collective-permute-start | bytes 3145736 | tf_op jit(solution)/shard_map/ppermute | solution.py:218
  58.3 6.9 %collective-permute-start.16 = (bf16[512,1024]{1,0:T(8,128)(2,1)S(1)}, bf16[512,1024]{1,0:T(8,128)(2,1)S(1)}, u32[]{:S(2)}, u32[]{:S(2)}) collective-permute-start(bf16[512,1024]{1,0:T(8,128)(2,1)S(1)} %bitcast.15), channel_id=1, source_target_pairs={{0,4},{4,0},{8,12},{12,8},{16,20},{20,16},{24,28},{28,24},{1,5},{5... | collective-permute-start | bytes 3145736 | tf_op jit(solution)/shard_map/ppermute | solution.py:218
  58.4 6.9 %collective-permute-start.15 = (bf16[512,1024]{1,0:T(8,128)(2,1)S(1)}, bf16[512,1024]{1,0:T(8,128)(2,1)S(1)}, u32[]{:S(2)}, u32[]{:S(2)}) collective-permute-start(bf16[512,1024]{1,0:T(8,128)(2,1)S(1)} %bitcast.21), channel_id=1, source_target_pairs={{0,4},{4,0},{8,12},{12,8},{16,20},{20,16},{24,28},{28,24},{1,5},{5... | collective-permute-start | bytes 3145736 | tf_op jit(solution)/shard_map/ppermute | solution.py:218
  60.8 9.5 %collective-permute-start.20 = (bf16[64,1024]{1,0:T(8,128)(2,1)S(1)}, bf16[64,1024]{1,0:T(8,128)(2,1)S(1)}, u32[]{:S(2)}, u32[]{:S(2)}) collective-permute-start(bf16[64,1024]{1,0:T(8,128)(2,1)S(1)} %get-tuple-element.42), channel_id=1, source_target_pairs={{0,3},{1,2},{2,1},{3,0},{4,7},{5,6},{6,5},{7,4},{8,11},{9,10},{10,... | collective-permute-start | bytes 393224 | tf_op jit(solution)/shard_map/ppermute | solution.py:213
  64.1 9.1 %collective-permute-start.21 = (bf16[64,1024]{1,0:T(8,128)(2,1)S(1)}, bf16[64,1024]{1,0:T(8,128)(2,1)S(1)}, u32[]{:S(2)}, u32[]{:S(2)}) collective-permute-start(bf16[64,1024]{1,0:T(8,128)(2,1)S(1)} %get-tuple-element.43), channel_id=1, source_target_pairs={{0,1},{1,0},{2,3},{3,2},{4,5},{5,4},{6,7},{7,6},{8,9},{9,8},{10,11... | collective-permute-start | bytes 393224 | tf_op jit(solution)/shard_map/ppermute | solution.py:213
  64.1 14.5 %collective-permute-start.22 = (bf16[64,1024]{1,0:T(8,128)(2,1)S(1)}, bf16[64,1024]{1,0:T(8,128)(2,1)S(1)}, u32[]{:S(2)}, u32[]{:S(2)}) collective-permute-start(bf16[64,1024]{1,0:T(8,128)(2,1)S(1)} %get-tuple-element.44), channel_id=1, source_target_pairs={{0,2},{1,3},{2,0},{3,1},{4,6},{5,7},{6,4},{7,5},{8,10},{9,11},{10,... | collective-permute-start | bytes 393224 | tf_op jit(solution)/shard_map/ppermute | solution.py:213
  67.1 12.8 %collective-permute-start.17 = (bf16[64,1024]{1,0:T(8,128)(2,1)S(1)}, bf16[64,1024]{1,0:T(8,128)(2,1)S(1)}, u32[]{:S(2)}, u32[]{:S(2)}) collective-permute-start(bf16[64,1024]{1,0:T(8,128)(2,1)S(1)} %get-tuple-element.38), channel_id=1, source_target_pairs={{0,3},{1,2},{2,1},{3,0},{4,7},{5,6},{6,5},{7,4},{8,11},{9,10},{10,... | collective-permute-start | bytes 393224 | tf_op jit(solution)/shard_map/ppermute | solution.py:213
  70.3 9.6 %collective-permute-start.18 = (bf16[64,1024]{1,0:T(8,128)(2,1)S(1)}, bf16[64,1024]{1,0:T(8,128)(2,1)S(1)}, u32[]{:S(2)}, u32[]{:S(2)}) collective-permute-start(bf16[64,1024]{1,0:T(8,128)(2,1)S(1)} %get-tuple-element.39), channel_id=1, source_target_pairs={{0,1},{1,0},{2,3},{3,2},{4,5},{5,4},{6,7},{7,6},{8,9},{9,8},{10,11... | collective-permute-start | bytes 393224 | tf_op jit(solution)/shard_map/ppermute | solution.py:213
  70.4 15.7 %collective-permute-start.19 = (bf16[64,1024]{1,0:T(8,128)(2,1)S(1)}, bf16[64,1024]{1,0:T(8,128)(2,1)S(1)}, u32[]{:S(2)}, u32[]{:S(2)}) collective-permute-start(bf16[64,1024]{1,0:T(8,128)(2,1)S(1)} %get-tuple-element.40), channel_id=1, source_target_pairs={{0,2},{1,3},{2,0},{3,1},{4,6},{5,7},{6,4},{7,5},{8,10},{9,11},{10,... | collective-permute-start | bytes 393224 | tf_op jit(solution)/shard_map/ppermute | solution.py:213

commit v5 on v4

--- a/solution.py
+++ b/solution.py
@@ -99,7 +99,7 @@
     cols = own_weight.shape[1] // CORES
     share = depth // chips
     rows_out = rows // planes
-    block = min(cols, 512)
+    block = min(cols, 1024)
     size = (planes - 1) * depth
     aligned = share % HD == 0
     chip_orders = [chip_order(chips, core) for core in range(CORES)]

time: 87.8 us -> 87.8 us (level)
  no operation moved by 1% of the time
where the time goes in v5:
time: 87.8 us; the launch traced here: 87.4 us
  starting transfers between devices  36.9 us (42%)
  waiting for transfers between devices  33.6 us (38%)
  Pallas kernels  9.99 us (11%)
  local copies, waits for them, and re-layouts  5.63 us (6%)
  other arithmetic  1.11 us (1%)
    ppermute x12, waiting for transfers between devices, paired(): return lax.ppermute(shard, 'head', [(i, i ^ x) for i in range(length)])  29.9 us
    ppermute x12, starting transfers between devices, paired(): return lax.ppermute(shard, 'head', [(i, i ^ x) for i in range(length)])  18.8 us
    ppermute x4, starting transfers between devices, later(): return lax.ppermute(shard, 'ctx', [(i, i + by) for i in range(length - by)])  10.2 us
    ppermute x4, starting transfers between devices, crossed(): lax.ppermute(shard, 'ctx', [(i, i ^ CORES << bit[i % CORES]) for i in ran...  7.3 us
    pallas_call x2, Pallas kernels, project(): pl.pallas_call(kernel, out_shape=[jax.ShapeDtypeStruct((rows_out, cols),...  3.65 us
    pallas_call x1, Pallas kernels, attention(): pl.pallas_call(attention_kernel, out_shape=jax.ShapeDtypeStruct(queries.s...  3.6 us
    ppermute x4, waiting for transfers between devices, later(): return lax.ppermute(shard, 'ctx', [(i, i + by) for i in range(length - by)])  3.57 us
    pallas_call x2, Pallas kernels, assemble(): pl.pallas_call(kernel, out_shape=jax.ShapeDtypeStruct((rows, width), jnp....  2.73 us
  transfers between devices with their start and end apart: 23, of which 10 were waited for; matrix products, arithmetic and copies ran while one was open for 5% of the time, Pallas kernels for 10%

profile of v5, /device:TPU:0, one launch (start us, length us, event | category | flops | bytes accessed | tf_op | source)
XLA Modules:
  0.0 87.4 jit_solution(12139808646630307581)
XLA Ops:
  0.0 1.2 %fusion = (bf16[128,1024]{1,0:T(8,128)(2,1)S(1)}, bf16[128,1024]{1,0:T(8,128)(2,1)S(1)}, bf16[128,1024]{1,0:T(8,128)(2,1)S(1)}) fusion(bf16[512,8192]{1,0:T(8,128)(2,1)} %param.9, s32[]{:T(128)S(6)} %select_n.30, s32[]{:T(128)S(6)} %select_n.33, s32[]{:T(128)S(6)} %select_n.32, s32[]{:T(128)S(6)} %select_n.31), kind=kLoop, calls=%fused_computation.9 | loop fusion | bytes 1572880 | tf_op jit(solution)/shard_map/dynamic_slice | solution.py:250
  1.2 5.1 %collective-permute-start.6 = (bf16[128,1024]{1,0:T(8,128)(2,1)S(1)}, bf16[128,1024]{1,0:T(8,128)(2,1)S(1)}, u32[]{:S(2)}, u32[]{:S(2)}) collective-permute-start(bf16[128,1024]{1,0:T(8,128)(2,1)S(1)} %get-tuple-element.46), channel_id=1, source_target_pairs={{0,3},{1,2},{2,1},{3,0},{4,7},{5,6},{6,5},{7,4},{8,11},{9,10},{10,... | collective-permute-start | bytes 786440 | tf_op jit(solution)/shard_map/ppermute | solution.py:213
  6.3 0.8 constant_dynamic-update-slice_fusion.1
  7.1 0.9 constant_dynamic-update-slice_fusion.refs_4_
  8.0 2.6 %collective-permute-start.1 = (bf16[512,128]{1,0:T(8,128)(2,1)S(1)}, bf16[512,128]{1,0:T(8,128)(2,1)S(1)}, u32[]{:S(2)}, u32[]{:S(2)}) collective-permute-start(bf16[512,128]{1,0:T(8,128)(2,1)S(1)} %constant_dynamic-update-slice_fusion.refs_4_), channel_id=1, source_target_pairs={{0,12},{4,16},{8,20},{12,24},{16,28},{1,13},{5,17},{9,21},{13,25},... | collective-permute-start | bytes 393224 | tf_op jit(solution)/shard_map/ppermute | solution.py:232
  10.5 3.4 %collective-permute-start.2 = (bf16[512,128]{1,0:T(8,128)(2,1)S(1)}, bf16[512,128]{1,0:T(8,128)(2,1)S(1)}, u32[]{:S(2)}, u32[]{:S(2)}) collective-permute-start(bf16[512,128]{1,0:T(8,128)(2,1)S(1)} %constant_dynamic-update-slice_fusion.refs_4_), channel_id=1, source_target_pairs={{0,8},{4,12},{8,16},{12,20},{16,24},{20,28},{1,9},{5,13},{9,17},{1... | collective-permute-start | bytes 393224 | tf_op jit(solution)/shard_map/ppermute | solution.py:232
  14.0 2.6 %collective-permute-start.3 = (bf16[512,128]{1,0:T(8,128)(2,1)S(1)}, bf16[512,128]{1,0:T(8,128)(2,1)S(1)}, u32[]{:S(2)}, u32[]{:S(2)}) collective-permute-start(bf16[512,128]{1,0:T(8,128)(2,1)S(1)} %constant_dynamic-update-slice_fusion.refs_4_), channel_id=1, source_target_pairs={{0,4},{4,8},{8,12},{12,16},{16,20},{20,24},{24,28},{1,5},{5,9},{9,... | collective-permute-start | bytes 393224 | tf_op jit(solution)/shard_map/ppermute | solution.py:232
  16.6 1.2 %collective-permute-done.2.refs_2_ = bf16[512,128]{1,0:T(8,128)(2,1)S(1)} collective-permute-done((bf16[512,128]{1,0:T(8,128)(2,1)S(1)}, bf16[512,128]{1,0:T(8,128)(2,1)S(1)}, u32[]{:S(2)}, u32[]{:S(2)}) %collective-permute-start.2) | collective-permute-done | bytes 131104 | tf_op jit(solution)/shard_map/ppermute | solution.py:232
  18.4 3.5 %collective-permute-start.9 = (bf16[1,2,128,1024]{3,2,1,0:T(8,128)(2,1)S(1)}, bf16[1,2,128,1024]{3,2,1,0:T(8,128)(2,1)S(1)}, u32[]{:S(2)}, u32[]{:S(2)}) collective-permute-start(bf16[1,2,128,1024]{3,2,1,0:T(8,128)(2,1)S(1)} %maximum_bitcast_fusion), channel_id=1, source_target_pairs={{0,8},{4,20},{8,0},{12,28},{16,24},{20,4},{24,16},{28,12},{1,9},{5... | collective-permute-start | bytes 1572872 | tf_op jit(solution)/shard_map/ppermute | solution.py:225
  21.9 1.6 %collective-permute-start = (bf16[512,128]{1,0:T(8,128)(2,1)S(1)}, bf16[512,128]{1,0:T(8,128)(2,1)S(1)}, u32[]{:S(2)}, u32[]{:S(2)}) collective-permute-start(bf16[512,128]{1,0:T(8,128)(2,1)S(1)} %constant_dynamic-update-slice_fusion.refs_4_), channel_id=1, source_target_pairs={{0,16},{4,20},{8,24},{12,28},{1,17},{5,21},{9,25},{13,29},{2,18},{... | collective-permute-start | bytes 393224 | tf_op jit(solution)/shard_map/ppermute | solution.py:232
  23.5 0.8 collective-permute-start.7
  25.1 2.3 %collective-permute-done.refs_0_ = bf16[512,128]{1,0:T(8,128)(2,1)S(1)} collective-permute-done((bf16[512,128]{1,0:T(8,128)(2,1)S(1)}, bf16[512,128]{1,0:T(8,128)(2,1)S(1)}, u32[]{:S(2)}, u32[]{:S(2)}) %collective-permute-start) | collective-permute-done | bytes 131104 | tf_op jit(solution)/shard_map/ppermute | solution.py:232
  27.4 0.9 %copy-done = bf16[256,512]{1,0:T(8,128)(2,1)S(1)} copy-done((bf16[256,512]{1,0:T(8,128)(2,1)S(1)}, bf16[256,512]{1,0:T(8,128)(2,1)}, u32[]{:S(2)}) %copy-start) | copy-done | bytes 262168
  28.4 3.6 %attention.1 = bf16[256,512]{1,0:T(8,128)(2,1)S(1)} custom-call(s32[9]{0:T(128)S(1)} %pad_add_fusion.1.place_ref, bf16[256,512]{1,0:T(8,128)(2,1)S(1)} %copy-done, bf16[512,128]{1,0:T(8,128)(2,1)S(1)} %collective-permute-done.refs_0_, bf16[512,128]{1,0:T(8,128)(2,1)S(1)} %collective-permute-done.1.refs_1_, ...), custom_call_target="tpu_custom_call" | custom-call | tf_op jit(solution)/shard_map/attention/pallas_call | solution.py:59
  32.0 2.1 %collective-permute-start.4 = (bf16[1,256,512]{2,1,0:T(8,128)(2,1)S(1)}, bf16[1,256,512]{2,1,0:T(8,128)(2,1)S(1)}, u32[]{:S(2)}, u32[]{:S(2)}) collective-permute-start(bf16[1,256,512]{2,1,0:T(8,128)(2,1)S(1)} %bitcast.17), channel_id=1, source_target_pairs={{0,1},{1,0},{2,3},{3,2},{4,5},{5,4},{6,7},{7,6},{8,9},{9,8},{10,11... | collective-permute-start | bytes 786440 | tf_op jit(solution)/shard_map/ppermute | solution.py:213
  34.4 2.5 %collective-permute-start.14 = (bf16[2,2,128,1024]{3,2,1,0:T(8,128)(2,1)S(1)}, bf16[2,2,128,1024]{3,2,1,0:T(8,128)(2,1)S(1)}, u32[]{:S(2)}, u32[]{:S(2)}) collective-permute-start(bf16[2,2,128,1024]{3,2,1,0:T(8,128)(2,1)S(1)} %pad_maximum_fusion), channel_id=1, source_target_pairs={{0,16},{4,12},{8,24},{12,4},{16,0},{20,28},{24,8},{28,20},{1,17},{... | collective-permute-start | bytes 3145736 | tf_op jit(solution)/shard_map/ppermute | solution.py:225
  37.0 1.3 %collective-permute-done.7 = bf16[128,1024]{1,0:T(8,128)(2,1)S(1)} collective-permute-done((bf16[128,1024]{1,0:T(8,128)(2,1)S(1)}, bf16[128,1024]{1,0:T(8,128)(2,1)S(1)}, u32[]{:S(2)}, u32[]{:S(2)}) %collective-permute-start.7) | collective-permute-done | bytes 262176 | tf_op jit(solution)/shard_map/ppermute | solution.py:213
  38.8 1.8 %constant_dynamic-slice_fusion.refs_4_ = bf16[512,2048]{1,0:T(8,128)(2,1)S(1)} fusion(bf16[512,8192]{1,0:T(8,128)(2,1)} %param.9, s32[]{:T(128)S(6)} %select_n.34), kind=kLoop, calls=%fused_computation.8 | loop fusion | bytes 4194308 | tf_op jit(solution)/shard_map/dynamic_slice | solution.py:269
  40.7 8.2 %collective-permute-done.4.refs_2_ = bf16[1,256,512]{2,1,0:T(8,128)(2,1)S(1)} collective-permute-done((bf16[1,256,512]{2,1,0:T(8,128)(2,1)S(1)}, bf16[1,256,512]{2,1,0:T(8,128)(2,1)S(1)}, u32[]{:S(2)}, u32[]{:S(2)}) %collective-permute-start.4) | collective-permute-done | bytes 262176 | tf_op jit(solution)/shard_map/ppermute | solution.py:213
  49.7 1.6 %collective-permute-start.11 = (bf16[1,256,512]{2,1,0:T(8,128)(2,1)S(1)}, bf16[1,256,512]{2,1,0:T(8,128)(2,1)S(1)}, u32[]{:S(2)}, u32[]{:S(2)}) collective-permute-start(bf16[1,256,512]{2,1,0:T(8,128)(2,1)S(1)} %collective-permute-done.5.refs_1_), channel_id=1, source_target_pairs={{0,1},{1,0},{2,3},{3,2},{4,5},{5,4},{6,7},{7,6},{8,9},{9,8},{10,11... | collective-permute-start | bytes 786440 | tf_op jit(solution)/shard_map/ppermute | solution.py:213
  51.4 6.7 %collective-permute-done.11.refs_3_ = bf16[1,256,512]{2,1,0:T(8,128)(2,1)S(1)} collective-permute-done((bf16[1,256,512]{2,1,0:T(8,128)(2,1)S(1)}, bf16[1,256,512]{2,1,0:T(8,128)(2,1)S(1)}, u32[]{:S(2)}, u32[]{:S(2)}) %collective-permute-start.11) | collective-permute-done | bytes 262176 | tf_op jit(solution)/shard_map/ppermute | solution.py:213
  59.0 1.8 %project.3 = (bf16[64,1024]{1,0:T(8,128)(2,1)S(1)}, bf16[64,1024]{1,0:T(8,128)(2,1)S(1)}, bf16[64,1024]{1,0:T(8,128)(2,1)S(1)}, bf16[64,1024]{1,0:T(8,128)(2,1)S(1)}) custom-call(s32[3]{0:T(128)S(1)} %pad_add_fusion.place_ref, bf16[1,256,512]{2,1,0:T(8,128)(2,1)S(1)} %bitcast.19, bf16[1,256,512]{2,1,0:T(8,128)(2,1)S(1)} %collective-permute-done.5.refs_1_, ...), custom_call_target="tpu_custom_call" | custom-call | flops 1073741824 | bytes 5767168 | tf_op jit(solution)/shard_map/project/pallas_call | solution.py:156
  60.8 3.2 %collective-permute-start.20 = (bf16[64,1024]{1,0:T(8,128)(2,1)S(1)}, bf16[64,1024]{1,0:T(8,128)(2,1)S(1)}, u32[]{:S(2)}, u32[]{:S(2)}) collective-permute-start(bf16[64,1024]{1,0:T(8,128)(2,1)S(1)} %get-tuple-element.42), channel_id=1, source_target_pairs={{0,3},{1,2},{2,1},{3,0},{4,7},{5,6},{6,5},{7,4},{8,11},{9,10},{10,... | collective-permute-start | bytes 393224 | tf_op jit(solution)/shard_map/ppermute | solution.py:213
  64.1 1.2 %collective-permute-start.22 = (bf16[64,1024]{1,0:T(8,128)(2,1)S(1)}, bf16[64,1024]{1,0:T(8,128)(2,1)S(1)}, u32[]{:S(2)}, u32[]{:S(2)}) collective-permute-start(bf16[64,1024]{1,0:T(8,128)(2,1)S(1)} %get-tuple-element.44), channel_id=1, source_target_pairs={{0,2},{1,3},{2,0},{3,1},{4,6},{5,7},{6,4},{7,5},{8,10},{9,11},{10,... | collective-permute-start | bytes 393224 | tf_op jit(solution)/shard_map/ppermute | solution.py:213
  65.3 1.8 %project.2 = (bf16[64,1024]{1,0:T(8,128)(2,1)S(1)}, bf16[64,1024]{1,0:T(8,128)(2,1)S(1)}, bf16[64,1024]{1,0:T(8,128)(2,1)S(1)}, bf16[64,1024]{1,0:T(8,128)(2,1)S(1)}) custom-call(s32[3]{0:T(128)S(1)} %pad_add_fusion.place_ref, bf16[1,256,512]{2,1,0:T(8,128)(2,1)S(1)} %bitcast.20, bf16[1,256,512]{2,1,0:T(8,128)(2,1)S(1)} %collective-permute-done.5.refs_1_, ...), custom_call_target="tpu_custom_call" | custom-call | flops 1073741824 | bytes 5767168 | tf_op jit(solution)/shard_map/project/pallas_call | solution.py:156
  67.1 3.2 %collective-permute-start.17 = (bf16[64,1024]{1,0:T(8,128)(2,1)S(1)}, bf16[64,1024]{1,0:T(8,128)(2,1)S(1)}, u32[]{:S(2)}, u32[]{:S(2)}) collective-permute-start(bf16[64,1024]{1,0:T(8,128)(2,1)S(1)} %get-tuple-element.38), channel_id=1, source_target_pairs={{0,3},{1,2},{2,1},{3,0},{4,7},{5,6},{6,5},{7,4},{8,11},{9,10},{10,... | collective-permute-start | bytes 393224 | tf_op jit(solution)/shard_map/ppermute | solution.py:213
  70.4 1.2 %collective-permute-start.19 = (bf16[64,1024]{1,0:T(8,128)(2,1)S(1)}, bf16[64,1024]{1,0:T(8,128)(2,1)S(1)}, u32[]{:S(2)}, u32[]{:S(2)}) collective-permute-start(bf16[64,1024]{1,0:T(8,128)(2,1)S(1)} %get-tuple-element.40), channel_id=1, source_target_pairs={{0,2},{1,3},{2,0},{3,1},{4,6},{5,7},{6,4},{7,5},{8,10},{9,11},{10,... | collective-permute-start | bytes 393224 | tf_op jit(solution)/shard_map/ppermute | solution.py:213
  71.6 1.6 %collective-permute-done.21.refs_2_ = bf16[64,1024]{1,0:T(8,128)(2,1)S(1)} collective-permute-done((bf16[64,1024]{1,0:T(8,128)(2,1)S(1)}, bf16[64,1024]{1,0:T(8,128)(2,1)S(1)}, u32[]{:S(2)}, u32[]{:S(2)}) %collective-permute-start.21) | collective-permute-done | bytes 131104 | tf_op jit(solution)/shard_map/ppermute | solution.py:213
  73.1 5.4 %collective-permute-done.22.refs_3_ = bf16[64,1024]{1,0:T(8,128)(2,1)S(1)} collective-permute-done((bf16[64,1024]{1,0:T(8,128)(2,1)S(1)}, bf16[64,1024]{1,0:T(8,128)(2,1)S(1)}, u32[]{:S(2)}, u32[]{:S(2)}) %collective-permute-start.22) | collective-permute-done | bytes 131104 | tf_op jit(solution)/shard_map/ppermute | solution.py:213
  78.5 1.4 %assemble.2.refs_4_ = bf16[64,8192]{1,0:T(8,128)(2,1)} custom-call(s32[3]{0:T(128)S(1)} %pad_add_fusion.place_ref, bf16[64,1024]{1,0:T(8,128)(2,1)S(1)} %get-tuple-element.41.refs_0_, bf16[64,1024]{1,0:T(8,128)(2,1)S(1)} %collective-permute-done.20.refs_1_, bf16[64,1024]{1,0:T(8,128)(2,1)S(1)} %collective-permute-done.21.refs_2_, ...), custom_call_target="tpu_custom_call" | custom-call | tf_op jit(solution)/shard_map/assemble/pallas_call | solution.py:197
  79.9 6.1 %collective-permute-done.19.refs_3_ = bf16[64,1024]{1,0:T(8,128)(2,1)S(1)} collective-permute-done((bf16[64,1024]{1,0:T(8,128)(2,1)S(1)}, bf16[64,1024]{1,0:T(8,128)(2,1)S(1)}, u32[]{:S(2)}, u32[]{:S(2)}) %collective-permute-start.19) | collective-permute-done | bytes 131104 | tf_op jit(solution)/shard_map/ppermute | solution.py:213
  86.1 1.4 %assemble.3 = bf16[64,8192]{1,0:T(8,128)(2,1)} custom-call(s32[3]{0:T(128)S(1)} %pad_add_fusion.place_ref, bf16[64,1024]{1,0:T(8,128)(2,1)S(1)} %get-tuple-element.37.refs_0_, bf16[64,1024]{1,0:T(8,128)(2,1)S(1)} %collective-permute-done.17.refs_1_, bf16[64,1024]{1,0:T(8,128)(2,1)S(1)} %collective-permute-done.18.refs_2_, ...), custom_call_target="tpu_custom_call", output_to_operand_aliasing={{}: (5, {})} | custom-call | tf_op jit(solution)/shard_map/assemble/pallas_call | solution.py:197
  (31 shorter events, 3.8 us)
Async XLA Ops:
  1.2 16.6 %collective-permute-start.6 = (bf16[128,1024]{1,0:T(8,128)(2,1)S(1)}, bf16[128,1024]{1,0:T(8,128)(2,1)S(1)}, u32[]{:S(2)}, u32[]{:S(2)}) collective-permute-start(bf16[128,1024]{1,0:T(8,128)(2,1)S(1)} %get-tuple-element.46), channel_id=1, source_target_pairs={{0,3},{1,2},{2,1},{3,0},{4,7},{5,6},{6,5},{7,4},{8,11},{9,10},{10,... | collective-permute-start | bytes 786440 | tf_op jit(solution)/shard_map/ppermute | solution.py:213
  6.3 12.0 %collective-permute-start.8 = (bf16[128,1024]{1,0:T(8,128)(2,1)S(1)}, bf16[128,1024]{1,0:T(8,128)(2,1)S(1)}, u32[]{:S(2)}, u32[]{:S(2)}) collective-permute-start(bf16[128,1024]{1,0:T(8,128)(2,1)S(1)} %get-tuple-element.45), channel_id=1, source_target_pairs={{0,1},{1,0},{2,3},{3,2},{4,5},{5,4},{6,7},{7,6},{8,9},{9,8},{10,11... | collective-permute-start | bytes 786440 | tf_op jit(solution)/shard_map/ppermute | solution.py:213
  8.0 8.6 %collective-permute-start.1 = (bf16[512,128]{1,0:T(8,128)(2,1)S(1)}, bf16[512,128]{1,0:T(8,128)(2,1)S(1)}, u32[]{:S(2)}, u32[]{:S(2)}) collective-permute-start(bf16[512,128]{1,0:T(8,128)(2,1)S(1)} %constant_dynamic-update-slice_fusion.refs_4_), channel_id=1, source_target_pairs={{0,12},{4,16},{8,20},{12,24},{16,28},{1,13},{5,17},{9,21},{13,25},... | collective-permute-start | bytes 393224 | tf_op jit(solution)/shard_map/ppermute | solution.py:232
  10.5 7.3 %collective-permute-start.2 = (bf16[512,128]{1,0:T(8,128)(2,1)S(1)}, bf16[512,128]{1,0:T(8,128)(2,1)S(1)}, u32[]{:S(2)}, u32[]{:S(2)}) collective-permute-start(bf16[512,128]{1,0:T(8,128)(2,1)S(1)} %constant_dynamic-update-slice_fusion.refs_4_), channel_id=1, source_target_pairs={{0,8},{4,12},{8,16},{12,20},{16,24},{20,28},{1,9},{5,13},{9,17},{1... | collective-permute-start | bytes 393224 | tf_op jit(solution)/shard_map/ppermute | solution.py:232
  14.0 3.9 %collective-permute-start.3 = (bf16[512,128]{1,0:T(8,128)(2,1)S(1)}, bf16[512,128]{1,0:T(8,128)(2,1)S(1)}, u32[]{:S(2)}, u32[]{:S(2)}) collective-permute-start(bf16[512,128]{1,0:T(8,128)(2,1)S(1)} %constant_dynamic-update-slice_fusion.refs_4_), channel_id=1, source_target_pairs={{0,4},{4,8},{8,12},{12,16},{16,20},{20,24},{24,28},{1,5},{5,9},{9,... | collective-permute-start | bytes 393224 | tf_op jit(solution)/shard_map/ppermute | solution.py:232
  18.4 16.0 %collective-permute-start.9 = (bf16[1,2,128,1024]{3,2,1,0:T(8,128)(2,1)S(1)}, bf16[1,2,128,1024]{3,2,1,0:T(8,128)(2,1)S(1)}, u32[]{:S(2)}, u32[]{:S(2)}) collective-permute-start(bf16[1,2,128,1024]{3,2,1,0:T(8,128)(2,1)S(1)} %maximum_bitcast_fusion), channel_id=1, source_target_pairs={{0,8},{4,20},{8,0},{12,28},{16,24},{20,4},{24,16},{28,12},{1,9},{5... | collective-permute-start | bytes 1572872 | tf_op jit(solution)/shard_map/ppermute | solution.py:225
  21.9 5.6 %collective-permute-start = (bf16[512,128]{1,0:T(8,128)(2,1)S(1)}, bf16[512,128]{1,0:T(8,128)(2,1)S(1)}, u32[]{:S(2)}, u32[]{:S(2)}) collective-permute-start(bf16[512,128]{1,0:T(8,128)(2,1)S(1)} %constant_dynamic-update-slice_fusion.refs_4_), channel_id=1, source_target_pairs={{0,16},{4,20},{8,24},{12,28},{1,17},{5,21},{9,25},{13,29},{2,18},{... | collective-permute-start | bytes 393224 | tf_op jit(solution)/shard_map/ppermute | solution.py:232
  23.5 14.8 %collective-permute-start.7 = (bf16[128,1024]{1,0:T(8,128)(2,1)S(1)}, bf16[128,1024]{1,0:T(8,128)(2,1)S(1)}, u32[]{:S(2)}, u32[]{:S(2)}) collective-permute-start(bf16[128,1024]{1,0:T(8,128)(2,1)S(1)} %get-tuple-element.25), channel_id=1, source_target_pairs={{0,2},{1,3},{2,0},{3,1},{4,6},{5,7},{6,4},{7,5},{8,10},{9,11},{10,... | collective-permute-start | bytes 786440 | tf_op jit(solution)/shard_map/ppermute | solution.py:213
  27.4 0.9 %copy-start = (bf16[256,512]{1,0:T(8,128)(2,1)S(1)}, bf16[256,512]{1,0:T(8,128)(2,1)}, u32[]{:S(2)}) copy-start(bf16[256,512]{1,0:T(8,128)(2,1)} %query_hbm.1) | copy-start | bytes 786436
  32.0 16.9 %collective-permute-start.4 = (bf16[1,256,512]{2,1,0:T(8,128)(2,1)S(1)}, bf16[1,256,512]{2,1,0:T(8,128)(2,1)S(1)}, u32[]{:S(2)}, u32[]{:S(2)}) collective-permute-start(bf16[1,256,512]{2,1,0:T(8,128)(2,1)S(1)} %bitcast.17), channel_id=1, source_target_pairs={{0,1},{1,0},{2,3},{3,2},{4,5},{5,4},{6,7},{7,6},{8,9},{9,8},{10,11... | collective-permute-start | bytes 786440 | tf_op jit(solution)/shard_map/ppermute | solution.py:213
  34.1 14.8 %collective-permute-start.5 = (bf16[1,256,512]{2,1,0:T(8,128)(2,1)S(1)}, bf16[1,256,512]{2,1,0:T(8,128)(2,1)S(1)}, u32[]{:S(2)}, u32[]{:S(2)}) collective-permute-start(bf16[1,256,512]{2,1,0:T(8,128)(2,1)S(1)} %bitcast.18), channel_id=1, source_target_pairs={{0,3},{1,2},{2,1},{3,0},{4,7},{5,6},{6,5},{7,4},{8,11},{9,10},{10,... | collective-permute-start | bytes 786440 | tf_op jit(solution)/shard_map/ppermute | solution.py:213
  34.4 24.0 %collective-permute-start.14 = (bf16[2,2,128,1024]{3,2,1,0:T(8,128)(2,1)S(1)}, bf16[2,2,128,1024]{3,2,1,0:T(8,128)(2,1)S(1)}, u32[]{:S(2)}, u32[]{:S(2)}) collective-permute-start(bf16[2,2,128,1024]{3,2,1,0:T(8,128)(2,1)S(1)} %pad_maximum_fusion), channel_id=1, source_target_pairs={{0,16},{4,12},{8,24},{12,4},{16,0},{20,28},{24,8},{28,20},{1,17},{... | collective-permute-start | bytes 3145736 | tf_op jit(solution)/shard_map/ppermute | solution.py:225
  38.3 10.6 %collective-permute-start.10 = (bf16[1,1,128,1024]{3,2,1,0:T(8,128)(2,1)S(1)}, bf16[1,1,128,1024]{3,2,1,0:T(8,128)(2,1)S(1)}, u32[]{:S(2)}, u32[]{:S(2)}) collective-permute-start(bf16[1,1,128,1024]{3,2,1,0:T(8,128)(2,1)S(1)} %bitcast.23), channel_id=1, source_target_pairs={{0,8},{4,20},{8,0},{12,28},{16,24},{20,4},{24,16},{28,12},{1,9},{5... | collective-permute-start | bytes 786440 | tf_op jit(solution)/shard_map/ppermute | solution.py:225
  49.0 9.2 %collective-permute-start.12 = (bf16[2,1,128,1024]{3,2,1,0:T(8,128)(2,1)S(1)}, bf16[2,1,128,1024]{3,2,1,0:T(8,128)(2,1)S(1)}, u32[]{:S(2)}, u32[]{:S(2)}) collective-permute-start(bf16[2,1,128,1024]{3,2,1,0:T(8,128)(2,1)S(1)} %pad_maximum_fusion.2), channel_id=1, source_target_pairs={{0,16},{4,12},{8,24},{12,4},{16,0},{20,28},{24,8},{28,20},{1,17},{... | collective-permute-start | bytes 1572872 | tf_op jit(solution)/shard_map/ppermute | solution.py:225
  49.7 8.4 %collective-permute-start.11 = (bf16[1,256,512]{2,1,0:T(8,128)(2,1)S(1)}, bf16[1,256,512]{2,1,0:T(8,128)(2,1)S(1)}, u32[]{:S(2)}, u32[]{:S(2)}) collective-permute-start(bf16[1,256,512]{2,1,0:T(8,128)(2,1)S(1)} %collective-permute-done.5.refs_1_), channel_id=1, source_target_pairs={{0,1},{1,0},{2,3},{3,2},{4,5},{5,4},{6,7},{7,6},{8,9},{9,8},{10,11... | collective-permute-start | bytes 786440 | tf_op jit(solution)/shard_map/ppermute | solution.py:213
  51.4 12.7 %collective-permute-start.13 = (bf16[512,1024]{1,0:T(8,128)(2,1)S(1)}, bf16[512,1024]{1,0:T(8,128)(2,1)S(1)}, u32[]{:S(2)}, u32[]{:S(2)}) collective-permute-start(bf16[512,1024]{1,0:T(8,128)(2,1)S(1)} %bitcast.13), channel_id=1, source_target_pairs={{0,4},{4,0},{8,12},{12,8},{16,20},{20,16},{24,28},{28,24},{1,5},{5... | collective-permute-start | bytes 3145736 | tf_op jit(solution)/shard_map/ppermute | solution.py:218
  58.3 7.0 %collective-permute-start.16 = (bf16[512,1024]{1,0:T(8,128)(2,1)S(1)}, bf16[512,1024]{1,0:T(8,128)(2,1)S(1)}, u32[]{:S(2)}, u32[]{:S(2)}) collective-permute-start(bf16[512,1024]{1,0:T(8,128)(2,1)S(1)} %bitcast.15), channel_id=1, source_target_pairs={{0,4},{4,0},{8,12},{12,8},{16,20},{20,16},{24,28},{28,24},{1,5},{5... | collective-permute-start | bytes 3145736 | tf_op jit(solution)/shard_map/ppermute | solution.py:218
  58.4 6.9 %collective-permute-start.15 = (bf16[512,1024]{1,0:T(8,128)(2,1)S(1)}, bf16[512,1024]{1,0:T(8,128)(2,1)S(1)}, u32[]{:S(2)}, u32[]{:S(2)}) collective-permute-start(bf16[512,1024]{1,0:T(8,128)(2,1)S(1)} %bitcast.21), channel_id=1, source_target_pairs={{0,4},{4,0},{8,12},{12,8},{16,20},{20,16},{24,28},{28,24},{1,5},{5... | collective-permute-start | bytes 3145736 | tf_op jit(solution)/shard_map/ppermute | solution.py:218
  60.8 9.5 %collective-permute-start.20 = (bf16[64,1024]{1,0:T(8,128)(2,1)S(1)}, bf16[64,1024]{1,0:T(8,128)(2,1)S(1)}, u32[]{:S(2)}, u32[]{:S(2)}) collective-permute-start(bf16[64,1024]{1,0:T(8,128)(2,1)S(1)} %get-tuple-element.42), channel_id=1, source_target_pairs={{0,3},{1,2},{2,1},{3,0},{4,7},{5,6},{6,5},{7,4},{8,11},{9,10},{10,... | collective-permute-start | bytes 393224 | tf_op jit(solution)/shard_map/ppermute | solution.py:213
  64.1 9.1 %collective-permute-start.21 = (bf16[64,1024]{1,0:T(8,128)(2,1)S(1)}, bf16[64,1024]{1,0:T(8,128)(2,1)S(1)}, u32[]{:S(2)}, u32[]{:S(2)}) collective-permute-start(bf16[64,1024]{1,0:T(8,128)(2,1)S(1)} %get-tuple-element.43), channel_id=1, source_target_pairs={{0,1},{1,0},{2,3},{3,2},{4,5},{5,4},{6,7},{7,6},{8,9},{9,8},{10,11... | collective-permute-start | bytes 393224 | tf_op jit(solution)/shard_map/ppermute | solution.py:213
  64.1 14.5 %collective-permute-start.22 = (bf16[64,1024]{1,0:T(8,128)(2,1)S(1)}, bf16[64,1024]{1,0:T(8,128)(2,1)S(1)}, u32[]{:S(2)}, u32[]{:S(2)}) collective-permute-start(bf16[64,1024]{1,0:T(8,128)(2,1)S(1)} %get-tuple-element.44), channel_id=1, source_target_pairs={{0,2},{1,3},{2,0},{3,1},{4,6},{5,7},{6,4},{7,5},{8,10},{9,11},{10,... | collective-permute-start | bytes 393224 | tf_op jit(solution)/shard_map/ppermute | solution.py:213
  67.1 12.8 %collective-permute-start.17 = (bf16[64,1024]{1,0:T(8,128)(2,1)S(1)}, bf16[64,1024]{1,0:T(8,128)(2,1)S(1)}, u32[]{:S(2)}, u32[]{:S(2)}) collective-permute-start(bf16[64,1024]{1,0:T(8,128)(2,1)S(1)} %get-tuple-element.38), channel_id=1, source_target_pairs={{0,3},{1,2},{2,1},{3,0},{4,7},{5,6},{6,5},{7,4},{8,11},{9,10},{10,... | collective-permute-start | bytes 393224 | tf_op jit(solution)/shard_map/ppermute | solution.py:213
  70.4 9.6 %collective-permute-start.18 = (bf16[64,1024]{1,0:T(8,128)(2,1)S(1)}, bf16[64,1024]{1,0:T(8,128)(2,1)S(1)}, u32[]{:S(2)}, u32[]{:S(2)}) collective-permute-start(bf16[64,1024]{1,0:T(8,128)(2,1)S(1)} %get-tuple-element.39), channel_id=1, source_target_pairs={{0,1},{1,0},{2,3},{3,2},{4,5},{5,4},{6,7},{7,6},{8,9},{9,8},{10,11... | collective-permute-start | bytes 393224 | tf_op jit(solution)/shard_map/ppermute | solution.py:213
  70.4 15.7 %collective-permute-start.19 = (bf16[64,1024]{1,0:T(8,128)(2,1)S(1)}, bf16[64,1024]{1,0:T(8,128)(2,1)S(1)}, u32[]{:S(2)}, u32[]{:S(2)}) collective-permute-start(bf16[64,1024]{1,0:T(8,128)(2,1)S(1)} %get-tuple-element.40), channel_id=1, source_target_pairs={{0,2},{1,3},{2,0},{3,1},{4,6},{5,7},{6,4},{7,5},{8,10},{9,11},{10,... | collective-permute-start | bytes 393224 | tf_op jit(solution)/shard_map/ppermute | solution.py:213
